TPU v7x, 32 devices: a whole 2x2x4 slice. The times are simulated.
32 devices in a mesh: dp: 4 (over z), tx: 4 (over y, core), ty: 2 (over x).
Axes of the slice: x: 2, y: 2, z: 4, core: 2. Of those that a mesh axis runs over, the one named last changes fastest.
Arguments:
- tokens: bfloat16 [8192, 2048], P(('dp', 'tx'), 'ty'), may hold values from -6 to 6
- seg_ids: int32 [8, 1024], P(('dp', 'ty')), may hold values from 0 to 3, as said below
- w_query: bfloat16 [2048, 2048], P('ty', 'tx'), may hold values from -0.125 to 0.125
- w_key: bfloat16 [2048, 1024], P('ty', 'tx'), may hold values from -0.125 to 0.125
- w_value: bfloat16 [2048, 1024], P('ty', 'tx'), may hold values from -0.125 to 0.125
- w_out: bfloat16 [2048, 2048], P('tx', 'ty'), may hold values from -1 to 1
- w_gate: bfloat16 [2048, 6144], P('ty', 'tx'), may hold values from -0.125 to 0.125
- w_up: bfloat16 [2048, 6144], P('ty', 'tx'), may hold values from -0.125 to 0.125
- w_down: bfloat16 [6144, 2048], P('tx', 'ty'), may hold values from -0.078125 to 0.078125
- attn_gain: float32 [2048], P('ty'), may hold values from 0.5 to 1.5
- mlp_gain: float32 [2048], P('ty'), may hold values from 0.5 to 1.5
- query_gain: float32 [128], replicated, may hold values from 1 to 2
- key_gain: float32 [128], replicated, may hold values from 1 to 2
- cotangent: bfloat16 [8192, 2048], P(('dp', 'tx'), 'ty'), may hold values from -6 to 6
Outputs:
- output: bfloat16 [8192, 2048], P(('dp', 'tx'), 'ty')
- input_grad: bfloat16 [8192, 2048], P(('dp', 'tx'), 'ty')
- query_weight_grad: float32 [2048, 2048], P(('ty', 'dp'), 'tx')
- key_weight_grad: float32 [2048, 1024], P(('ty', 'dp'), 'tx')
- value_weight_grad: float32 [2048, 1024], P(('ty', 'dp'), 'tx')
- out_weight_grad: float32 [2048, 2048], P('tx', ('ty', 'dp'))
- gate_weight_grad: float32 [2048, 6144], P(('ty', 'dp'), 'tx')
- up_weight_grad: float32 [2048, 6144], P(('ty', 'dp'), 'tx')
- down_weight_grad: float32 [6144, 2048], P('tx', ('ty', 'dp'))
- attn_gain_grad: float32 [2048], replicated
- mlp_gain_grad: float32 [2048], replicated
- query_gain_grad: float32 [128], replicated
- key_gain_grad: float32 [128], replicated
Inputs may be any that keep to these rules, and one draw needn't show every extreme that they name: `seg_ids`: document numbers never fall along a sequence and every one of 0 to 3 occurs; each document has 102 to 512 tokens, and in every sequence one document has exactly 512.
All inputs are finite; a program needn't handle non-finite values.
Results may differ from a plain program's by a relative error of at most 0.023.
Values may be sent and summed in bfloat16 or wider, within the bound.
A program may use at most 256 MiB of HBM per device.

v0:
```python
import jax
import jax.numpy as jnp
from jax import lax
from jax.sharding import PartitionSpec as P

EPS = 1e-06
THETA = 1000000.0
NEG = -1e30
F32 = jnp.float32
B16 = jnp.bfloat16


def width_sum(value):
    return lax.psum(value, "ty")


def token_gather(rows):
    return lax.all_gather(rows, "tx", axis=0, tiled=True)


def branch_gather(rows):
    return lax.all_gather(rows, "ty", axis=0, tiled=True)


def width_reduce(whole, apply):
    return lax.psum_scatter(apply(whole), "ty", scatter_dimension=0, tiled=True)


def head_reduce(whole, apply):
    return lax.psum_scatter(
        apply(whole).astype(jnp.bfloat16), "tx", scatter_dimension=0, tiled=True
    ).astype(jnp.float32)


def forward_with(weight):
    return lambda rows: jnp.dot(rows, weight, preferred_element_type=F32)


def backward_with(weight):
    return lambda rows: lax.dot_general(
        rows, weight, (((1,), (1,)), ((), ())), preferred_element_type=F32
    )


def weight_grad(left, right):
    return lax.dot_general(left, right, (((0,), (0,)), ((), ())), preferred_element_type=F32)


def norm_scale(rows):
    width = rows.shape[1] * lax.axis_size("ty")
    return lax.rsqrt(width_sum(jnp.sum(rows * rows, axis=1)) / width + EPS)


def norm_back(rows, scale, gain, upstream):
    width = rows.shape[1] * lax.axis_size("ty")
    inner = width_sum(jnp.sum(upstream * gain * rows, axis=1))
    back = scale[:, None] * gain * upstream - rows * (scale**3 * inner / width)[:, None]
    gain_part = jnp.sum(upstream * rows * scale[:, None], axis=0)
    return (back, gain_part)


def widen(part):
    whole = jnp.zeros((part.shape[0] * lax.axis_size("ty"),), F32)
    return lax.dynamic_update_slice_in_dim(whole, part, lax.axis_index("ty") * part.shape[0], 0)


def doc_positions(seg):
    count = seg.shape[-1]
    index = jnp.arange(count, dtype=jnp.int32)
    edge = jnp.concatenate([jnp.ones((1,), dtype=jnp.bool_), seg[1:] != seg[:-1]])
    first = lax.cummax(jnp.where(edge, index, jnp.zeros_like(index)), axis=0)
    return index - first


def rotary(positions, depth):
    half = depth // 2
    freq = THETA ** (-jnp.arange(half, dtype=F32) * 2.0 / depth)
    angle = positions.astype(F32)[..., None] * freq
    return (jnp.cos(angle), jnp.sin(angle))


def turn(value, gain, cosine, sine):
    normed = value * lax.rsqrt(jnp.mean(value * value, axis=-1, keepdims=True) + EPS) * gain
    half = value.shape[-1] // 2
    first = normed[..., :half]
    second = normed[..., half:]
    return jnp.concatenate(
        [first * cosine - second * sine, second * cosine + first * sine], axis=-1
    )


def block_scores(part, seq_keys, seq_ids, start, scale):
    block = part.shape[0]
    length = seq_ids.shape[0]
    index = jnp.arange(length, dtype=jnp.int32)
    rows = start + jnp.arange(block, dtype=jnp.int32)
    row_ids = lax.dynamic_slice_in_dim(seq_ids, start, block, 0)
    mask = (seq_ids[None, :] == row_ids[:, None]) & (index[None, :] <= rows[:, None])
    scores = jnp.einsum("qkgd,mkd->kgqm", part, seq_keys, preferred_element_type=F32) * scale
    return jnp.where(mask[None, None], scores, NEG)


def attend_forward(query, keys, values, seg, block):
    seqs, length, heads, depth = query.shape
    kv_heads = keys.shape[2]
    groups = heads // kv_heads
    scale = depth ** (-0.5)
    count = length // block
    starts = jnp.arange(count, dtype=jnp.int32) * block

    def one_sequence(operands):
        seq_query, seq_keys, seq_values, seq_ids = operands
        blocks = seq_query.reshape(count, block, kv_heads, groups, depth)

        def one_block(inputs):
            part, start = inputs
            scores = block_scores(part, seq_keys, seq_ids, start, scale)
            top = jnp.max(scores, axis=-1)
            weights = jnp.exp(scores - top[..., None])
            total = jnp.sum(weights, axis=-1)
            probs = (weights / total[..., None]).astype(B16)
            mixed = jnp.einsum("kgqm,mkd->qkgd", probs, seq_values, preferred_element_type=F32)
            return (mixed, top + jnp.log(total))

        mixed, logs = lax.map(one_block, (blocks, starts))
        return (mixed.reshape(length, heads * depth), logs)

    return lax.map(one_sequence, (query, keys, values, seg))


def attend_backward(query, keys, values, seg, logs, grad_out, block):
    seqs, length, heads, depth = query.shape
    kv_heads = keys.shape[2]
    groups = heads // kv_heads
    scale = depth ** (-0.5)
    count = length // block
    starts = jnp.arange(count, dtype=jnp.int32) * block

    def one_sequence(operands):
        seq_query, seq_keys, seq_values, seq_ids, seq_logs, seq_grad = operands
        blocks = seq_query.reshape(count, block, kv_heads, groups, depth)
        grads = seq_grad.reshape(count, block, kv_heads, groups, depth)

        def one_block(carry, inputs):
            key_acc, value_acc = carry
            part, grad_part, log_part, start = inputs
            scores = block_scores(part, seq_keys, seq_ids, start, scale)
            probs = jnp.exp(scores - log_part[..., None])
            value_acc = value_acc + jnp.einsum(
                "kgqm,qkgd->mkd", probs.astype(B16), grad_part, preferred_element_type=F32
            )
            prob_grad = jnp.einsum(
                "qkgd,mkd->kgqm", grad_part, seq_values, preferred_element_type=F32
            )
            delta = jnp.sum(probs * prob_grad, axis=-1, keepdims=True)
            score_grad = (probs * (prob_grad - delta)).astype(B16)
            query_grad = (
                jnp.einsum("kgqm,mkd->qkgd", score_grad, seq_keys, preferred_element_type=F32)
                * scale
            )
            key_acc = (
                key_acc
                + jnp.einsum("kgqm,qkgd->mkd", score_grad, part, preferred_element_type=F32) * scale
            )
            return ((key_acc, value_acc), query_grad)

        zeros = jnp.zeros((length, kv_heads, depth), F32)
        (key_grad, value_grad), query_grad = lax.scan(
            one_block, (zeros, zeros), (blocks, grads, seq_logs, starts)
        )
        return (query_grad.reshape(length, heads, depth), key_grad, value_grad)

    return lax.map(one_sequence, (query, keys, values, seg, logs, grad_out))


def per_device(
    tokens,
    seg_ids,
    w_query,
    w_key,
    w_value,
    w_out,
    w_gate,
    w_up,
    w_down,
    attn_gain,
    mlp_gain,
    query_gain,
    key_gain,
    cotangent,
):
    seqs, length = seg_ids.shape
    depth = query_gain.shape[0]
    query_width = w_query.shape[1]
    key_width = w_key.shape[1]
    units = w_gate.shape[1]
    block = min(512, length)
    inputs = tokens.astype(F32)
    first_scale = norm_scale(inputs)
    first_normed = (inputs * first_scale[:, None] * attn_gain).astype(B16)
    first_whole = token_gather(first_normed)
    w_project = jnp.concatenate([w_query, w_key, w_value], axis=1)
    projected = width_reduce(first_whole, forward_with(w_project))
    query_proj = projected[:, :query_width].reshape(seqs, length, -1, depth)
    key_proj = projected[:, query_width : query_width + key_width].reshape(seqs, length, -1, depth)
    values = projected[:, query_width + key_width :].astype(B16).reshape(seqs, length, -1, depth)
    positions = jax.vmap(doc_positions)(seg_ids)
    cosine, sine = rotary(positions, depth)
    cosine = cosine[:, :, None, :]
    sine = sine[:, :, None, :]
    query = turn(query_proj, query_gain, cosine, sine).astype(B16)
    keys = turn(key_proj, key_gain, cosine, sine).astype(B16)
    mixed, logs = attend_forward(query, keys, values, seg_ids, block)
    attended = mixed.reshape(seqs * length, -1).astype(B16)
    attended_whole = branch_gather(attended)
    residual = inputs + head_reduce(attended_whole, forward_with(w_out))
    second_scale = norm_scale(residual)
    second_normed = (residual * second_scale[:, None] * mlp_gain).astype(B16)
    second_whole = token_gather(second_normed)
    w_both = jnp.concatenate([w_gate, w_up], axis=1)
    gate_up = width_reduce(second_whole, forward_with(w_both))
    gate = gate_up[:, :units]
    upper = gate_up[:, units:]
    hidden = (jax.nn.silu(gate) * upper).astype(B16)
    hidden_whole = branch_gather(hidden)
    output = residual + head_reduce(hidden_whole, forward_with(w_down))
    grad_whole = token_gather(cotangent)
    hidden_grad = width_reduce(grad_whole, backward_with(w_down))
    down_grad = weight_grad(hidden_whole, grad_whole)
    gate_grad, up_grad = jax.vjp(lambda left, right: jax.nn.silu(left) * right, gate, upper)[1](
        hidden_grad
    )
    unit_grads = jnp.concatenate([gate_grad, up_grad], axis=1).astype(B16)
    unit_whole = branch_gather(unit_grads)
    second_grad = head_reduce(unit_whole, backward_with(w_both))
    both_grad = weight_grad(second_whole, unit_whole)
    gate_weight = both_grad[:, :units]
    up_weight = both_grad[:, units:]
    resid_norm_grad, mlp_gain_part = norm_back(residual, second_scale, mlp_gain, second_grad)
    residual_grad = cotangent.astype(F32) + resid_norm_grad
    residual_whole = token_gather(residual_grad.astype(B16))
    mixed_grad = width_reduce(residual_whole, backward_with(w_out)).astype(B16)
    out_grad = weight_grad(attended_whole, residual_whole)
    query_grad, key_grad, value_grad = attend_backward(
        query, keys, values, seg_ids, logs, mixed_grad.reshape(seqs, length, -1), block
    )
    query_proj_grad, query_gain_grad = jax.vjp(
        lambda value, gain: turn(value, gain, cosine, sine), query_proj, query_gain
    )[1](query_grad)
    key_proj_grad, key_gain_grad = jax.vjp(
        lambda value, gain: turn(value, gain, cosine, sine), key_proj, key_gain
    )[1](key_grad)
    rows = seqs * length
    proj_grad = jnp.concatenate(
        [
            query_proj_grad.reshape(rows, -1),
            key_proj_grad.reshape(rows, -1),
            value_grad.reshape(rows, -1),
        ],
        axis=1,
    ).astype(B16)
    proj_whole = branch_gather(proj_grad)
    first_grad = head_reduce(proj_whole, backward_with(w_project))
    project_grad = weight_grad(first_whole, proj_whole)
    query_weight = project_grad[:, :query_width]
    key_weight = project_grad[:, query_width : query_width + key_width]
    value_weight = project_grad[:, query_width + key_width :]
    input_norm_grad, attn_gain_part = norm_back(inputs, first_scale, attn_gain, first_grad)
    input_grad = (residual_grad + input_norm_grad).astype(B16)
    attn_total, mlp_total, query_total, key_total = lax.psum(
        (widen(attn_gain_part), widen(mlp_gain_part), query_gain_grad, key_gain_grad),
        ("dp", "tx", "ty"),
    )
    query_share, key_share, value_share, gate_share, up_share = (
        lax.psum_scatter(
            query_weight.astype(jnp.bfloat16), "dp", scatter_dimension=0, tiled=True
        ).astype(jnp.float32),
        lax.psum_scatter(
            key_weight.astype(jnp.bfloat16), "dp", scatter_dimension=0, tiled=True
        ).astype(jnp.float32),
        lax.psum_scatter(
            value_weight.astype(jnp.bfloat16), "dp", scatter_dimension=0, tiled=True
        ).astype(jnp.float32),
        lax.psum_scatter(
            gate_weight.astype(jnp.bfloat16), "dp", scatter_dimension=0, tiled=True
        ).astype(jnp.float32),
        lax.psum_scatter(
            up_weight.astype(jnp.bfloat16), "dp", scatter_dimension=0, tiled=True
        ).astype(jnp.float32),
    )
    out_share, down_share = (
        lax.psum_scatter(
            out_grad.astype(jnp.bfloat16), "dp", scatter_dimension=1, tiled=True
        ).astype(jnp.float32),
        lax.psum_scatter(
            down_grad.astype(jnp.bfloat16), "dp", scatter_dimension=1, tiled=True
        ).astype(jnp.float32),
    )
    return (
        output.astype(B16),
        input_grad,
        query_share,
        key_share,
        value_share,
        out_share,
        gate_share,
        up_share,
        down_share,
        attn_total,
        mlp_total,
        query_total,
        key_total,
    )


def solution(mesh):
    placed = (
        P(("dp", "tx"), "ty"),
        P(("dp", "ty"), None),
        P("ty", "tx"),
        P("ty", "tx"),
        P("ty", "tx"),
        P("tx", "ty"),
        P("ty", "tx"),
        P("ty", "tx"),
        P("tx", "ty"),
        P("ty"),
        P("ty"),
        P(),
        P(),
        P(("dp", "tx"), "ty"),
    )
    return jax.shard_map(
        per_device,
        mesh=mesh,
        in_specs=placed,
        out_specs=(
            P(("dp", "tx"), "ty"),
            P(("dp", "tx"), "ty"),
            P(("ty", "dp"), "tx"),
            P(("ty", "dp"), "tx"),
            P(("ty", "dp"), "tx"),
            P("tx", ("ty", "dp")),
            P(("ty", "dp"), "tx"),
            P(("ty", "dp"), "tx"),
            P("tx", ("ty", "dp")),
            P(),
            P(),
            P(),
            P(),
        ),
        check_vma=False,
    )
```

profile of v0, /device:TPU:10, one launch (start us, length us, event | category | flops | bytes accessed | tf_op | source)
XLA Modules:
  0.0 1701.1 jit_solution(7299453238081051261)
XLA Ops:
  8.9 4.9 psum.56
  22.3 30.5 %all-gather.9.cloned.1.call-done = bf16[2048,1024]{1,0:T(8,128)(2,1)} async-done(((bf16[512,1024]{1,0:T(8,128)(2,1)}), bf16[2048,1024]{1,0:T(8,128)(2,1)}) %all-gather.9.cloned.1.call-update) | async-done | bytes 4194320 | tf_op jit(solution)/shard_map/all_gather | solution.py:18
  52.8 10.7 fusion.82
  69.8 92.2 %reduce-scatter.16.cloned.1.call-done = f32[1024,1024]{1,0:T(8,128)} async-done(((f32[2048,1024]{1,0:T(8,128)}), f32[1024,1024]{1,0:T(8,128)}) %reduce-scatter.16.cloned.1.call-update) | async-done | bytes 4194320 | tf_op jit(solution)/shard_map/reduce_scatter | solution.py:26
  209.1 25.9 %while.47 = (s32[]{:T(128)}, bf16[2,512,2,2,128]{4,1,3,2,0:T(8,128)(2,1)}, f32[2,2,2,512]{3,2,1,0:T(2,128)S(1)}, s32[1024]{0:T(1024)S(1)}, s32[2]{0:T(128)S(1)},...) while((s32[]{:T(128)}, ...), condition=%wide.region_10.11_spmd, body=%wide.region_7.10_spmd.sunk | while | flops 1100478976 | bytes 32062660 | solution.py:125
  240.6 33.2 %all-gather.11.cloned.1.call-done = bf16[2048,512]{1,0:T(8,128)(2,1)} async-done(((bf16[1024,512]{1,0:T(8,128)(2,1)}), bf16[2048,512]{1,0:T(8,128)(2,1)}) %all-gather.11.cloned.1.call-update) | async-done | bytes 2097168 | tf_op jit(solution)/shard_map/all_gather | solution.py:22
  273.9 6.2 convolution_convert_fusion.4
  280.7 44.9 %reduce-scatter.18.cloned.1.call-done = bf16[512,1024]{1,0:T(8,128)(2,1)} async-done(((bf16[2048,1024]{1,0:T(8,128)(2,1)}), bf16[512,1024]{1,0:T(8,128)(2,1)}) %reduce-scatter.18.cloned.1.call-update) | async-done | bytes 1048592 | tf_op jit(solution)/shard_map/reduce_scatter | solution.py:30
  327.6 4.9 psum.57
  335.7 25.8 %all-gather.17.cloned.1.call-done = bf16[2048,1024]{1,0:T(8,128)(2,1)} async-done(((bf16[512,1024]{1,0:T(8,128)(2,1)}), bf16[2048,1024]{1,0:T(8,128)(2,1)}) %all-gather.17.cloned.1.call-update) | async-done | bytes 4194320 | tf_op jit(solution)/shard_map/all_gather | solution.py:18
  361.6 11.5 fusion.84
  373.3 4.1 constant_dynamic-update-slice_fusion.4
  379.3 18.8 %all-gather.13.cloned.1.call-done = bf16[2048,1024]{1,0:T(8,128)(2,1)} async-done(((bf16[512,1024]{1,0:T(8,128)(2,1)}), bf16[2048,1024]{1,0:T(8,128)(2,1)}) %all-gather.13.cloned.1.call-update) | async-done | bytes 4194320 | tf_op jit(solution)/shard_map/all_gather | solution.py:18
  398.1 19.9 %fusion.83 = f32[2048,3072]{1,0:T(8,128)} fusion(bf16[2048,1024]{1,0:T(8,128)(2,1)} %all-gather.13.cloned.1.call-done, bf16[1024,3072]{1,0:T(8,128)(2,1)} %constant_dynamic-update-slice_fusion.3), kind=kOutput, calls=%fused_computation.170 | convolution fusion | flops 12884901888 | bytes 35651584 | tf_op jit(solution)/shard_map/dot_general | solution.py:36
  418.0 126.0 %reduce-scatter.24.cloned.1.call-done = f32[1024,1536]{1,0:T(8,128)} async-done(((f32[2048,1536]{1,0:T(8,128)}), f32[1024,1536]{1,0:T(8,128)}) %reduce-scatter.24.cloned.1.call-update) | async-done | bytes 6291472 | tf_op jit(solution)/shard_map/reduce_scatter | solution.py:26
  544.0 281.6 %reduce-scatter.20.cloned.1.call-done = f32[1024,3072]{1,0:T(8,128)} async-done(((f32[2048,3072]{1,0:T(8,128)}), f32[1024,3072]{1,0:T(8,128)}) %reduce-scatter.20.cloned.1.call-update) | async-done | bytes 12582928 | tf_op jit(solution)/shard_map/reduce_scatter | solution.py:26
  825.6 9.8 fusion.49
  839.0 152.6 %all-gather.19.cloned.1.call-done = bf16[2048,3072]{1,0:T(8,128)(2,1)} async-done(((bf16[1024,3072]{1,0:T(8,128)(2,1)}), bf16[2048,3072]{1,0:T(8,128)(2,1)}) %all-gather.19.cloned.1.call-update) | async-done | bytes 12582928 | tf_op jit(solution)/shard_map/all_gather | solution.py:22
  991.6 18.9 %convolution_convert_fusion.1 = bf16[2048,1024]{1,0:T(8,128)(2,1)} fusion(bf16[2048,3072]{1,0:T(8,128)(2,1)} %all-gather.19.cloned.1.call-done, bf16[1024,3072]{1,0:T(8,128)(2,1)} %constant_dynamic-update-slice_fusion.3), kind=kOutput, calls=%fused_computation.75 | convolution fusion | flops 12886999040 | bytes 23068672 | tf_op jit(solution)/shard_map/dot_general | solution.py:40
  1010.6 45.5 %reduce-scatter.26.cloned.1.call-done = bf16[512,1024]{1,0:T(8,128)(2,1)} async-done(((bf16[2048,1024]{1,0:T(8,128)(2,1)}), bf16[512,1024]{1,0:T(8,128)(2,1)}) %reduce-scatter.26.cloned.1.call-update) | async-done | bytes 1048592 | tf_op jit(solution)/shard_map/reduce_scatter | solution.py:30
  1059.4 4.9 psum.58
  1068.4 34.6 %all-gather.21.cloned.1.call-done = bf16[2048,1024]{1,0:T(8,128)(2,1)} async-done(((bf16[512,1024]{1,0:T(8,128)(2,1)}), bf16[2048,1024]{1,0:T(8,128)(2,1)}) %all-gather.21.cloned.1.call-update) | async-done | bytes 4194320 | tf_op jit(solution)/shard_map/all_gather | solution.py:18
  1102.9 6.9 fusion.85
  1110.7 52.7 %reduce-scatter.28.cloned.1.call-done = f32[1024,512]{1,0:T(8,128)} async-done(((f32[2048,512]{1,0:T(8,128)}), f32[1024,512]{1,0:T(8,128)}) %reduce-scatter.28.cloned.1.call-update) | async-done | bytes 2097168 | tf_op jit(solution)/shard_map/reduce_scatter | solution.py:26
  1168.7 54.8 %while.48 = (s32[]{:T(128)}, f32[1024,2,128]{0,2,1:T(8,128)}, f32[1024,2,128]{0,2,1:T(8,128)}, f32[2,512,2,2,128]{4,1,0,3,2:T(8,128)}, bf16[2,512,2,2,128]{4,1,3...) while((s32[]{:T(128)}, f32[1024,2,128]{0,2,1:T(8,128)}, ...), condition=%wide.region_23.24_spmd.clone, body=%wide.region_21.23_spmd.clone.sunk | while | flops 2718956032 | bytes 173613024 | solution.py:168
  1186.1 4.3 fusion.146
  1191.3 4.6 fusion.147
  1213.0 4.6 fusion.146
  1218.6 4.9 fusion.147
  1238.9 6.5 all-gather.15.cloned.1.call-done
  1245.4 11.4 convolution_convert_fusion.2
  1256.9 18.0 %convolution_convert_fusion = bf16[1024,3072]{1,0:T(8,128)(2,1)S(1)} fusion(bf16[2048,1024]{1,0:T(8,128)(2,1)} %all-gather.13.cloned.1.call-done, bf16[2048,3072]{1,0:T(8,128)(2,1)} %all-gather.19.cloned.1.call-done), kind=kOutput, calls=%fused_computation.68 | convolution fusion | flops 12888047616 | bytes 23068672 | tf_op jit(solution)/shard_map/dot_general | solution.py:46
  1278.7 6.1 convolution_convert_fusion.7
  1285.2 18.4 %all-gather.23.cloned.1.call-done = bf16[2048,1024]{0,1:T(8,128)(2,1)} async-done(((bf16[1024,1024]{0,1:T(8,128)(2,1)}), bf16[2048,1024]{0,1:T(8,128)(2,1)}) %all-gather.23.cloned.1.call-update) | async-done | bytes 4194320 | tf_op jit(solution)/shard_map/all_gather | solution.py:22
  1303.6 8.0 convolution_convert_fusion.6
  1317.0 9.5 convolution_convert_fusion.5
  1326.8 11.1 convolution_convert_fusion.3
  1338.0 28.5 %reduce-scatter.44.cloned.1.call-done = bf16[1536,256]{1,0:T(8,128)(2,1)} async-done(((bf16[1536,1024]{1,0:T(8,128)(2,1)}), bf16[1536,256]{1,0:T(8,128)(2,1)}) %reduce-scatter.44.cloned.1.call-update) | async-done | bytes 786448 | tf_op jit(solution)/shard_map/reduce_scatter | solution.py:295
  1368.8 60.1 %reduce-scatter.40.cloned.1.call-done = bf16[256,1536]{1,0:T(8,128)(2,1)} async-done(((bf16[1024,1536]{1,0:T(8,128)(2,1)}), bf16[256,1536]{1,0:T(8,128)(2,1)}) %reduce-scatter.40.cloned.1.call-update) | async-done | bytes 786448 | tf_op jit(solution)/shard_map/reduce_scatter | solution.py:284
  1431.4 60.0 %reduce-scatter.42.cloned.1.call-done = bf16[256,1536]{1,0:T(8,128)(2,1)} async-done(((bf16[1024,1536]{1,0:T(8,128)(2,1)}), bf16[256,1536]{1,0:T(8,128)(2,1)}) %reduce-scatter.42.cloned.1.call-update) | async-done | bytes 786448 | tf_op jit(solution)/shard_map/reduce_scatter | solution.py:287
  1494.0 25.7 %reduce-scatter.38.cloned.1.call-done = bf16[512,256]{1,0:T(8,128)(2,1)} async-done(((bf16[512,1024]{1,0:T(8,128)(2,1)}), bf16[512,256]{1,0:T(8,128)(2,1)}) %reduce-scatter.38.cloned.1.call-update) | async-done | bytes 262160 | tf_op jit(solution)/shard_map/reduce_scatter | solution.py:292
  1521.5 19.9 %reduce-scatter.34.cloned.1.call-done = bf16[256,256]{1,0:T(8,128)(2,1)} async-done(((bf16[1024,256]{1,0:T(8,128)(2,1)}), bf16[256,256]{1,0:T(8,128)(2,1)}) %reduce-scatter.34.cloned.1.call-update) | async-done | bytes 131088 | tf_op jit(solution)/shard_map/reduce_scatter | solution.py:278
  1543.0 21.1 %reduce-scatter.36.cloned.1.call-done = bf16[256,256]{1,0:T(8,128)(2,1)} async-done(((bf16[1024,256]{1,0:T(8,128)(2,1)}), bf16[256,256]{1,0:T(8,128)(2,1)}) %reduce-scatter.36.cloned.1.call-update) | async-done | bytes 131088 | tf_op jit(solution)/shard_map/reduce_scatter | solution.py:281
  1565.8 27.8 %reduce-scatter.32.cloned.1.call-done = bf16[256,512]{1,0:T(8,128)(2,1)} async-done(((bf16[1024,512]{1,0:T(8,128)(2,1)}), bf16[256,512]{1,0:T(8,128)(2,1)}) %reduce-scatter.32.cloned.1.call-update) | async-done | bytes 262160 | tf_op jit(solution)/shard_map/reduce_scatter | solution.py:275
  1595.4 46.0 %reduce-scatter.30.cloned.1.call-done = bf16[512,1024]{1,0:T(8,128)(2,1)} async-done(((bf16[2048,1024]{1,0:T(8,128)(2,1)}), bf16[512,1024]{1,0:T(8,128)(2,1)}) %reduce-scatter.30.cloned.1.call-update) | async-done | bytes 1048592 | tf_op jit(solution)/shard_map/reduce_scatter | solution.py:30
  1644.1 4.9 psum.59
  1649.0 40.7 %all-reduce.4 = (f32[2048]{0:T(1024)}, f32[2048]{0:T(1024)}, f32[128]{0:T(128)}, f32[128]{0:T(128)}) all-reduce(f32[2048]{0:T(1024)S(1)} %dynamic_update_slice.31, f32[2048]{0:T(1024)S(1)} %dynamic_update_slice.32, f32[128]{0:T(128)S(1)} %get-tuple-element.327, ...), channel_id=1, replica_groups=mesh['dp'=4,'tx'=4,'ty'=2] {'dp','tx','ty'}, use_global_device_ids=true, to_apply=%region_37.38 | all-reduce | flops 4352 | bytes 34816 | tf_op jit(solution)/shard_map/psum | solution.py:270
  1689.7 4.6 fusion.60
  (281 shorter events, 189.8 us)
Async XLA Ops:
  7.2 354.4 %copy-start = (bf16[1536,1024]{1,0:T(8,128)(2,1)S(1)}, bf16[1536,1024]{1,0:T(8,128)(2,1)}, u32[]{:S(2)}) copy-start(bf16[1536,1024]{1,0:T(8,128)(2,1)} %param.26) | copy-start | bytes 9437188
  7.2 45.6 %all-gather.9.cloned.1.call-start = ((), (), s32[]{:S(2)}) async-start(), calls=%async_computation.15 | async-start | bytes 5242880 | tf_op jit(solution)/shard_map/all_gather | solution.py:18
  13.8 7.5 copy-start.37
  17.0 145.0 %reduce-scatter.16.cloned.1.call-start = ((), (), s32[]{:S(2)}) async-start(), calls=%async_computation.16 | async-start | bytes 12582912 | tf_op jit(solution)/shard_map/reduce_scatter | solution.py:26
  63.5 210.4 %all-gather.11.cloned.1.call-start = ((), (), s32[]{:S(2)}) async-start(), calls=%async_computation.17 | async-start | bytes 3145728 | tf_op jit(solution)/shard_map/all_gather | solution.py:22
  66.8 136.2 %copy-start.15 = (f32[1024,64]{0,1:T(8,128)}, f32[1024,64]{0,1:T(8,128)S(1)}, u32[]{:S(2)}) copy-start(f32[1024,64]{0,1:T(8,128)S(1)} %get-tuple-element.398) | copy-start | bytes 786436
  175.6 8.4 copy-start.44
  183.3 4.9 copy-start.24
  190.4 11.3 copy-start.42
  201.0 6.0 copy-start.28
  240.6 85.1 %reduce-scatter.18.cloned.1.call-start = ((), (), s32[]{:S(2)}) async-start(), calls=%async_computation.18 | async-start | bytes 5242880 | tf_op jit(solution)/shard_map/reduce_scatter | solution.py:30
  280.0 52.5 %copy-start.30 = (f32[1024]{0:T(1024)S(1)}, f32[1024]{0:T(1024)}, u32[]{:S(2)}) copy-start(f32[1024]{0:T(1024)} %param.28) | copy-start | bytes 12292
  280.1 81.5 %all-gather.17.cloned.1.call-start = ((), (), s32[]{:S(2)}) async-start(), calls=%async_computation.23 | async-start | bytes 5242880 | tf_op jit(solution)/shard_map/all_gather | solution.py:18
  280.7 117.4 %all-gather.13.cloned.1.call-start = ((), (), s32[]{:S(2)}) async-start(), calls=%async_computation.19 | async-start | bytes 5242880 | tf_op jit(solution)/shard_map/all_gather | solution.py:18
  332.5 731.8 %copy-start.32 = (f32[512]{0:T(512)}, f32[512]{0:T(512)S(1)}, u32[]{:S(2)}) copy-start(f32[512]{0:T(512)S(1)} %add_rsqrt_fusion) | copy-start | bytes 6148
  335.7 208.3 %reduce-scatter.24.cloned.1.call-start = ((), (), s32[]{:S(2)}) async-start(), calls=%async_computation.24 | async-start | bytes 18874368 | tf_op jit(solution)/shard_map/reduce_scatter | solution.py:26
  373.0 452.5 %reduce-scatter.20.cloned.1.call-start = ((), (), s32[]{:S(2)}) async-start(), calls=%async_computation.20 | async-start | bytes 37748736 | tf_op jit(solution)/shard_map/reduce_scatter | solution.py:26
  417.9 573.7 %all-gather.19.cloned.1.call-start = ((), (), s32[]{:S(2)}) async-start(), calls=%async_computation.25 | async-start | bytes 18874368 | tf_op jit(solution)/shard_map/all_gather | solution.py:22
  839.0 217.1 %reduce-scatter.26.cloned.1.call-start = ((), (), s32[]{:S(2)}) async-start(), calls=%async_computation.26 | async-start | bytes 5242880 | tf_op jit(solution)/shard_map/reduce_scatter | solution.py:30
  1010.5 92.4 %all-gather.21.cloned.1.call-start = ((), (), s32[]{:S(2)}) async-start(), calls=%async_computation.27 | async-start | bytes 5242880 | tf_op jit(solution)/shard_map/all_gather | solution.py:18
  1068.3 95.1 %reduce-scatter.28.cloned.1.call-start = ((), (), s32[]{:S(2)}) async-start(), calls=%async_computation.28 | async-start | bytes 6291456 | tf_op jit(solution)/shard_map/reduce_scatter | solution.py:26
  1109.9 135.5 %all-gather.15.cloned.1.call-start = ((), (), s32[]{:S(2)}) async-start(), calls=%async_computation.21 | async-start | bytes 9437184 | tf_op jit(solution)/shard_map/all_gather | solution.py:22
  1110.6 192.9 %all-gather.23.cloned.1.call-start = ((), (), s32[]{:S(2)}) async-start(), calls=%async_computation.29 | async-start | bytes 6291456 | tf_op jit(solution)/shard_map/all_gather | solution.py:22
  1172.5 6.7 copy-start.4
  1186.0 5.2 copy-start.2
  1186.1 5.2 copy-start.5
  1199.7 6.6 copy-start.4
  1206.3 4.5 copy-start.6
  1213.0 5.5 copy-start.2
  1213.0 5.5 copy-start.5
  1231.4 5.2 copy-start.27
  1231.4 5.2 copy-start.43
  1238.9 127.6 %reduce-scatter.44.cloned.1.call-start = ((), (), s32[]{:S(2)}) async-start(), calls=%async_computation.37 | async-start | bytes 3932160 | tf_op jit(solution)/shard_map/reduce_scatter | solution.py:295
  1256.9 172.0 %reduce-scatter.40.cloned.1.call-start = ((), (), s32[]{:S(2)}) async-start(), calls=%async_computation.35 | async-start | bytes 3932160 | tf_op jit(solution)/shard_map/reduce_scatter | solution.py:284
  1278.1 213.3 %reduce-scatter.42.cloned.1.call-start = ((), (), s32[]{:S(2)}) async-start(), calls=%async_computation.36 | async-start | bytes 3932160 | tf_op jit(solution)/shard_map/reduce_scatter | solution.py:287
  1278.7 241.0 %reduce-scatter.38.cloned.1.call-start = ((), (), s32[]{:S(2)}) async-start(), calls=%async_computation.34 | async-start | bytes 1310720 | tf_op jit(solution)/shard_map/reduce_scatter | solution.py:292
  1284.9 256.5 %reduce-scatter.34.cloned.1.call-start = ((), (), s32[]{:S(2)}) async-start(), calls=%async_computation.32 | async-start | bytes 655360 | tf_op jit(solution)/shard_map/reduce_scatter | solution.py:278
  1314.0 250.1 %reduce-scatter.36.cloned.1.call-start = ((), (), s32[]{:S(2)}) async-start(), calls=%async_computation.33 | async-start | bytes 655360 | tf_op jit(solution)/shard_map/reduce_scatter | solution.py:281
  1314.6 279.0 %reduce-scatter.32.cloned.1.call-start = ((), (), s32[]{:S(2)}) async-start(), calls=%async_computation.31 | async-start | bytes 1310720 | tf_op jit(solution)/shard_map/reduce_scatter | solution.py:275
  1316.9 324.4 %reduce-scatter.30.cloned.1.call-start = ((), (), s32[]{:S(2)}) async-start(), calls=%async_computation.30 | async-start | bytes 5242880 | tf_op jit(solution)/shard_map/reduce_scatter | solution.py:30
  1326.5 363.2 %reduce-scatter.22.cloned.1.call-start = ((), (), s32[]{:S(2)}) async-start(), calls=%async_computation.22 | async-start | bytes 5242880 | tf_op jit(solution)/shard_map/reduce_scatter | solution.py:30
  1338.0 155.9 %copy-start.41 = (f32[1024]{0:T(1024)S(1)}, f32[1024]{0:T(1024)}, u32[]{:S(2)}) copy-start(f32[1024]{0:T(1024)} %get-tuple-element.329) | copy-start | bytes 12292
  1368.8 272.5 %copy-start.34 = (f32[1024]{0:T(1024)S(1)}, f32[1024]{0:T(1024)}, u32[]{:S(2)}) copy-start(f32[1024]{0:T(1024)} %param.27) | copy-start | bytes 12292
  1368.8 272.5 %copy-start.36 = (f32[512]{0:T(512)S(1)}, f32[512]{0:T(512)}, u32[]{:S(2)}) copy-start(f32[512]{0:T(512)} %copy-done.35) | copy-start | bytes 6148
  1431.4 258.3 %copy-start.38 = (f32[512]{0:T(512)S(1)}, f32[512]{0:T(512)}, u32[]{:S(2)}) copy-start(f32[512]{0:T(512)} %copy-done.37) | copy-start | bytes 6148
  1431.4 258.4 %copy-start.31 = (f32[1024]{0:T(1024)S(1)}, f32[1024]{0:T(1024)}, u32[]{:S(2)}) copy-start(f32[1024]{0:T(1024)} %param.28) | copy-start | bytes 12292
  1431.4 258.4 %copy-start.33 = (f32[512]{0:T(512)S(1)}, f32[512]{0:T(512)}, u32[]{:S(2)}) copy-start(f32[512]{0:T(512)} %copy-done.32) | copy-start | bytes 6148
  1431.4 258.4 %copy-start.40 = (f32[512]{0:T(512)S(1)}, f32[512]{0:T(512)}, u32[]{:S(2)}) copy-start(f32[512]{0:T(512)} %copy-done.39) | copy-start | bytes 6148
  (31 other events, 85.7 us)
Sparse Core Ops, SparseCore 0:
  17.1 35.6 all-gather.8
  63.6 98.3 reduce-scatter.15
  240.7 33.1 all-gather.10
  280.2 45.4 reduce-scatter.17
  327.0 34.4 all-gather.16
  363.5 34.4 all-gather.12
  400.4 143.5 reduce-scatter.23
  546.3 279.2 reduce-scatter.19
  839.1 152.5 all-gather.18
  1010.6 45.4 reduce-scatter.25
  1068.4 34.4 all-gather.20
  1110.0 53.3 reduce-scatter.27
  1165.0 80.3 all-gather.14
  1246.8 56.7 all-gather.22
  1305.7 60.6 reduce-scatter.43
  1368.6 60.2 reduce-scatter.39
  1431.1 60.2 reduce-scatter.41
  1494.1 25.5 reduce-scatter.37
  1522.1 19.2 reduce-scatter.33
  1544.2 19.9 reduce-scatter.35
  1567.1 26.3 reduce-scatter.31
  1596.1 45.2 reduce-scatter.29
  1644.1 45.1 reduce-scatter.21
where the time goes:
time: 1710 us; the launch traced here: 1700 us
  waiting for transfers between devices  1260 us (74%)
  matrix products  186 us (11%)
  other arithmetic  101 us (6%)
  local copies, waits for them, and re-layouts  72.8 us (4%)
  blocking collectives  60.4 us (4%)
    reduce_scatter x4, waiting for transfers between devices, width_reduce(): return lax.psum_scatter(apply(whole), 'ty', scatter_dimension=0, tiled=True)  552 us
    all_gather x4, waiting for transfers between devices, branch_gather(): return lax.all_gather(rows, 'ty', axis=0, tiled=True)  211 us
    reduce_scatter x4, waiting for transfers between devices, head_reduce(): lax.psum_scatter(apply(whole).astype(jnp.bfloat16), 'tx', scatter_dimensi...  136 us
    all_gather x4, waiting for transfers between devices, token_gather(): return lax.all_gather(rows, 'tx', axis=0, tiled=True)  110 us
    reduce_scatter x1, waiting for transfers between devices, per_device(): lax.psum_scatter(gate_weight.astype(jnp.bfloat16), 'dp', scatter_dimensio...  60.1 us
    reduce_scatter x1, waiting for transfers between devices, per_device(): lax.psum_scatter(up_weight.astype(jnp.bfloat16), 'dp', scatter_dimension=...  60 us
    dot_general x4, matrix products, forward_with(): return lambda rows: jnp.dot(rows, weight, preferred_element_type=F32)  47.9 us
    dot_general x4, matrix products, backward_with(): lax.dot_general(rows, weight, (((1,), (1,)), ((), ())), preferred_element...  46.7 us
  transfers between devices with their start and end apart: 23, of which 22 were waited for; matrix products, arithmetic and copies ran while one was open for 12% of the time, Pallas kernels for 0%

commit v1 on v0

--- a/solution.py
+++ b/solution.py
@@ -1,6 +1,8 @@
 import jax
 import jax.numpy as jnp
 from jax import lax
+from jax.experimental import pallas as pl
+from jax.experimental.pallas import tpu as pltpu
 from jax.sharding import PartitionSpec as P
 
 EPS = 1e-06
@@ -8,6 +10,7 @@
 NEG = -1e30
 F32 = jnp.float32
 B16 = jnp.bfloat16
+MESH = pl.DeviceIdType.MESH
 
 
 def width_sum(value):
@@ -173,7 +176,7 @@
     return lax.map(one_sequence, (query, keys, values, seg, logs, grad_out))
 
 
-def per_device(
+def general_device(
     tokens,
     seg_ids,
     w_query,
@@ -313,6 +316,983 @@
     )
 
 
+PARTS = 2
+
+
+def fits(mesh):
+    return mesh.shape["tx"] == 4 and mesh.shape["ty"] == 2 and mesh.shape["dp"] == 4
+
+
+def swap_x(value):
+    return lax.ppermute(value, "ty", [(0, 1), (1, 0)])
+
+
+def swap_y(value):
+    return lax.ppermute(value, "tx", [(i, i ^ 2) for i in range(4)])
+
+
+def swap_core(value):
+    return lax.ppermute(value, "tx", [(i, i ^ 1) for i in range(4)])
+
+
+def after(value, *waits):
+    return lax.optimization_barrier((value,) + waits)[0]
+
+
+def plane_gather(block, part):
+    beside = swap_x(block)
+    across = swap_y(block)
+    corner = swap_y(beside) if part % 2 == 0 else swap_x(across)
+    mine = [block, across, swap_core(block), swap_core(across)]
+    theirs = [beside, corner, swap_core(beside), swap_core(corner)]
+    return jnp.concatenate(mine, axis=0), jnp.concatenate(theirs, axis=0)
+
+
+def plane_reduce(rows, apply_mine, apply_theirs, part):
+    count = rows.shape[0] // 2
+    other = rows[count:]
+    own = rows[:count]
+    from_mine = swap_core(apply_mine(other).astype(B16))
+    from_theirs = swap_core(apply_theirs(other).astype(B16))
+    mine = (apply_mine(own) + from_mine.astype(F32)).astype(B16)
+    theirs = (apply_theirs(own) + from_theirs.astype(F32)).astype(B16)
+    step = count // 2
+    own_mine, far_mine = mine[:step], mine[step:]
+    own_theirs, far_theirs = theirs[:step], theirs[step:]
+    if part % 2 == 0:
+        far_mine = (far_mine.astype(F32) + swap_x(far_theirs).astype(F32)).astype(B16)
+    else:
+        own_theirs = (own_theirs.astype(F32) + swap_y(far_theirs).astype(F32)).astype(B16)
+    return own_mine.astype(F32) + swap_x(own_theirs).astype(F32) + swap_y(far_mine).astype(F32)
+
+
+def line_reduce(share):
+    place = lax.axis_index("dp")
+    count = lax.axis_size("dp")
+    up = None
+    down = None
+    for step in range(1, count):
+        rise = share(lax.rem(place - step + count, count)).astype(F32)
+        fall = share(lax.rem(place + step, count)).astype(F32)
+        if up is not None:
+            rise = rise + up.astype(F32)
+            fall = fall + down.astype(F32)
+        up = lax.ppermute(rise.astype(B16), "dp", [(i, i + 1) for i in range(step)])
+        down = lax.ppermute(
+            fall.astype(B16), "dp", [(i, i - 1) for i in range(count - step, count)]
+        )
+    return share(place).astype(F32) + up.astype(F32) + down.astype(F32)
+
+
+def row_share(grad):
+    size = grad.shape[0] // lax.axis_size("dp")
+    return lambda place: lax.dynamic_slice_in_dim(grad, place * size, size, 0)
+
+
+def column_share(grad):
+    size = grad.shape[1] // lax.axis_size("dp")
+    return lambda place: lax.dynamic_slice_in_dim(grad, place * size, size, 1)
+
+
+def in_order(mine, theirs, axis):
+    first = lax.axis_index("ty") == 0
+    return jnp.concatenate(
+        [jnp.where(first, mine, theirs), jnp.where(first, theirs, mine)], axis=axis
+    )
+
+
+def half_of(weight, place, axis):
+    size = weight.shape[axis] // 2
+    return lax.dynamic_slice_in_dim(weight, place * size, size, axis)
+
+
+def spin(value, cosine, sine):
+    return value * cosine + pltpu.roll(value, value.shape[1] // 2, 1) * sine
+
+
+def spin_back(value, cosine, sine):
+    return value * cosine + pltpu.roll(value * sine, value.shape[1] // 2, 1)
+
+
+def head_scale(value):
+    return lax.rsqrt(jnp.mean(value * value, axis=1, keepdims=True) + EPS)
+
+
+def window(first, block, most):
+    return max(0, first - most), first + block
+
+
+def kept(first, block, low, high, starts):
+    shape = (block, high - low)
+    column = low + lax.broadcasted_iota(jnp.int32, shape, 1)
+    row = first + lax.broadcasted_iota(jnp.int32, shape, 0)
+    return (column >= starts) & (column <= row)
+
+
+def rows_dot(left, right):
+    return lax.dot_general(left, right, (((1,), (1,)), ((), ())), preferred_element_type=F32)
+
+
+def attend_kernel(parts, heads, depth, block, most, core_ref, *refs):
+    projected = refs[:parts]
+    starts_ref, cosine_ref, sine_ref, query_gain_ref, key_gain_ref = refs[parts : parts + 5]
+    refs = refs[parts + 5 :]
+    mixed = refs[:parts]
+    query_ref, key_ref, value_ref, log_ref = refs[parts:]
+    core = core_ref[0]
+    rows = projected[0].shape[2]
+    length = query_ref.shape[1]
+    scale = depth ** (-0.5)
+    for half in range(2):
+        place = jnp.bitwise_xor(core, half)
+        for part in range(parts):
+            at = half * (length // 2) + part * rows
+            cosine = cosine_ref[0, at : at + rows, :]
+            sine = sine_ref[0, at : at + rows, :]
+            whole = projected[part][place, 0]
+            for head in range(heads):
+                value = whole[:, head * depth : (head + 1) * depth]
+                normed = value * head_scale(value) * query_gain_ref[...]
+                query_ref[0, at : at + rows, head * depth : (head + 1) * depth] = spin(
+                    normed, cosine, sine
+                ).astype(B16)
+            value = whole[:, heads * depth : (heads + 1) * depth]
+            normed = value * head_scale(value) * key_gain_ref[...]
+            key_ref[0, at : at + rows, :] = spin(normed, cosine, sine).astype(B16)
+            value_ref[0, at : at + rows, :] = whole[:, (heads + 1) * depth :].astype(B16)
+    for first in range(0, length, block):
+        low, high = window(first, block, most)
+        mask = kept(first, block, low, high, starts_ref[0, first : first + block, :])
+        half, left = divmod(first, length // 2)
+        part, inner = divmod(left, rows)
+        for head in range(heads):
+            query = query_ref[0, first : first + block, head * depth : (head + 1) * depth]
+            scores = rows_dot(query, key_ref[0, low:high, :]) * scale
+            scores = jnp.where(mask, scores, NEG)
+            top = jnp.max(scores, axis=1, keepdims=True)
+            weights = jnp.exp(scores - top)
+            total = jnp.sum(weights, axis=1, keepdims=True)
+            probs = (weights * (1.0 / total)).astype(B16)
+            out = jnp.dot(probs, value_ref[0, low:high, :], preferred_element_type=F32)
+            mixed[part][
+                jnp.bitwise_xor(core, half),
+                0,
+                inner : inner + block,
+                head * depth : (head + 1) * depth,
+            ] = out.astype(B16)
+            log_ref[0, head, first : first + block, :] = top + jnp.log(total)
+
+
+def attend_back_kernel(parts, heads, depth, block, most, core_ref, *refs):
+    projected = refs[:parts]
+    upstream = refs[parts : 2 * parts]
+    refs = refs[2 * parts :]
+    starts_ref, cosine_ref, sine_ref, query_gain_ref, key_gain_ref = refs[:5]
+    query_ref, key_ref, value_ref, log_ref = refs[5:9]
+    refs = refs[9:]
+    result = refs[:parts]
+    gain_ref, query_acc, key_acc, value_acc = refs[parts:]
+    core = core_ref[0]
+    rows = projected[0].shape[2]
+    length = query_ref.shape[1]
+    scale = depth ** (-0.5)
+    key_acc[...] = jnp.zeros_like(key_acc)
+    value_acc[...] = jnp.zeros_like(value_acc)
+    for first in range(0, length, block):
+        low, high = window(first, block, most)
+        mask = kept(first, block, low, high, starts_ref[0, first : first + block, :])
+        half, left = divmod(first, length // 2)
+        part, inner = divmod(left, rows)
+        keys = key_ref[0, low:high, :]
+        values = value_ref[0, low:high, :]
+        for head in range(heads):
+            lanes = slice(head * depth, (head + 1) * depth)
+            query = query_ref[0, first : first + block, lanes]
+            grad = upstream[part][jnp.bitwise_xor(core, half), 0, inner : inner + block, lanes]
+            scores = rows_dot(query, keys) * scale - log_ref[0, head, first : first + block, :]
+            probs = jnp.where(mask, jnp.exp(jnp.where(mask, scores, 0.0)), 0.0)
+            prob_grad = rows_dot(grad, values)
+            delta = jnp.sum(probs * prob_grad, axis=1, keepdims=True)
+            score_grad = (probs * (prob_grad - delta)).astype(B16)
+            query_acc[first : first + block, lanes] = (
+                jnp.dot(score_grad, keys, preferred_element_type=F32) * scale
+            )
+            key_acc[low:high, :] += weight_grad(score_grad, query) * scale
+            value_acc[low:high, :] += weight_grad(probs.astype(B16), grad)
+    query_total = jnp.zeros((1, depth), F32)
+    key_total = jnp.zeros((1, depth), F32)
+    for half in range(2):
+        place = jnp.bitwise_xor(core, half)
+        for part in range(parts):
+            at = half * (length // 2) + part * rows
+            cosine = cosine_ref[0, at : at + rows, :]
+            sine = sine_ref[0, at : at + rows, :]
+            for head in range(heads + 1):
+                lanes = slice(head * depth, (head + 1) * depth)
+                value = projected[part][place, 0, :, lanes]
+                if head < heads:
+                    grad = query_acc[at : at + rows, lanes]
+                    gain = query_gain_ref[...]
+                else:
+                    grad = key_acc[at : at + rows, :]
+                    gain = key_gain_ref[...]
+                grad = spin_back(grad, cosine, sine)
+                scaled = value * head_scale(value)
+                share = jnp.sum(grad * scaled, axis=0, keepdims=True)
+                if head < heads:
+                    query_total += share
+                else:
+                    key_total += share
+                inner = jnp.mean(gain * grad * scaled, axis=1, keepdims=True)
+                back = head_scale(value) * (gain * grad - scaled * inner)
+                result[part][place, 0, :, lanes] = back.astype(B16)
+            result[part][place, 0, :, (heads + 1) * depth :] = value_acc[
+                at : at + rows, :
+            ].astype(B16)
+    gain_ref[0, 0:1, :] = query_total
+    gain_ref[0, 1:2, :] = key_total
+
+
+def by_sequence(shape):
+    return pl.BlockSpec((1,) + shape[1:], lambda i, core: (i,) + (0,) * (len(shape) - 1))
+
+
+def by_block(shape):
+    return pl.BlockSpec((shape[0], 1) + shape[2:], lambda i, core: (0, i, 0, 0))
+
+
+def fixed(shape):
+    return pl.BlockSpec(shape, lambda i, core: (0,) * len(shape))
+
+
+def attend_sizes(projected, cosine, depth):
+    parts = len(projected)
+    heads = projected[0].shape[3] // depth - 2
+    rows = projected[0].shape[2]
+    length = cosine.shape[1]
+    return parts, heads, rows, length, min(rows, 256)
+
+
+def attend(projected, core, starts, cosine, sine, query_gain, key_gain, most):
+    depth = query_gain.shape[1]
+    parts, heads, rows, length, block = attend_sizes(projected, cosine, depth)
+    common = (starts, cosine, sine)
+    outs = [jax.ShapeDtypeStruct((2, 2, rows, heads * depth), B16)] * parts + [
+        jax.ShapeDtypeStruct((2, length, heads * depth), B16),
+        jax.ShapeDtypeStruct((2, length, depth), B16),
+        jax.ShapeDtypeStruct((2, length, depth), B16),
+        jax.ShapeDtypeStruct((2, heads, length, 1), F32),
+    ]
+    made = pl.pallas_call(
+        lambda *refs: attend_kernel(parts, heads, depth, block, most, *refs),
+        out_shape=outs,
+        grid_spec=pltpu.PrefetchScalarGridSpec(
+            num_scalar_prefetch=1,
+            grid=(2,),
+            in_specs=[by_block(item.shape) for item in projected]
+            + [by_sequence(item.shape) for item in common]
+            + [fixed(query_gain.shape)] * 2,
+            out_specs=[by_block(item.shape) for item in outs[:parts]]
+            + [by_sequence(item.shape) for item in outs[parts:]],
+        ),
+        compiler_params=pltpu.CompilerParams(vmem_limit_bytes=48 * 1024 * 1024),
+        cost_estimate=pl.CostEstimate(
+            flops=8 * length * length * depth * heads // 2 * 2,
+            bytes_accessed=16 * 1024 * 1024,
+            transcendentals=2 * heads * length * length // 2,
+        ),
+    )(core, *projected, *common, query_gain, key_gain)
+    return made[:parts], made[parts:]
+
+
+def attend_back(projected, upstream, saved, core, starts, cosine, sine, query_gain, key_gain, most):
+    depth = query_gain.shape[1]
+    parts, heads, rows, length, block = attend_sizes(projected, cosine, depth)
+    common = (starts, cosine, sine)
+    outs = [jax.ShapeDtypeStruct((2, 2, rows, (heads + 2) * depth), B16)] * parts + [
+        jax.ShapeDtypeStruct((2, 8, depth), F32)
+    ]
+    made = pl.pallas_call(
+        lambda *refs: attend_back_kernel(parts, heads, depth, block, most, *refs),
+        out_shape=outs,
+        grid_spec=pltpu.PrefetchScalarGridSpec(
+            num_scalar_prefetch=1,
+            grid=(2,),
+            in_specs=[by_block(item.shape) for item in projected]
+            + [by_block(item.shape) for item in upstream]
+            + [by_sequence(item.shape) for item in common]
+            + [fixed(query_gain.shape)] * 2
+            + [by_sequence(item.shape) for item in saved],
+            out_specs=[by_block(item.shape) for item in outs[:parts]]
+            + [by_sequence(item.shape) for item in outs[parts:]],
+            scratch_shapes=[
+                pltpu.VMEM((length, heads * depth), F32),
+                pltpu.VMEM((length, depth), F32),
+                pltpu.VMEM((length, depth), F32),
+            ],
+        ),
+        compiler_params=pltpu.CompilerParams(vmem_limit_bytes=48 * 1024 * 1024),
+        cost_estimate=pl.CostEstimate(
+            flops=20 * length * length * depth * heads // 2 * 2,
+            bytes_accessed=20 * 1024 * 1024,
+            transcendentals=2 * heads * length * length // 2,
+        ),
+    )(core, *projected, *upstream, *common, query_gain, key_gain, *saved)
+    return made[:parts], made[parts]
+
+
+def neighbours():
+    spot = lax.axis_index("tx")
+    core = lax.rem(spot, 2)
+    return (
+        {"ty": 1 - lax.axis_index("ty")},
+        {"tx": lax.rem(spot + 2, 4)},
+        {"tx": spot + 1 - 2 * core},
+    )
+
+
+def greet(targets):
+    barrier = pltpu.get_barrier_semaphore()
+    for target in targets:
+        pl.semaphore_signal(barrier, inc=1, device_id=target, device_id_type=MESH)
+    pl.semaphore_wait(barrier, len(targets))
+
+
+class Wires:
+    def __init__(self, send_sems, recv_sems):
+        self.send_sems = send_sems
+        self.recv_sems = recv_sems
+
+    def copy(self, kind, chunk, source, target, device):
+        return pltpu.make_async_remote_copy(
+            src_ref=source,
+            dst_ref=target,
+            send_sem=self.send_sems.at[kind, chunk],
+            recv_sem=self.recv_sems.at[kind, chunk],
+            device_id=device,
+            device_id_type=MESH,
+        )
+
+
+CHUNK = 256
+SIBLING, CORNER, FINAL_X, FINAL_Y = 0, 1, 2, 3
+REDUCE_KINDS = 4
+OUT_X, OUT_Y, OUT_CORNER, CORE_OWN, CORE_X, CORE_Y, CORE_CORNER = range(7)
+GATHER_KINDS = 7
+
+
+def lanes(chunk, half, width):
+    return pl.ds(pl.multiple_of(half * width + chunk * CHUNK, CHUNK), CHUNK)
+
+
+class Gather:
+    def __init__(self, wires, base, whole, own, local_sem):
+        self.wires, self.base, self.whole, self.own, self.local_sem = (
+            wires,
+            base,
+            whole,
+            own,
+            local_sem,
+        )
+        self.width = whole.shape[2] // 2
+        self.count = self.width // CHUNK
+
+    def place(self, block, chunk, half):
+        return self.whole.at[block, :, lanes(chunk, half, self.width)]
+
+    def copy(self, name, chunk):
+        side, across, core = neighbours()
+        at = self.place
+        own = self.own.at[chunk]
+        if name == "local":
+            return pltpu.make_async_copy(own, at(0, chunk, 0), self.local_sem.at[chunk])
+        kind, source, target, device = {
+            "x": (OUT_X, own, at(0, chunk, 1), side),
+            "y": (OUT_Y, own, at(1, chunk, 0), across),
+            "core": (CORE_OWN, own, at(2, chunk, 0), core),
+            "even": (OUT_CORNER, at(0, chunk, 1), at(1, chunk, 1), across),
+            "odd": (OUT_CORNER, at(1, chunk, 0), at(1, chunk, 1), side),
+            "core_x": (CORE_X, at(0, chunk, 1), at(2, chunk, 1), core),
+            "core_y": (CORE_Y, at(1, chunk, 0), at(3, chunk, 0), core),
+            "core_corner": (CORE_CORNER, at(1, chunk, 1), at(3, chunk, 1), core),
+        }[name]
+        return self.wires.copy(self.base + kind, chunk, source, target, device)
+
+    def send(self, chunk):
+        for name in ("x", "y", "core", "local"):
+            self.copy(name, chunk).start()
+
+    def finish(self):
+        @pl.loop(0, self.count)
+        def _(chunk):
+            even = lax.rem(chunk, 2) == 0
+            self.copy("x", chunk).wait_recv()
+
+            @pl.when(even)
+            def _():
+                self.copy("even", chunk).start()
+
+            self.copy("core_x", chunk).start()
+            self.copy("y", chunk).wait_recv()
+
+            @pl.when(jnp.logical_not(even))
+            def _():
+                self.copy("odd", chunk).start()
+
+            self.copy("core_y", chunk).start()
+
+        @pl.loop(0, self.count)
+        def _(chunk):
+            self.copy("even", chunk).wait_recv()
+            self.copy("core_corner", chunk).start()
+
+        @pl.loop(0, self.count)
+        def _(chunk):
+            for name in ("core", "core_x", "core_y", "core_corner"):
+                self.copy(name, chunk).wait_recv()
+            for name in ("x", "y", "core", "even", "core_x", "core_y", "core_corner"):
+                self.copy(name, chunk).wait_send()
+            self.copy("local", chunk).wait()
+
+
+def reduce_stage(wires, rows_ref, weight_ref, transposed, bufs):
+    sibling_send, sibling_recv, kept_ref, send, corner_recv, x_recv, y_recv = bufs
+    side, across, core = neighbours()
+    rows, depth = rows_ref.shape[1:]
+    width = (weight_ref.shape[0] if transposed else weight_ref.shape[1]) // 2
+    count = width // CHUNK
+
+    def product(block, chunk, half):
+        left = rows_ref[block : block + 2].reshape(2 * rows, depth)
+        at = lanes(chunk, half, width)
+        if transposed:
+            return rows_dot(left, weight_ref[at, :])
+        return jnp.dot(left, weight_ref[:, at], preferred_element_type=F32)
+
+    def sibling(chunk):
+        return wires.copy(SIBLING, chunk, sibling_send.at[chunk], sibling_recv.at[chunk], core)
+
+    def corner(chunk, device):
+        return wires.copy(CORNER, chunk, send.at[2, chunk], corner_recv.at[chunk], device)
+
+    def final_x(chunk):
+        return wires.copy(FINAL_X, chunk, send.at[0, chunk], x_recv.at[chunk], side)
+
+    def final_y(chunk):
+        return wires.copy(FINAL_Y, chunk, send.at[1, chunk], y_recv.at[chunk], across)
+
+    @pl.loop(0, count)
+    def _(chunk):
+        @pl.loop(0, 2)
+        def _(half):
+            sibling_send[chunk, half] = product(2, chunk, half).astype(B16)
+
+        sibling(chunk).start()
+
+    @pl.loop(0, count)
+    def _(chunk):
+        even = lax.rem(chunk, 2) == 0
+        sibling(chunk).wait_recv()
+
+        @pl.loop(0, 2)
+        def _(half):
+            total = product(0, chunk, half) + sibling_recv[chunk, half].astype(F32)
+
+            @pl.when(half == 1)
+            def _():
+                send[0, chunk] = total[:rows].astype(B16)
+                send[2, chunk] = total[rows:].astype(B16)
+
+            @pl.when(half == 0)
+            def _():
+                kept_ref[chunk] = total[:rows]
+                send[1, chunk] = total[rows:].astype(B16)
+
+        @pl.when(even)
+        def _():
+            corner(chunk, side).start()
+            final_x(chunk).start()
+
+        @pl.when(jnp.logical_not(even))
+        def _():
+            corner(chunk, across).start()
+            final_y(chunk).start()
+
+    @pl.loop(0, count)
+    def _(chunk):
+        even = lax.rem(chunk, 2) == 0
+        corner(chunk, side).wait_recv()
+
+        @pl.when(even)
+        def _():
+            send[1, chunk] = (send[1, chunk].astype(F32) + corner_recv[chunk].astype(F32)).astype(
+                B16
+            )
+            final_y(chunk).start()
+
+        @pl.when(jnp.logical_not(even))
+        def _():
+            send[0, chunk] = (send[0, chunk].astype(F32) + corner_recv[chunk].astype(F32)).astype(
+                B16
+            )
+            final_x(chunk).start()
+
+    def total(chunk):
+        final_x(chunk).wait_recv()
+        final_y(chunk).wait_recv()
+        return kept_ref[chunk] + x_recv[chunk].astype(F32) + y_recv[chunk].astype(F32)
+
+    def finish():
+        @pl.loop(0, count)
+        def _(chunk):
+            sibling(chunk).wait_send()
+            corner(chunk, side).wait_send()
+            final_x(chunk).wait_send()
+            final_y(chunk).wait_send()
+
+    return total, finish
+
+
+def reduce_scratch(rows, width):
+    count = width // CHUNK
+    return [
+        pltpu.VMEM((count, 2, 2 * rows, CHUNK), B16),
+        pltpu.VMEM((count, 2, 2 * rows, CHUNK), B16),
+        pltpu.VMEM((count, rows, CHUNK), F32),
+        pltpu.VMEM((3, count, rows, CHUNK), B16),
+        pltpu.VMEM((count, rows, CHUNK), B16),
+        pltpu.VMEM((count, rows, CHUNK), B16),
+        pltpu.VMEM((count, rows, CHUNK), B16),
+    ]
+
+
+def wire_scratch(kinds, count):
+    return [pltpu.SemaphoreType.DMA((kinds, count))] * 2
+
+
+IN_VMEM = pl.BlockSpec(memory_space=pltpu.VMEM)
+IN_ANY = pl.BlockSpec(memory_space=pl.ANY)
+VMEM_MOST = 58 * 1024 * 1024
+
+
+def remote_params(number):
+    return pltpu.CompilerParams(
+        collective_id=number, has_side_effects=True, vmem_limit_bytes=VMEM_MOST
+    )
+
+
+def gather_kernel(block_ref, whole_ref, own, send_sems, recv_sems, local_sem):
+    count = own.shape[0]
+    for chunk in range(count):
+        own[chunk] = block_ref[:, chunk * CHUNK : (chunk + 1) * CHUNK]
+    greet(neighbours())
+    gather = Gather(Wires(send_sems, recv_sems), 0, whole_ref, own, local_sem)
+
+    @pl.loop(0, count)
+    def _(chunk):
+        gather.send(chunk)
+
+    gather.finish()
+
+
+def gather_call(block, number):
+    rows, width = block.shape
+    count = width // CHUNK
+    return pl.pallas_call(
+        gather_kernel,
+        out_shape=jax.ShapeDtypeStruct((4, rows, 2 * width), B16),
+        in_specs=[IN_VMEM],
+        out_specs=IN_ANY,
+        scratch_shapes=[pltpu.VMEM((count, rows, CHUNK), B16)]
+        + wire_scratch(GATHER_KINDS, count)
+        + [pltpu.SemaphoreType.DMA((count,))],
+        compiler_params=remote_params(number),
+        cost_estimate=pl.CostEstimate(
+            flops=0, bytes_accessed=16 * rows * width * 2, transcendentals=0
+        ),
+    )(block)
+
+
+def branch_kernel(
+    rows_ref, weight_ref, input_ref, residual_ref, whole_ref, *scratch
+):
+    bufs = scratch[:7]
+    own, send_sems, recv_sems, local_sem = scratch[7:]
+    width = input_ref.shape[1]
+    greet(neighbours())
+    wires = Wires(send_sems, recv_sems)
+    total, finish = reduce_stage(wires, rows_ref, weight_ref, False, bufs)
+    gather = Gather(wires, REDUCE_KINDS, whole_ref, own, local_sem)
+
+    @pl.loop(0, width // CHUNK)
+    def _(chunk):
+        at = lanes(chunk, 0, width)
+        residual = input_ref[:, at].astype(F32) + total(chunk)
+        residual_ref[:, at] = residual
+        own[chunk] = residual.astype(B16)
+        gather.send(chunk)
+
+    gather.finish()
+    finish()
+
+
+def branch_call(rows, weight, inputs, number):
+    count = inputs.shape[1] // CHUNK
+    height, width = inputs.shape
+    return pl.pallas_call(
+        branch_kernel,
+        out_shape=(
+            jax.ShapeDtypeStruct((height, width), F32),
+            jax.ShapeDtypeStruct((4, height, 2 * width), B16),
+        ),
+        in_specs=[IN_VMEM] * 3,
+        out_specs=(IN_VMEM, IN_ANY),
+        scratch_shapes=reduce_scratch(height, width)
+        + [pltpu.VMEM((count, height, CHUNK), B16)]
+        + wire_scratch(REDUCE_KINDS + GATHER_KINDS, count)
+        + [pltpu.SemaphoreType.DMA((count,))],
+        compiler_params=remote_params(number),
+        cost_estimate=pl.CostEstimate(
+            flops=2 * 4 * height * rows.shape[2] * 2 * width,
+            bytes_accessed=32 * height * width * 2,
+            transcendentals=0,
+        ),
+    )(rows, weight, inputs)
+
+
+def share_stats(wires, base, stats_ref, recv):
+    side, across, core = neighbours()
+    first = wires.copy(base, 0, stats_ref.at[2:4], recv.at[0:2], core)
+    first.start()
+    first.wait()
+    stats_ref[0:2] = stats_ref[0:2] + recv[0:2]
+    second = wires.copy(base, 1, stats_ref.at[1:2], recv.at[2:3], across)
+    second.start()
+    second.wait()
+    stats_ref[0:1] = stats_ref[0:1] + recv[2:3]
+    third = wires.copy(base, 2, stats_ref.at[0:1], recv.at[3:4], side)
+    third.start()
+    third.wait()
+    stats_ref[0:1] = stats_ref[0:1] + recv[3:4]
+
+
+def stand(row):
+    return jnp.transpose(jnp.broadcast_to(row, (row.shape[1], row.shape[1])))
+
+
+def pull_kernel(
+    gathers,
+    rows_ref,
+    weight_ref,
+    stats_in_ref,
+    scale_ref,
+    value_ref,
+    gain_ref,
+    base_ref,
+    *refs,
+):
+    if gathers:
+        result_ref, gain_grad_ref, whole_ref = refs[:3]
+        scratch = refs[3:]
+    else:
+        result_ref, gain_grad_ref = refs[:2]
+        scratch = refs[2:]
+    bufs = scratch[:7]
+    stats_ref, stats_recv, column_ref, send_sems, recv_sems = scratch[7:12]
+    rows, width = value_ref.shape
+    stats_ref[...] = stats_in_ref[...]
+    greet(neighbours())
+    wires = Wires(send_sems, recv_sems)
+    total, finish = reduce_stage(wires, rows_ref, weight_ref, True, bufs)
+    share_stats(wires, REDUCE_KINDS, stats_ref, stats_recv)
+    for part in range(rows // 128):
+        at = slice(part * 128, (part + 1) * 128)
+        scale = stand(scale_ref[part : part + 1, :])
+        column_ref[0, at, :] = scale
+        column_ref[1, at, :] = (
+            stand(stats_ref[0, part : part + 1, :]) * scale * scale / (2 * width)
+        )
+    if gathers:
+        own, local_sem = scratch[12:]
+        gather = Gather(wires, REDUCE_KINDS + 1, whole_ref, own, local_sem)
+
+    @pl.loop(0, width // CHUNK)
+    def _(chunk):
+        at = lanes(chunk, 0, width)
+        upstream = total(chunk)
+        value = value_ref[:, at].astype(F32)
+        scale = column_ref[0, :, 0:1]
+        pulled = base_ref[:, at].astype(F32) + (
+            scale * gain_ref[:, at] * upstream - value * column_ref[1, :, 0:1]
+        )
+        gain_grad_ref[:, at] = jnp.sum(upstream * value * scale, axis=0, keepdims=True)
+        result_ref[:, at] = pulled.astype(result_ref.dtype)
+        if gathers:
+            own[chunk] = pulled.astype(B16)
+            gather.send(chunk)
+
+    if gathers:
+        gather.finish()
+    finish()
+
+
+def pull_call(rows, weight, stats, scale, value, gain, base, gathers, kind, number):
+    height, width = value.shape
+    count = width // CHUNK
+    outs = [
+        jax.ShapeDtypeStruct((height, width), kind),
+        jax.ShapeDtypeStruct((1, width), F32),
+    ]
+    scratch = reduce_scratch(height, width) + [
+        pltpu.VMEM((4, 8, 128), F32),
+        pltpu.VMEM((4, 8, 128), F32),
+        pltpu.VMEM((2, height, 128), F32),
+    ]
+    specs = [IN_VMEM] * 2
+    if gathers:
+        outs.append(jax.ShapeDtypeStruct((4, height, 2 * width), B16))
+        specs.append(IN_ANY)
+        scratch += wire_scratch(REDUCE_KINDS + 1 + GATHER_KINDS, count)
+        scratch += [
+            pltpu.VMEM((count, height, CHUNK), B16),
+            pltpu.SemaphoreType.DMA((count,)),
+        ]
+    else:
+        scratch += wire_scratch(REDUCE_KINDS + 1, count)
+    return pl.pallas_call(
+        lambda *refs: pull_kernel(gathers, *refs),
+        out_shape=tuple(outs),
+        in_specs=[IN_VMEM] * 7,
+        out_specs=tuple(specs),
+        scratch_shapes=scratch,
+        compiler_params=remote_params(number),
+        cost_estimate=pl.CostEstimate(
+            flops=2 * 4 * height * rows.shape[2] * 2 * width,
+            bytes_accessed=32 * height * width * 2,
+            transcendentals=0,
+        ),
+    )(rows, weight, stats, scale, value, gain, base)
+
+
+def sum_kernel(rows_ref, weight_ref, base_ref, result_ref, *scratch):
+    bufs = scratch[:7]
+    width = base_ref.shape[1]
+    greet(neighbours())
+    total, finish = reduce_stage(Wires(*scratch[7:]), rows_ref, weight_ref, False, bufs)
+
+    @pl.loop(0, width // CHUNK)
+    def _(chunk):
+        at = lanes(chunk, 0, width)
+        result_ref[:, at] = (base_ref[:, at] + total(chunk)).astype(B16)
+
+    finish()
+
+
+def sum_call(rows, weight, base, number):
+    height, width = base.shape
+    count = width // CHUNK
+    return pl.pallas_call(
+        sum_kernel,
+        out_shape=jax.ShapeDtypeStruct((height, width), B16),
+        in_specs=[IN_VMEM] * 3,
+        out_specs=IN_VMEM,
+        scratch_shapes=reduce_scratch(height, width) + wire_scratch(REDUCE_KINDS, count),
+        compiler_params=remote_params(number),
+        cost_estimate=pl.CostEstimate(
+            flops=2 * 4 * height * rows.shape[2] * 2 * width,
+            bytes_accessed=16 * height * width * 2,
+            transcendentals=0,
+        ),
+    )(rows, weight, base)
+
+
+def whole_norm(whole, gain):
+    value = whole.reshape(-1, whole.shape[2]).astype(F32)
+    scale = lax.rsqrt(jnp.mean(value * value, axis=1) + EPS)
+    return (value * scale[:, None] * gain).astype(B16), scale
+
+
+def as_rows(value):
+    return value.reshape(-1, 128)
+
+
+def as_stats(value):
+    return jnp.pad(value.reshape(4, -1, 128), ((0, 0), (0, 8 - value.shape[0] // 512), (0, 0)))
+
+
+def row_shares(grad):
+    size = grad.shape[0] // (2 * lax.axis_size("dp"))
+    parts = grad.reshape(2, -1, grad.shape[1])
+    return lambda place: lax.dynamic_slice_in_dim(parts, place * size, size, 1)
+
+
+def column_shares(grad):
+    width = grad.shape[1] // 2
+    size = width // lax.axis_size("dp")
+    return lambda place: jnp.stack(
+        [
+            lax.dynamic_slice_in_dim(grad, place * size, size, 1),
+            lax.dynamic_slice_in_dim(grad, width + place * size, size, 1),
+        ]
+    )
+
+
+def meet(shares, axis):
+    return in_order(shares[0], swap_x(shares[1].astype(B16)).astype(F32), axis)
+
+
+def plane_device(
+    tokens,
+    seg_ids,
+    w_query,
+    w_key,
+    w_value,
+    w_out,
+    w_gate,
+    w_up,
+    w_down,
+    attn_gain,
+    mlp_gain,
+    query_gain,
+    key_gain,
+    cotangent,
+):
+    place = lax.axis_index("ty")
+    spot = lax.axis_index("tx")
+    core = lax.rem(spot, 2)
+    depth = query_gain.shape[0]
+    length = seg_ids.shape[1]
+    most = length // 2
+    rows, width = tokens.shape
+    head_width = w_query.shape[1] // 2
+    kv_width = w_key.shape[1] // 2
+    units = w_gate.shape[1] // 2
+
+    def columns(weights, which):
+        return jnp.concatenate([half_of(item, which, 1) for item in weights], axis=1)
+
+    def full(mine, theirs, axis):
+        return jnp.concatenate([mine, swap_x(theirs)], axis=axis)
+
+    w_project = full(
+        columns([w_query, w_key, w_value], place),
+        columns([w_query, w_key, w_value], 1 - place),
+        0,
+    )
+    gains = jnp.stack([attn_gain, mlp_gain])
+    gains = jnp.concatenate([gains, swap_x(gains)], axis=1)
+    seg_theirs = swap_x(seg_ids)
+    token_whole = gather_call(tokens, 0)
+    w_branch = full(half_of(w_out, place, 0), half_of(w_out, 1 - place, 0), 1)
+    w_both = full(columns([w_gate, w_up], place), columns([w_gate, w_up], 1 - place), 0)
+    w_back = full(half_of(w_down, place, 0), half_of(w_down, 1 - place, 0), 1)
+    grad_whole = gather_call(cotangent, 1).reshape(4 * rows, 2 * width)
+
+    seg_all = in_order(seg_ids, seg_theirs, 0)
+    seg_all = jnp.where(lax.div(spot, 2) == 0, seg_all, seg_all[::-1])
+    index = jnp.arange(length, dtype=jnp.int32)[None]
+    edge = jnp.concatenate(
+        [jnp.ones((2, 1), dtype=jnp.bool_), seg_all[:, 1:] != seg_all[:, :-1]], axis=1
+    )
+    starts = lax.cummax(jnp.where(edge, index, 0), axis=1)
+    cosine, sine = rotary(index - starts, depth)
+    cosine = jnp.concatenate([cosine, cosine], axis=-1)
+    sine = jnp.concatenate([-sine, sine], axis=-1)
+    starts = starts[:, :, None]
+    core_arg = core.reshape(1).astype(jnp.int32)
+    fixed_args = (core_arg, starts, cosine, sine, query_gain[None], key_gain[None], most)
+
+    first, first_scale = whole_norm(token_whole, gains[0])
+    projected = forward_with(w_project)(first)
+    blocks = [projected.reshape(2, 2, rows, -1)]
+    mixed, saved = attend(blocks, *fixed_args)
+    attended = mixed[0].reshape(4 * rows, head_width)
+    residual, residual_whole = branch_call(
+        attended.reshape(4, rows, head_width), w_branch, tokens, 2
+    )
+    second, second_scale = whole_norm(residual_whole, gains[1])
+    gate_up = forward_with(w_both)(second)
+    gate = gate_up[:, :units]
+    upper = gate_up[:, units:]
+    sigma = jax.nn.sigmoid(gate)
+    hidden = (gate * sigma * upper).astype(B16)
+    hidden_grad = backward_with(w_back)(grad_whole)
+    gate_grad = hidden_grad * upper * (sigma * (1.0 + gate * (1.0 - sigma)))
+    up_grad = hidden_grad * (gate * sigma)
+    unit_grads = jnp.concatenate([gate_grad, up_grad], axis=1).astype(B16)
+    unit_stats = jnp.sum(unit_grads.astype(F32) * gate_up, axis=1)
+    down_sums = line_reduce(column_shares(weight_grad(hidden, grad_whole).astype(B16)))
+    residual_grad, mlp_gain_part, branch_whole = pull_call(
+        unit_grads.reshape(4, rows, 2 * units),
+        w_both,
+        as_stats(unit_stats),
+        as_rows(second_scale[:rows]),
+        residual,
+        mlp_gain[None],
+        cotangent,
+        True,
+        F32,
+        3,
+    )
+    both_sums = line_reduce(row_shares(weight_grad(second, unit_grads).astype(B16)))
+    branch_whole = branch_whole.reshape(4 * rows, 2 * width)
+    upstream = [
+        backward_with(w_branch)(branch_whole).astype(B16).reshape(2, 2, rows, head_width)
+    ]
+    out_sums = line_reduce(column_shares(weight_grad(attended, branch_whole).astype(B16)))
+    output = sum_call(hidden.reshape(4, rows, units), w_back, residual, 4)
+    proj_grads, gain_parts = attend_back(blocks, upstream, saved, *fixed_args)
+    proj_grads = proj_grads[0].reshape(4 * rows, -1)
+    proj_stats = jnp.sum(proj_grads.astype(F32) * projected, axis=1)
+    input_grad, attn_gain_part = pull_call(
+        proj_grads.reshape(4, rows, -1),
+        w_project,
+        as_stats(proj_stats),
+        as_rows(first_scale[:rows]),
+        tokens,
+        attn_gain[None],
+        residual_grad,
+        False,
+        B16,
+        5,
+    )
+    project_sums = line_reduce(row_shares(weight_grad(first, proj_grads).astype(B16)))
+
+    down_share = meet(down_sums, 0)
+    out_share = meet(out_sums, 0)
+    both_theirs = swap_x(both_sums[1].astype(B16)).astype(F32)
+    project_theirs = swap_x(project_sums[1].astype(B16)).astype(F32)
+    ends = (0, head_width, head_width + kv_width, head_width + 2 * kv_width)
+    query_share, key_share, value_share = (
+        in_order(project_sums[0][:, low:high], project_theirs[:, low:high], 1)
+        for low, high in zip(ends[:-1], ends[1:])
+    )
+    gate_share, up_share = (
+        in_order(both_sums[0][:, low:high], both_theirs[:, low:high], 1)
+        for low, high in ((0, units), (units, 2 * units))
+    )
+    gain_sums = jnp.sum(gain_parts, axis=0)
+    attn_total, mlp_total, query_total, key_total = lax.psum(
+        (widen(attn_gain_part[0]), widen(mlp_gain_part[0]), gain_sums[0], gain_sums[1]),
+        ("dp", "tx", "ty"),
+    )
+    return (
+        output,
+        input_grad,
+        query_share,
+        key_share,
+        value_share,
+        out_share,
+        gate_share,
+        up_share,
+        down_share,
+        attn_total,
+        mlp_total,
+        query_total,
+        key_total,
+    )
+
+
 def solution(mesh):
     placed = (
         P(("dp", "tx"), "ty"),
@@ -331,7 +1311,7 @@
         P(("dp", "tx"), "ty"),
     )
     return jax.shard_map(
-        per_device,
+        plane_device if fits(mesh) else general_device,
         mesh=mesh,
         in_specs=placed,
         out_specs=(

time: 1710 us -> 950 us (0.56)
  waiting for transfers between devices: 1260 us -> 114 us
  Pallas kernels: 0 us -> 453 us
  matrix products: 186 us -> 90.8 us
  starting transfers between devices: 1.76 us -> 61.7 us
  local copies, waits for them, and re-layouts: 72.8 us -> 28.5 us
  other arithmetic: 101 us -> 124 us
    reduce_scatter x15 -> x0, waiting for transfers between devices: 932 us -> none  [the longest x4 552 us: width_reduce(): return lax.psum_scatter(apply(whole), 'ty', scatter_dimension=0, tiled=True)]
    pallas_call x0 -> x8, Pallas kernels: none -> 453 us  [the longest x2 148 us: pull_call(): pl.pallas_call(lambda *refs: pull_kernel(gathers, *refs), out_shape=tuple...]
    all_gather x8 -> x0, waiting for transfers between devices: 320 us -> none  [the longest x4 211 us: branch_gather(): return lax.all_gather(rows, 'ty', axis=0, tiled=True)]
    ppermute x0 -> x34, waiting for transfers between devices: none -> 114 us  [the longest x12 77.3 us: line_reduce(): up = lax.ppermute(rise.astype(B16), 'dp', [(i, i + 1) for i in range(step)])]
    ppermute x0 -> x34, starting transfers between devices: none -> 61.7 us  [the longest x12 32.2 us: line_reduce(): up = lax.ppermute(rise.astype(B16), 'dp', [(i, i + 1) for i in range(step)])]
    dot_general x14 -> x0, matrix products: 48 us -> none  [the longest x4 11.5 us: block_scores(): jnp.einsum('qkgd,mkd->kgqm', part, seq_keys, preferred_element_type=F32)]
    dot_general x4 -> x2, matrix products: 46.7 us -> 18.3 us  [backward_with(): lax.dot_general(rows, weight, (((1,), (1,)), ((), ())), preferred_element...]
    concatenate x6 -> x17, other arithmetic: 10.7 us -> 38.8 us  [the longest x4 22.9 us: full(): return jnp.concatenate([mine, swap_x(theirs)], axis=axis)]
  transfers between devices with their start and end apart: 23 -> 34, of which waited for: 22 -> 10; matrix products, arithmetic and copies ran while one was open for 12% -> 14% of each run, Pallas kernels for 0% -> 38%
where the time goes in v1:
time: 950 us; the launch traced here: 943 us
  Pallas kernels  453 us (48%)
  other arithmetic  124 us (13%)
  waiting for transfers between devices  114 us (12%)
  matrix products  90.8 us (10%)
  blocking collectives  69.8 us (7%)
  starting transfers between devices  61.7 us (6%)
  local copies, waits for them, and re-layouts  28.5 us (3%)
    pallas_call x2, Pallas kernels, pull_call(): pl.pallas_call(lambda *refs: pull_kernel(gathers, *refs), out_shape=tuple...  148 us
    pallas_call x2, Pallas kernels, gather_call(): pl.pallas_call(gather_kernel, out_shape=jax.ShapeDtypeStruct((4, rows, 2...  135 us
    pallas_call x1, Pallas kernels, branch_call(): pl.pallas_call(branch_kernel, out_shape=(jax.ShapeDtypeStruct((height, wi...  85.1 us
    ppermute x12, waiting for transfers between devices, line_reduce(): up = lax.ppermute(rise.astype(B16), 'dp', [(i, i + 1) for i in range(step)])  77.3 us
    psum x1, blocking collectives, plane_device(): lax.psum((widen(attn_gain_part[0]), widen(mlp_gain_part[0]), gain_sums[0]...  69.8 us
    pallas_call x1, Pallas kernels, sum_call(): pl.pallas_call(sum_kernel, out_shape=jax.ShapeDtypeStruct((height, width)...  49.1 us
    dot_general x4, matrix products, weight_grad(): lax.dot_general(left, right, (((0,), (0,)), ((), ())), preferred_element_...  42.8 us
    ppermute x12, starting transfers between devices, line_reduce(): up = lax.ppermute(rise.astype(B16), 'dp', [(i, i + 1) for i in range(step)])  32.2 us
  transfers between devices with their start and end apart: 34, of which 10 were waited for; matrix products, arithmetic and copies ran while one was open for 14% of the time, Pallas kernels for 38%

profile of v1, /device:TPU:10, one launch (start us, length us, event | category | flops | bytes accessed | tf_op | source)
XLA Modules:
  0.0 943.4 jit_solution(8599103949133909937)
XLA Ops:
  16.8 94.3 %shard_map.237 = bf16[4,512,2048]{2,1,0:T(8,128)(2,1)} custom-call(bf16[512,1024]{1,0:T(8,128)(2,1)} %refs_4_.1), custom_call_target="tpu_custom_call" | custom-call | bytes 16777216 | tf_op jit(solution)/shard_map/pallas_call | solution.py:901
  111.2 5.2 multiply_reduce_fusion.1
  121.0 40.5 %shard_map.241 = bf16[4,512,2048]{2,1,0:T(8,128)(2,1)} custom-call(bf16[512,1024]{1,0:T(8,128)(2,1)} %refs_6_.1), custom_call_target="tpu_custom_call" | custom-call | bytes 16777216 | tf_op jit(solution)/shard_map/pallas_call | solution.py:901
  165.2 3.7 fusion.18
  171.5 8.7 fusion.3
  180.2 8.8 multiply_convert_fusion
  191.2 10.4 %fusion.27 = f32[2048,512]{1,0:T(8,128)} fusion(bf16[2048,2048]{1,0:T(8,128)(2,1)} %fusion.3, bf16[1024,512]{1,0:T(8,128)(2,1)} %collective-permute-done.1, bf16[1024,128]{1,0:T(8,128)(2,1)S(1)} %get-tuple-element.96, bf16[1024,128]{1,0:T(8,128)(2,1)S(1)} %copy-done.34, bf16[1024,256]{1,0:T(8,128)(2,1)S(1)} %copy-done.23), kind=kOutput, calls=%fused_computation.161 | convolution fusion | flops 4303355904 | bytes 14680064 | tf_op jit(solution)/shard_map/dot_general | solution.py:39
  201.6 14.8 %shard_map.238 = (bf16[2,2,512,256]{3,2,1,0:T(8,128)(2,1)S(1)}, bf16[2,1024,256]{2,1,0:T(8,128)(2,1)S(1)}, bf16[2,1024,128]{2,1,0:T(8,128)(2,1)S(1)}, bf16[2,1024,128]{2,1,0:T(8,128)(2,1)S(1)}, f32[2,2,1024,1]{3,2,1,0:T(8,128)}) custom-call(s32[1]{0:T(128)} %bitcast.refs_0_, f32[2,2,512,512]{3,2,1,0:T(8,128)} %bitcast.172, ...), custom_call_target="tpu_custom_call" | custom-call | flops 2147483648 | bytes 16777216 | tf_op jit(solution)/shard_map/pallas_call | solution.py:586
  218.3 85.1 %shard_map.239 = (f32[512,1024]{1,0:T(8,128)}, bf16[4,512,2048]{2,1,0:T(8,128)(2,1)}) custom-call(bf16[4,512,256]{2,1,0:T(8,128)(2,1)} %bitcast.138, bf16[256,2048]{1,0:T(8,128)(2,1)} %pad_maximum_fusion.13.weight_ref, bf16[512,1024]{1,0:T(8,128)(2,1)} %refs_4_.1), custom_call_target="tpu_custom_call" | custom-call | flops 2147483648 | bytes 33554432 | tf_op jit(solution)/shard_map/pallas_call | solution.py:942
  303.5 5.1 multiply_reduce_fusion
  309.2 2.7 pad_maximum_fusion.6.refs_1_
  311.9 8.8 fusion.1
  320.8 3.5 pad_maximum_fusion.5.weight_ref
  324.3 19.2 %fusion.28 = f32[2048,1536]{1,0:T(8,128)} fusion(bf16[2048,2048]{1,0:T(8,128)(2,1)} %fusion.1, bf16[1024,1536]{1,0:T(8,128)(2,1)} %collective-permute-done.4, bf16[1024,768]{1,0:T(8,128)(2,1)S(1)} %copy-done.8, bf16[1024,768]{1,0:T(8,128)(2,1)} %get-tuple-element.118), kind=kOutput, calls=%fused_computation.162 | convolution fusion | flops 12903776256 | bytes 27262976 | tf_op jit(solution)/shard_map/dot_general | solution.py:39
  343.6 14.7 %fusion.5 = (bf16[2048,768]{1,0:T(8,128)(2,1)}, bf16[2048,768]{1,0:T(8,128)(2,1)}, bf16[2048,768]{1,0:T(8,128)(2,1)}) fusion(f32[2048,1536]{1,0:T(8,128)} %fusion.28, bf16[2048,2048]{1,0:T(8,128)(2,1)S(1)} %bitcast.165, bf16[768,1024]{1,0:T(8,128)(2,1)} %collective-permute-done.5, bf16[768,1024]{1,0:T(8,128)(2,1)} %get-tuple-element.64), kind=kOutput, calls=%fused_computation.17 | convolution fusion | flops 6472335360 | bytes 33554432 | tf_op jit(solution)/shard_map/dot_general | solution.py:43
  358.3 7.7 multiply_reduce_fusion.2
  365.9 19.9 %convolution_convert_fusion = bf16[2048,1536]{1,0:T(8,128)(2,1)} fusion(bf16[2048,2048]{1,0:T(8,128)(2,1)} %fusion.1, bf16[2048,768]{1,0:T(8,128)(2,1)} %get-tuple-element.50, bf16[2048,768]{1,0:T(8,128)(2,1)} %get-tuple-element.49), kind=kOutput, calls=%fused_computation.10 | convolution fusion | flops 12900630528 | bytes 20971520 | tf_op jit(solution)/shard_map/dot_general | solution.py:49
  385.8 10.5 %convolution_convert_fusion.1 = bf16[768,2048]{1,0:T(8,128)(2,1)} fusion(bf16[2048,768]{1,0:T(8,128)(2,1)S(1)} %copy-done.42, bf16[2048,2048]{1,0:T(8,128)(2,1)} %bitcast.162), kind=kOutput, calls=%fused_computation.25 | convolution fusion | flops 6444023808 | bytes 14680064 | tf_op jit(solution)/shard_map/dot_general | solution.py:49
  396.4 3.2 pad_maximum_fusion.1.refs_0_
  400.2 14.5 %pad_maximum_fusion.refs_1_ = bf16[2048,1536]{1,0:T(8,128)(2,1)} fusion(bf16[1024,1536]{1,0:T(8,128)(2,1)} %collective-permute-done.4, bf16[1024,768]{1,0:T(8,128)(2,1)S(1)} %copy-done.9, bf16[1024,768]{1,0:T(8,128)(2,1)S(1)} %copy-done.10), kind=kLoop, calls=%fused_computation.11 | loop fusion | flops 18874368 | bytes 12582912 | tf_op jit(solution)/shard_map/concatenate | solution.py:1175
  414.7 96.4 %shard_map.242 = (f32[512,1024]{1,0:T(8,128)}, f32[1,1024]{1,0:T(1,128)}, bf16[4,512,2048]{2,1,0:T(8,128)(2,1)}) custom-call(bf16[4,512,1536]{2,1,0:T(8,128)(2,1)} %pad_maximum_fusion.1.refs_0_, bf16[2048,1536]{1,0:T(8,128)(2,1)} %pad_maximum_fusion.refs_1_, f32[4,8,128]{2,1,0:T(8,128)} %pad.8.refs_2_, f32[4,128]{1,0:T(4,128)} %bitcast.195, ...), custom_call_target="tpu_custom_call" | custom-call | flops 12884901888 | bytes 33554432 | tf_op jit(solution)/shard_map/pallas_call | solution.py:1062
  511.2 5.9 convolution_convert_fusion.3
  522.1 2.7 constant_dynamic-slice_fusion
  526.2 3.6 convolution_convert_fusion.4
  529.8 20.4 %shard_map.243 = (bf16[2,2,512,512]{3,2,1,0:T(8,128)(2,1)}, f32[2,8,128]{2,1,0:T(8,128)S(1)}) custom-call(s32[1]{0:T(128)} %bitcast.refs_0_, f32[2,2,512,512]{3,2,1,0:T(8,128)} %bitcast.173, bf16[2,2,512,256]{3,2,1,0:T(8,128)(2,1)S(1)} %bitcast.144, s32[2,1024,1]{2,1,0:T(8,128)S(1)} %reduce_window_max.30.refs_2_.refs_3_, ...), custom_call_target="tpu_custom_call" | custom-call | flops 5368709120 | bytes 20971520 | tf_op jit(solution)/shard_map/pallas_call | solution.py:615
  550.3 6.5 convolution_convert_fusion.2
  563.6 49.1 %shard_map.240 = bf16[512,1024]{1,0:T(8,128)(2,1)} custom-call(bf16[4,512,768]{2,1,0:T(8,128)(2,1)} %bitcast.196, bf16[768,2048]{1,0:T(8,128)(2,1)} %pad_maximum_fusion.5.weight_ref, f32[512,1024]{1,0:T(8,128)} %get-tuple-element.29.base_ref.refs_4_), custom_call_target="tpu_custom_call" | custom-call | flops 6442450944 | bytes 16777216 | tf_op jit(solution)/shard_map/pallas_call | solution.py:1094
  615.8 3.7 collective-permute-start.14
  625.0 18.5 %collective-permute-done.14 = bf16[2,256,256]{2,1,0:T(8,128)(2,1)S(1)} collective-permute-done((bf16[2,256,256]{2,1,0:T(8,128)(2,1)S(1)}, bf16[2,256,256]{2,1,0:T(8,128)(2,1)S(1)}, u32[]{:S(2)}, u32[]{:S(2)}) %collective-permute-start.14) | collective-permute-done | bytes 262176 | tf_op jit(solution)/shard_map/ppermute | solution.py:380
  645.6 4.5 collective-permute-start.15
  654.5 3.9 collective-permute-start.18
  658.4 2.6 fusion.10
  663.0 31.1 %collective-permute-done.7 = bf16[2,256,512]{2,1,0:T(8,128)(2,1)S(1)} collective-permute-done((bf16[2,256,512]{2,1,0:T(8,128)(2,1)S(1)}, bf16[2,256,512]{2,1,0:T(8,128)(2,1)S(1)}, u32[]{:S(2)}, u32[]{:S(2)}) %collective-permute-start.7) | collective-permute-done | bytes 524320 | tf_op jit(solution)/shard_map/ppermute | solution.py:380
  696.7 3.6 add_convert_fusion.1
  702.1 51.8 %shard_map.244 = (bf16[512,1024]{1,0:T(8,128)(2,1)}, f32[1,1024]{1,0:T(1,128)}) custom-call(bf16[4,512,512]{2,1,0:T(8,128)(2,1)} %bitcast.175, bf16[2048,512]{1,0:T(8,128)(2,1)} %pad_maximum_fusion.6.refs_1_, f32[4,8,128]{2,1,0:T(8,128)} %pad.9.refs_2_, f32[4,128]{1,0:T(4,128)} %bitcast.194, bf16[512,1024]{1,0:T(8,128)(2,1)} %refs_4_.1, ...), custom_call_target="tpu_custom_call" | custom-call | flops 4294967296 | bytes 33554432 | tf_op jit(solution)/shard_map/pallas_call | solution.py:1062
  764.8 5.3 collective-permute-start.29
  770.1 7.1 collective-permute-done.31
  780.4 3.6 fusion.9
  787.0 69.8 %all-reduce.3 = (f32[2048]{0:T(1024)}, f32[2048]{0:T(1024)}, f32[128]{0:T(128)}, f32[128]{0:T(128)}) all-reduce(f32[2048]{0:T(1024)S(1)} %dynamic_update_slice.6, f32[2048]{0:T(1024)S(1)} %dynamic_update_slice.7, f32[128]{0:T(128)} %get-tuple-element.112, ...), channel_id=1, replica_groups=mesh['dp'=4,'tx'=4,'ty'=2] {'dp','tx','ty'}, use_global_device_ids=true, to_apply=%region_6.7 | all-reduce | flops 4352 | bytes 34816 | tf_op jit(solution)/shard_map/psum | solution.py:1275
  857.7 3.6 collective-permute-start.8
  862.7 2.5 collective-permute-start.11
  867.2 6.2 collective-permute-done.8
  873.4 4.5 collective-permute-done.11
  879.1 3.6 collective-permute-start.22
  888.5 4.9 collective-permute-done.12
  894.3 21.5 %collective-permute-done.22 = bf16[2,256,1536]{2,1,0:T(8,128)(2,1)S(1)} collective-permute-done((bf16[2,256,1536]{2,1,0:T(8,128)(2,1)S(1)}, bf16[2,256,1536]{2,1,0:T(8,128)(2,1)S(1)}, u32[]{:S(2)}, u32[]{:S(2)}) %collective-permute-start.22) | collective-permute-done | bytes 1572896 | tf_op jit(solution)/shard_map/ppermute | solution.py:380
  915.8 4.9 collective-permute-done.25
  923.1 14.7 %collective-permute-done.26 = bf16[256,1536]{1,0:T(8,128)(2,1)S(1)} collective-permute-done((bf16[256,1536]{1,0:T(8,128)(2,1)S(1)}, bf16[256,1536]{1,0:T(8,128)(2,1)S(1)}, u32[]{:S(2)}, u32[]{:S(2)}) %collective-permute-start.26) | collective-permute-done | bytes 786464 | tf_op jit(solution)/shard_map/ppermute | solution.py:327
  (244 shorter events, 102.9 us)
Async XLA Ops:
  0.6 160.9 %collective-permute-start.2 = (s32[1,1024]{1,0:T(1,128)}, s32[1,1024]{1,0:T(1,128)S(1)}, u32[]{:S(2)}, u32[]{:S(2)}) collective-permute-start(s32[1,1024]{1,0:T(1,128)} %param.15), channel_id=1, source_target_pairs={{0,1},{1,0},{2,3},{3,2},{4,5},{5,4},{6,7},{7,6},{8,9},{9,8},{10,11... | collective-permute-start | bytes 12296 | tf_op jit(solution)/shard_map/ppermute | solution.py:327
  2.0 169.4 %collective-permute-start = (f32[2,1024]{1,0:T(2,128)S(1)}, f32[2,1024]{1,0:T(2,128)S(1)}, u32[]{:S(2)}, u32[]{:S(2)}) collective-permute-start(f32[2,1024]{1,0:T(2,128)S(1)} %pad_maximum_fusion.25), channel_id=1, source_target_pairs={{0,1},{1,0},{2,3},{3,2},{4,5},{5,4},{6,7},{7,6},{8,9},{9,8},{10,11... | collective-permute-start | bytes 24584 | tf_op jit(solution)/shard_map/ppermute | solution.py:327
  5.8 183.2 %collective-permute-start.3 = (bf16[256,1024]{1,0:T(8,128)(2,1)}, bf16[256,1024]{1,0:T(8,128)(2,1)}, u32[]{:S(2)}, u32[]{:S(2)}) collective-permute-start(bf16[256,1024]{1,0:T(8,128)(2,1)} %get-tuple-element.87), channel_id=1, source_target_pairs={{0,1},{1,0},{2,3},{3,2},{4,5},{5,4},{6,7},{7,6},{8,9},{9,8},{10,11... | collective-permute-start | bytes 1572872 | tf_op jit(solution)/shard_map/ppermute | solution.py:327
  12.8 178.4 %collective-permute-start.1 = (bf16[1024,512]{1,0:T(8,128)(2,1)}, bf16[1024,512]{1,0:T(8,128)(2,1)}, u32[]{:S(2)}, u32[]{:S(2)}) collective-permute-start(bf16[1024,512]{1,0:T(8,128)(2,1)} %pad_maximum_fusion.10), channel_id=1, source_target_pairs={{0,1},{1,0},{2,3},{3,2},{4,5},{5,4},{6,7},{7,6},{8,9},{9,8},{10,11... | collective-permute-start | bytes 3145736 | tf_op jit(solution)/shard_map/ppermute | solution.py:327
  16.3 304.5 %collective-permute-start.5 = (bf16[768,1024]{1,0:T(8,128)(2,1)}, bf16[768,1024]{1,0:T(8,128)(2,1)}, u32[]{:S(2)}, u32[]{:S(2)}) collective-permute-start(bf16[768,1024]{1,0:T(8,128)(2,1)} %get-tuple-element.65), channel_id=1, source_target_pairs={{0,1},{1,0},{2,3},{3,2},{4,5},{5,4},{6,7},{7,6},{8,9},{9,8},{10,11... | collective-permute-start | bytes 4718600 | tf_op jit(solution)/shard_map/ppermute | solution.py:327
  121.0 42.1 %copy-start.41 = (s32[1,1024]{1,0:T(1,128)S(1)}, s32[1,1024]{1,0:T(1,128)}, u32[]{:S(2)}) copy-start(s32[1,1024]{1,0:T(1,128)} %param.15) | copy-start | bytes 12292
  161.6 162.7 %collective-permute-start.4 = (bf16[1024,1536]{1,0:T(8,128)(2,1)}, bf16[1024,1536]{1,0:T(8,128)(2,1)}, u32[]{:S(2)}, u32[]{:S(2)}) collective-permute-start(bf16[1024,1536]{1,0:T(8,128)(2,1)} %pad_maximum_fusion.4), channel_id=1, source_target_pairs={{0,1},{1,0},{2,3},{3,2},{4,5},{5,4},{6,7},{7,6},{8,9},{9,8},{10,11... | collective-permute-start | bytes 9437192 | tf_op jit(solution)/shard_map/ppermute | solution.py:327
  320.7 22.8 %slice-start.6 = ((s8[8388608]{0:T(1024)(128)(4,1)}), s8[4194304]{0:T(1024)(128)(4,1)S(1)}, s32[]{:S(2)}) async-start(s8[8388608]{0:T(1024)(128)(4,1)} %bitcast.163), calls=%async_computation.6 | async-start | bytes 8388608
  414.7 96.5 %copy-start.1 = (bf16[2,2,512,256]{3,2,1,0:T(8,128)(2,1)S(1)}, bf16[2,2,512,256]{3,2,1,0:T(8,128)(2,1)}, u32[]{:S(2)}) copy-start(bf16[2,2,512,256]{3,2,1,0:T(8,128)(2,1)} %copy-done) | copy-start | bytes 3145732
  518.7 94.1 %collective-permute-start.16 = (bf16[2,256,256]{2,1,0:T(8,128)(2,1)}, bf16[2,256,256]{2,1,0:T(8,128)(2,1)}, u32[]{:S(2)}, u32[]{:S(2)}) collective-permute-start(bf16[2,256,256]{2,1,0:T(8,128)(2,1)} %pad_maximum_fusion.21), channel_id=1, source_target_pairs={{24,16},{25,17},{26,18},{27,19},{28,20},{29,21},{30,22},{31,23}} | collective-permute-start | bytes 786440 | tf_op jit(solution)/shard_map/ppermute | solution.py:381
  520.8 93.5 %collective-permute-start.13 = (bf16[2,256,256]{2,1,0:T(8,128)(2,1)}, bf16[2,256,256]{2,1,0:T(8,128)(2,1)}, u32[]{:S(2)}, u32[]{:S(2)}) collective-permute-start(bf16[2,256,256]{2,1,0:T(8,128)(2,1)} %pad_maximum_fusion.23), channel_id=1, source_target_pairs={{0,8},{1,9},{2,10},{3,11},{4,12},{5,13},{6,14},{7,15}} | collective-permute-start | bytes 786440 | tf_op jit(solution)/shard_map/ppermute | solution.py:380
  524.8 94.8 %collective-permute-start.20 = (bf16[2,256,1536]{2,1,0:T(8,128)(2,1)}, bf16[2,256,1536]{2,1,0:T(8,128)(2,1)}, u32[]{:S(2)}, u32[]{:S(2)}) collective-permute-start(bf16[2,256,1536]{2,1,0:T(8,128)(2,1)} %constant_dynamic-slice_fusion), channel_id=1, source_target_pairs={{0,8},{1,9},{2,10},{3,11},{4,12},{5,13},{6,14},{7,15}} | collective-permute-start | bytes 4718600 | tf_op jit(solution)/shard_map/ppermute | solution.py:380
  526.2 24.1 %slice-start.4 = ((s8[8388608]{0:T(1024)(128)(4,1)}), s8[4194304]{0:T(1024)(128)(4,1)S(1)}, s32[]{:S(2)}) async-start(s8[8388608]{0:T(1024)(128)(4,1)} %bitcast.159), calls=%async_computation.4 | async-start | bytes 8388608
  556.8 202.5 %copy-start.12 = (bf16[2048,512]{1,0:T(8,128)(2,1)}, bf16[2048,512]{1,0:T(8,128)(2,1)S(1)}, u32[]{:S(2)}) copy-start(bf16[2048,512]{1,0:T(8,128)(2,1)S(1)} %convolution_convert_fusion.2) | copy-start | bytes 6291460
  557.7 87.9 %collective-permute-start.6 = (bf16[2,256,512]{2,1,0:T(8,128)(2,1)}, bf16[2,256,512]{2,1,0:T(8,128)(2,1)}, u32[]{:S(2)}, u32[]{:S(2)}) collective-permute-start(bf16[2,256,512]{2,1,0:T(8,128)(2,1)} %constant_dynamic-slice_fusion.2), channel_id=1, source_target_pairs={{0,8},{1,9},{2,10},{3,11},{4,12},{5,13},{6,14},{7,15}} | collective-permute-start | bytes 1572872 | tf_op jit(solution)/shard_map/ppermute | solution.py:380
  562.0 92.4 %collective-permute-start.30 = (bf16[2,768,256]{2,1,0:T(8,128)(2,1)}, bf16[2,768,256]{2,1,0:T(8,128)(2,1)}, u32[]{:S(2)}, u32[]{:S(2)}) collective-permute-start(bf16[2,768,256]{2,1,0:T(8,128)(2,1)} %pad_maximum_fusion.14), channel_id=1, source_target_pairs={{24,16},{25,17},{26,18},{27,19},{28,20},{29,21},{30,22},{31,23}} | collective-permute-start | bytes 2359304 | tf_op jit(solution)/shard_map/ppermute | solution.py:381
  612.8 45.6 %collective-permute-start.27 = (bf16[2,768,256]{2,1,0:T(8,128)(2,1)S(1)}, bf16[2,768,256]{2,1,0:T(8,128)(2,1)S(1)}, u32[]{:S(2)}, u32[]{:S(2)}) collective-permute-start(bf16[2,768,256]{2,1,0:T(8,128)(2,1)S(1)} %pad_maximum_fusion.16), channel_id=1, source_target_pairs={{0,8},{1,9},{2,10},{3,11},{4,12},{5,13},{6,14},{7,15}} | collective-permute-start | bytes 2359304 | tf_op jit(solution)/shard_map/ppermute | solution.py:380
  615.8 27.8 %collective-permute-start.14 = (bf16[2,256,256]{2,1,0:T(8,128)(2,1)S(1)}, bf16[2,256,256]{2,1,0:T(8,128)(2,1)S(1)}, u32[]{:S(2)}, u32[]{:S(2)}) collective-permute-start(bf16[2,256,256]{2,1,0:T(8,128)(2,1)S(1)} %get-tuple-element.98), channel_id=1, source_target_pairs={{0,8},{8,16},{1,9},{9,17},{2,10},{10,18},{3,11},{11,19},{4,12},{12... | collective-permute-start | bytes 786440 | tf_op jit(solution)/shard_map/ppermute | solution.py:380
  621.8 23.0 %copy-start.31 = (bf16[1,256,256]{2,1,0:T(8,128)(2,1)S(1)}, bf16[1,256,256]{2,1,0:T(8,128)(2,1)}, u32[]{:S(2)}) copy-start(bf16[1,256,256]{2,1,0:T(8,128)(2,1)} %copy-done.30) | copy-start | bytes 393220
  621.8 74.9 %collective-permute-start.21 = (bf16[2,256,1536]{2,1,0:T(8,128)(2,1)S(1)}, bf16[2,256,1536]{2,1,0:T(8,128)(2,1)S(1)}, u32[]{:S(2)}, u32[]{:S(2)}) collective-permute-start(bf16[2,256,1536]{2,1,0:T(8,128)(2,1)S(1)} %fusion.8), channel_id=1, source_target_pairs={{0,8},{8,16},{1,9},{9,17},{2,10},{10,18},{3,11},{11,19},{4,12},{12... | collective-permute-start | bytes 4718600 | tf_op jit(solution)/shard_map/ppermute | solution.py:380
  624.4 34.0 %copy-start.29 = (bf16[1,768,256]{2,1,0:T(8,128)(2,1)S(1)}, bf16[1,768,256]{2,1,0:T(8,128)(2,1)}, u32[]{:S(2)}) copy-start(bf16[1,768,256]{2,1,0:T(8,128)(2,1)} %get-tuple-element.56) | copy-start | bytes 1179652
  643.5 8.3 collective-permute-start.17
  645.6 109.0 %collective-permute-start.15 = (bf16[2,256,256]{2,1,0:T(8,128)(2,1)}, bf16[2,256,256]{2,1,0:T(8,128)(2,1)}, u32[]{:S(2)}, u32[]{:S(2)}) collective-permute-start(bf16[2,256,256]{2,1,0:T(8,128)(2,1)} %add_convert_fusion.7), channel_id=1, source_target_pairs={{0,8},{8,16},{16,24},{1,9},{9,17},{17,25},{2,10},{10,18},{18,26},{... | collective-permute-start | bytes 786440 | tf_op jit(solution)/shard_map/ppermute | solution.py:380
  651.8 42.3 %collective-permute-start.7 = (bf16[2,256,512]{2,1,0:T(8,128)(2,1)S(1)}, bf16[2,256,512]{2,1,0:T(8,128)(2,1)S(1)}, u32[]{:S(2)}, u32[]{:S(2)}) collective-permute-start(bf16[2,256,512]{2,1,0:T(8,128)(2,1)S(1)} %fusion.12), channel_id=1, source_target_pairs={{0,8},{8,16},{1,9},{9,17},{2,10},{10,18},{3,11},{11,19},{4,12},{12... | collective-permute-start | bytes 1572872 | tf_op jit(solution)/shard_map/ppermute | solution.py:380
  654.5 101.5 %collective-permute-start.18 = (bf16[2,256,256]{2,1,0:T(8,128)(2,1)}, bf16[2,256,256]{2,1,0:T(8,128)(2,1)}, u32[]{:S(2)}, u32[]{:S(2)}) collective-permute-start(bf16[2,256,256]{2,1,0:T(8,128)(2,1)} %add_convert_fusion.6), channel_id=1, source_target_pairs={{8,0},{16,8},{24,16},{9,1},{17,9},{25,17},{10,2},{18,10},{26,18},{... | collective-permute-start | bytes 786440 | tf_op jit(solution)/shard_map/ppermute | solution.py:381
  661.1 101.5 %collective-permute-start.28 = (bf16[2,768,256]{2,1,0:T(8,128)(2,1)}, bf16[2,768,256]{2,1,0:T(8,128)(2,1)}, u32[]{:S(2)}, u32[]{:S(2)}) collective-permute-start(bf16[2,768,256]{2,1,0:T(8,128)(2,1)} %get-tuple-element.90), channel_id=1, source_target_pairs={{0,8},{8,16},{1,9},{9,17},{2,10},{10,18},{3,11},{11,19},{4,12},{12... | collective-permute-start | bytes 2359304 | tf_op jit(solution)/shard_map/ppermute | solution.py:380
  695.2 64.1 %collective-permute-start.9 = (bf16[2,256,512]{2,1,0:T(8,128)(2,1)}, bf16[2,256,512]{2,1,0:T(8,128)(2,1)}, u32[]{:S(2)}, u32[]{:S(2)}) collective-permute-start(bf16[2,256,512]{2,1,0:T(8,128)(2,1)} %get-tuple-element.48), channel_id=1, source_target_pairs={{24,16},{25,17},{26,18},{27,19},{28,20},{29,21},{30,22},{31,23}} | collective-permute-start | bytes 1572872 | tf_op jit(solution)/shard_map/ppermute | solution.py:381
  700.3 80.1 %collective-permute-start.23 = (bf16[2,256,1536]{2,1,0:T(8,128)(2,1)}, bf16[2,256,1536]{2,1,0:T(8,128)(2,1)}, u32[]{:S(2)}, u32[]{:S(2)}) collective-permute-start(bf16[2,256,1536]{2,1,0:T(8,128)(2,1)} %get-tuple-element.46), channel_id=1, source_target_pairs={{24,16},{25,17},{26,18},{27,19},{28,20},{29,21},{30,22},{31,23}} | collective-permute-start | bytes 4718600 | tf_op jit(solution)/shard_map/ppermute | solution.py:381
  702.1 53.9 %copy-start.35 = (bf16[1,256,256]{2,1,0:T(8,128)(2,1)S(1)}, bf16[1,256,256]{2,1,0:T(8,128)(2,1)}, u32[]{:S(2)}) copy-start(bf16[1,256,256]{2,1,0:T(8,128)(2,1)} %get-tuple-element.72) | copy-start | bytes 393220
  702.1 53.9 %copy-start.36 = (bf16[1,256,256]{2,1,0:T(8,128)(2,1)S(1)}, bf16[1,256,256]{2,1,0:T(8,128)(2,1)}, u32[]{:S(2)}) copy-start(bf16[1,256,256]{2,1,0:T(8,128)(2,1)} %get-tuple-element.79) | copy-start | bytes 393220
  754.6 22.7 %collective-permute-start.31 = (bf16[2,768,256]{2,1,0:T(8,128)(2,1)}, bf16[2,768,256]{2,1,0:T(8,128)(2,1)S(1)}, u32[]{:S(2)}, u32[]{:S(2)}) collective-permute-start(bf16[2,768,256]{2,1,0:T(8,128)(2,1)} %get-tuple-element.91), channel_id=1, source_target_pairs={{16,8},{24,16},{17,9},{25,17},{18,10},{26,18},{19,11},{27,19},{20,... | collective-permute-start | bytes 2359304 | tf_op jit(solution)/shard_map/ppermute | solution.py:381
  758.6 98.3 %collective-permute-start.19 = (bf16[256,256]{1,0:T(8,128)(2,1)}, bf16[256,256]{1,0:T(8,128)(2,1)S(1)}, u32[]{:S(2)}, u32[]{:S(2)}) collective-permute-start(bf16[256,256]{1,0:T(8,128)(2,1)} %fusion.20), channel_id=1, source_target_pairs={{0,1},{1,0},{2,3},{3,2},{4,5},{5,4},{6,7},{7,6},{8,9},{9,8},{10,11... | collective-permute-start | bytes 393224 | tf_op jit(solution)/shard_map/ppermute | solution.py:327
  761.3 100.1 %collective-permute-start.10 = (bf16[2,256,512]{2,1,0:T(8,128)(2,1)}, bf16[2,256,512]{2,1,0:T(8,128)(2,1)}, u32[]{:S(2)}, u32[]{:S(2)}) collective-permute-start(bf16[2,256,512]{2,1,0:T(8,128)(2,1)} %fusion.13), channel_id=1, source_target_pairs={{16,8},{24,16},{17,9},{25,17},{18,10},{26,18},{19,11},{27,19},{20,... | collective-permute-start | bytes 1572872 | tf_op jit(solution)/shard_map/ppermute | solution.py:381
  764.8 92.1 %copy-start.25 = (f32[2,256,256]{2,1,0:T(8,128)S(1)}, f32[2,256,256]{2,1,0:T(8,128)}, u32[]{:S(2)}) copy-start(f32[2,256,256]{2,1,0:T(8,128)} %copy-done.24) | copy-start | bytes 1572868
  764.8 100.4 %collective-permute-start.29 = (bf16[2,768,256]{2,1,0:T(8,128)(2,1)}, bf16[2,768,256]{2,1,0:T(8,128)(2,1)}, u32[]{:S(2)}, u32[]{:S(2)}) collective-permute-start(bf16[2,768,256]{2,1,0:T(8,128)(2,1)} %add_convert_fusion.3), channel_id=1, source_target_pairs={{0,8},{8,16},{16,24},{1,9},{9,17},{17,25},{2,10},{10,18},{18,26},{... | collective-permute-start | bytes 2359304 | tf_op jit(solution)/shard_map/ppermute | solution.py:380
  778.3 86.9 %copy-start.27 = (bf16[1,768,256]{2,1,0:T(8,128)(2,1)S(1)}, bf16[1,768,256]{2,1,0:T(8,128)(2,1)}, u32[]{:S(2)}) copy-start(bf16[1,768,256]{2,1,0:T(8,128)(2,1)} %get-tuple-element.52) | copy-start | bytes 1179652
  778.3 86.9 %copy-start.28 = (bf16[1,768,256]{2,1,0:T(8,128)(2,1)S(1)}, bf16[1,768,256]{2,1,0:T(8,128)(2,1)}, u32[]{:S(2)}) copy-start(bf16[1,768,256]{2,1,0:T(8,128)(2,1)} %get-tuple-element.59) | copy-start | bytes 1179652
  778.3 86.9 %collective-permute-start.32 = (bf16[2,768,256]{2,1,0:T(8,128)(2,1)}, bf16[2,768,256]{2,1,0:T(8,128)(2,1)}, u32[]{:S(2)}, u32[]{:S(2)}) collective-permute-start(bf16[2,768,256]{2,1,0:T(8,128)(2,1)} %add_convert_fusion.2), channel_id=1, source_target_pairs={{8,0},{16,8},{24,16},{9,1},{17,9},{25,17},{10,2},{18,10},{26,18},{... | collective-permute-start | bytes 2359304 | tf_op jit(solution)/shard_map/ppermute | solution.py:381
  780.4 102.4 %slice-start.2 = ((s8[6291456]{0:T(1024)(128)(4,1)}), s8[2097152]{0:T(1024)(128)(4,1)S(1)}, s32[]{:S(2)}) async-start(s8[6291456]{0:T(1024)(128)(4,1)} %bitcast.153), calls=%async_computation.2 | async-start | bytes 4194304
  784.0 98.8 %collective-permute-start.24 = (bf16[2,256,1536]{2,1,0:T(8,128)(2,1)}, bf16[2,256,1536]{2,1,0:T(8,128)(2,1)}, u32[]{:S(2)}, u32[]{:S(2)}) collective-permute-start(bf16[2,256,1536]{2,1,0:T(8,128)(2,1)} %fusion.9), channel_id=1, source_target_pairs={{16,8},{24,16},{17,9},{25,17},{18,10},{26,18},{19,11},{27,19},{20,... | collective-permute-start | bytes 4718600 | tf_op jit(solution)/shard_map/ppermute | solution.py:381
  857.7 25.1 %slice-start.3 = ((s8[6291456]{0:T(1024)(128)(4,1)}), s8[4194304]{0:T(1024)(128)(4,1)S(1)}, s32[]{:S(2)}) async-start(s8[6291456]{0:T(1024)(128)(4,1)} %bitcast.153), calls=%async_computation.3 | async-start | bytes 8388608
  857.7 15.7 %collective-permute-start.8 = (bf16[2,256,512]{2,1,0:T(8,128)(2,1)}, bf16[2,256,512]{2,1,0:T(8,128)(2,1)S(1)}, u32[]{:S(2)}, u32[]{:S(2)}) collective-permute-start(bf16[2,256,512]{2,1,0:T(8,128)(2,1)} %get-tuple-element.47), channel_id=1, source_target_pairs={{0,8},{8,16},{16,24},{1,9},{9,17},{17,25},{2,10},{10,18},{18,26},{... | collective-permute-start | bytes 1572872 | tf_op jit(solution)/shard_map/ppermute | solution.py:380
  862.7 15.2 %collective-permute-start.11 = (bf16[2,256,512]{2,1,0:T(8,128)(2,1)S(1)}, bf16[2,256,512]{2,1,0:T(8,128)(2,1)S(1)}, u32[]{:S(2)}, u32[]{:S(2)}) collective-permute-start(bf16[2,256,512]{2,1,0:T(8,128)(2,1)S(1)} %add_convert_fusion.4), channel_id=1, source_target_pairs={{8,0},{16,8},{24,16},{9,1},{17,9},{25,17},{10,2},{18,10},{26,18},{... | collective-permute-start | bytes 1572872 | tf_op jit(solution)/shard_map/ppermute | solution.py:381
  867.1 20.0 %collective-permute-start.33 = (bf16[768,256]{1,0:T(8,128)(2,1)S(1)}, bf16[768,256]{1,0:T(8,128)(2,1)S(1)}, u32[]{:S(2)}, u32[]{:S(2)}) collective-permute-start(bf16[768,256]{1,0:T(8,128)(2,1)S(1)} %fusion.17), channel_id=1, source_target_pairs={{0,1},{1,0},{2,3},{3,2},{4,5},{5,4},{6,7},{7,6},{8,9},{9,8},{10,11... | collective-permute-start | bytes 1179656 | tf_op jit(solution)/shard_map/ppermute | solution.py:327
  879.1 36.6 %collective-permute-start.22 = (bf16[2,256,1536]{2,1,0:T(8,128)(2,1)S(1)}, bf16[2,256,1536]{2,1,0:T(8,128)(2,1)S(1)}, u32[]{:S(2)}, u32[]{:S(2)}) collective-permute-start(bf16[2,256,1536]{2,1,0:T(8,128)(2,1)S(1)} %copy-done.26), channel_id=1, source_target_pairs={{0,8},{8,16},{16,24},{1,9},{9,17},{17,25},{2,10},{10,18},{18,26},{... | collective-permute-start | bytes 4718600 | tf_op jit(solution)/shard_map/ppermute | solution.py:380
  884.6 36.1 %collective-permute-start.25 = (bf16[2,256,1536]{2,1,0:T(8,128)(2,1)S(1)}, bf16[2,256,1536]{2,1,0:T(8,128)(2,1)S(1)}, u32[]{:S(2)}, u32[]{:S(2)}) collective-permute-start(bf16[2,256,1536]{2,1,0:T(8,128)(2,1)S(1)} %add_convert_fusion), channel_id=1, source_target_pairs={{8,0},{16,8},{24,16},{9,1},{17,9},{25,17},{10,2},{18,10},{26,18},{... | collective-permute-start | bytes 4718600 | tf_op jit(solution)/shard_map/ppermute | solution.py:381
  887.0 6.4 collective-permute-start.12
  921.4 16.5 %collective-permute-start.26 = (bf16[256,1536]{1,0:T(8,128)(2,1)S(1)}, bf16[256,1536]{1,0:T(8,128)(2,1)S(1)}, u32[]{:S(2)}, u32[]{:S(2)}) collective-permute-start(bf16[256,1536]{1,0:T(8,128)(2,1)S(1)} %fusion.14), channel_id=1, source_target_pairs={{0,1},{1,0},{2,3},{3,2},{4,5},{5,4},{6,7},{7,6},{8,9},{9,8},{10,11... | collective-permute-start | bytes 2359304 | tf_op jit(solution)/shard_map/ppermute | solution.py:327
  (37 other events, 337.1 us)

commit v2 on v0

--- a/solution.py
+++ b/solution.py
@@ -1,6 +1,8 @@
 import jax
 import jax.numpy as jnp
 from jax import lax
+from jax.experimental import pallas as pl
+from jax.experimental.pallas import tpu as pltpu
 from jax.sharding import PartitionSpec as P
 
 EPS = 1e-06
@@ -8,6 +10,7 @@
 NEG = -1e30
 F32 = jnp.float32
 B16 = jnp.bfloat16
+MESH = pl.DeviceIdType.MESH
 
 
 def width_sum(value):
@@ -173,7 +176,7 @@
     return lax.map(one_sequence, (query, keys, values, seg, logs, grad_out))
 
 
-def per_device(
+def general_device(
     tokens,
     seg_ids,
     w_query,
@@ -313,6 +316,1492 @@
     )
 
 
+def fits(mesh):
+    return mesh.shape["tx"] == 4 and mesh.shape["ty"] == 2 and mesh.shape["dp"] == 4
+
+
+def swap_x(value):
+    return lax.ppermute(value, "ty", [(0, 1), (1, 0)])
+
+
+def in_order(mine, theirs, axis):
+    first = lax.axis_index("ty") == 0
+    return jnp.concatenate(
+        [jnp.where(first, mine, theirs), jnp.where(first, theirs, mine)], axis=axis
+    )
+
+
+def spin(value, cosine, sine):
+    return value * cosine + pltpu.roll(value, value.shape[1] // 2, 1) * sine
+
+
+def spin_back(value, cosine, sine):
+    return value * cosine + pltpu.roll(value * sine, value.shape[1] // 2, 1)
+
+
+def head_scale(value):
+    return lax.rsqrt(jnp.mean(value * value, axis=1, keepdims=True) + EPS)
+
+
+def window(first, block, most):
+    return max(0, first - most), first + block
+
+
+def kept(first, block, low, high, starts):
+    shape = (block, high - low)
+    column = low + lax.broadcasted_iota(jnp.int32, shape, 1)
+    row = first + lax.broadcasted_iota(jnp.int32, shape, 0)
+    return (column >= starts) & (column <= row)
+
+
+def rows_dot(left, right):
+    return lax.dot_general(left, right, (((1,), (1,)), ((), ())), preferred_element_type=F32)
+
+
+def stand(row):
+    return jnp.transpose(jnp.broadcast_to(row, (row.shape[1], row.shape[1])))
+
+
+def lie(column):
+    return jnp.transpose(jnp.broadcast_to(column, (column.shape[0], column.shape[0])))[0:1]
+
+
+def put_stats(stats_ref, tile, column):
+    stats_ref[tile, 0:1, :] = lie(column[:128])
+    stats_ref[tile, 1:2, :] = lie(column[128:])
+
+
+BLOCK = 256
+
+
+def attend_sequence(core, seq, most, projected, fixed_refs, mixed, saved_refs):
+    starts_ref, cosine_ref, sine_ref, query_gain_ref, key_gain_ref = fixed_refs
+    query_ref, key_ref, value_ref, log_ref = saved_refs
+    rows = projected.shape[1]
+    length = query_ref.shape[1]
+    depth = key_ref.shape[2]
+    heads = query_ref.shape[2] // depth
+    scale = depth ** (-0.5)
+    for half in range(2):
+        place = 2 * lax.rem(core + half, 2) + seq
+        for at in range(half * rows, (half + 1) * rows, BLOCK):
+            inner = at - half * rows
+            cosine = cosine_ref[seq, at : at + BLOCK, :]
+            sine = sine_ref[seq, at : at + BLOCK, :]
+            for head in range(heads + 2):
+                lane = slice(head * depth, (head + 1) * depth)
+                value = projected[place, inner : inner + BLOCK, lane]
+                if head < heads:
+                    normed = value * head_scale(value) * query_gain_ref[...]
+                    query_ref[seq, at : at + BLOCK, lane] = spin(normed, cosine, sine).astype(B16)
+                elif head == heads:
+                    normed = value * head_scale(value) * key_gain_ref[...]
+                    key_ref[seq, at : at + BLOCK, :] = spin(normed, cosine, sine).astype(B16)
+                else:
+                    value_ref[seq, at : at + BLOCK, :] = value.astype(B16)
+    for first in range(0, length, BLOCK):
+        low, high = window(first, BLOCK, most)
+        mask = kept(first, BLOCK, low, high, starts_ref[seq, first : first + BLOCK, :])
+        half, inner = divmod(first, rows)
+        place = 2 * lax.rem(core + half, 2) + seq
+        for head in range(heads):
+            lane = slice(head * depth, (head + 1) * depth)
+            query = query_ref[seq, first : first + BLOCK, lane]
+            scores = rows_dot(query, key_ref[seq, low:high, :]) * scale
+            scores = jnp.where(mask, scores, NEG)
+            top = jnp.max(scores, axis=1, keepdims=True)
+            weights = jnp.exp(scores - top)
+            total = jnp.sum(weights, axis=1, keepdims=True)
+            probs = (weights * (1.0 / total)).astype(B16)
+            out = jnp.dot(probs, value_ref[seq, low:high, :], preferred_element_type=F32)
+            mixed[place, inner : inner + BLOCK, lane] = out.astype(B16)
+            log_ref[seq, head, first : first + BLOCK, :] = top + jnp.log(total)
+
+
+def attend_sequence_back(
+    core, seq, most, projected, upstream, fixed_refs, saved_refs, result, stats, gains, accs
+):
+    starts_ref, cosine_ref, sine_ref, query_gain_ref, key_gain_ref = fixed_refs
+    query_ref, key_ref, value_ref, log_ref = saved_refs
+    query_acc, key_acc, value_acc = accs
+    rows = projected.shape[1]
+    length = query_ref.shape[1]
+    depth = key_ref.shape[2]
+    heads = query_ref.shape[2] // depth
+    scale = depth ** (-0.5)
+    key_acc[...] = jnp.zeros_like(key_acc)
+    value_acc[...] = jnp.zeros_like(value_acc)
+    for first in range(0, length, BLOCK):
+        low, high = window(first, BLOCK, most)
+        mask = kept(first, BLOCK, low, high, starts_ref[seq, first : first + BLOCK, :])
+        half, inner = divmod(first, rows)
+        place = 2 * lax.rem(core + half, 2) + seq
+        keys = key_ref[seq, low:high, :]
+        values = value_ref[seq, low:high, :]
+        for head in range(heads):
+            lane = slice(head * depth, (head + 1) * depth)
+            query = query_ref[seq, first : first + BLOCK, lane]
+            grad = upstream[place, inner : inner + BLOCK, lane]
+            scores = rows_dot(query, keys) * scale - log_ref[seq, head, first : first + BLOCK, :]
+            probs = jnp.exp(jnp.where(mask, scores, NEG))
+            prob_grad = rows_dot(grad, values)
+            delta = jnp.sum(probs * prob_grad, axis=1, keepdims=True)
+            score_grad = (probs * (prob_grad - delta)).astype(B16)
+            query_acc[first : first + BLOCK, lane] = (
+                jnp.dot(score_grad, keys, preferred_element_type=F32) * scale
+            )
+            key_acc[low:high, :] += weight_grad(score_grad, query) * scale
+            value_acc[low:high, :] += weight_grad(probs.astype(B16), grad)
+    query_total = jnp.zeros((1, depth), F32)
+    key_total = jnp.zeros((1, depth), F32)
+    for half in range(2):
+        block = 2 * lax.rem(core + half, 2) + seq
+        for at in range(half * rows, (half + 1) * rows, BLOCK):
+            inner = at - half * rows
+            cosine = cosine_ref[seq, at : at + BLOCK, :]
+            sine = sine_ref[seq, at : at + BLOCK, :]
+            total = jnp.zeros((BLOCK, 1), F32)
+            for head in range(heads + 2):
+                lane = slice(head * depth, (head + 1) * depth)
+                value = projected[block, inner : inner + BLOCK, lane]
+                if head == heads + 1:
+                    back = value_acc[at : at + BLOCK, :].astype(B16)
+                else:
+                    if head < heads:
+                        grad = query_acc[at : at + BLOCK, lane]
+                        gain = query_gain_ref[...]
+                    else:
+                        grad = key_acc[at : at + BLOCK, :]
+                        gain = key_gain_ref[...]
+                    grad = spin_back(grad, cosine, sine)
+                    rate = head_scale(value)
+                    scaled = value * rate
+                    share = jnp.sum(grad * scaled, axis=0, keepdims=True)
+                    if head < heads:
+                        query_total += share
+                    else:
+                        key_total += share
+                    middle = jnp.mean(gain * grad * scaled, axis=1, keepdims=True)
+                    back = (rate * (gain * grad - scaled * middle)).astype(B16)
+                result[block, inner : inner + BLOCK, lane] = back
+                total += jnp.sum(back.astype(F32) * value, axis=1, keepdims=True)
+            put_stats(stats, 2 * block + inner // BLOCK, total)
+    gains[seq, 0:1, :] = query_total
+    gains[seq, 1:2, :] = key_total
+
+
+def neighbours():
+    spot = lax.axis_index("tx")
+    core = lax.rem(spot, 2)
+    return (
+        {"ty": 1 - lax.axis_index("ty")},
+        {"tx": lax.rem(spot + 2, 4)},
+        {"tx": spot + 1 - 2 * core},
+    )
+
+
+def planes():
+    plane = lax.axis_index("dp")
+    return {"dp": plane + 1 - 2 * lax.rem(plane, 2)}, {"dp": lax.rem(plane + 2, 4)}
+
+
+def greet(targets):
+    barrier = pltpu.get_barrier_semaphore()
+    for target in targets:
+        pl.semaphore_signal(barrier, inc=1, device_id=target, device_id_type=MESH)
+    pl.semaphore_wait(barrier, len(targets))
+
+
+class Wires:
+    def __init__(self, send_sems, recv_sems):
+        self.send_sems = send_sems
+        self.recv_sems = recv_sems
+
+    def copy(self, kind, chunk, source, target, device):
+        return pltpu.make_async_remote_copy(
+            src_ref=source,
+            dst_ref=target,
+            send_sem=self.send_sems.at[kind, chunk],
+            recv_sem=self.recv_sems.at[kind, chunk],
+            device_id=device,
+            device_id_type=MESH,
+        )
+
+
+CHUNK = 256
+SIBLING, CORNER, FINAL_X, FINAL_Y = 0, 1, 2, 3
+REDUCE_KINDS = 4
+OUT_X, OUT_Y, OUT_CORNER, CORE_OWN, CORE_X, CORE_Y, CORE_CORNER = range(7)
+GATHER_KINDS = 7
+SHARE_X, SHARE_Z = 0, 1
+SHARE_KINDS = 2
+
+
+def lanes(chunk, half, width):
+    return pl.ds(pl.multiple_of(half * width + chunk * CHUNK, CHUNK), CHUNK)
+
+
+class Gather:
+    def __init__(self, wires, base, whole, own, local_sem):
+        self.wires, self.base, self.whole, self.own, self.local_sem = (
+            wires,
+            base,
+            whole,
+            own,
+            local_sem,
+        )
+        self.width = whole.shape[2] // 2
+        self.count = self.width // CHUNK
+
+    def place(self, block, chunk, half):
+        return self.whole.at[block, :, lanes(chunk, half, self.width)]
+
+    def copy(self, name, chunk):
+        side, across, core = neighbours()
+        at = self.place
+        own = self.own.at[chunk]
+        if name == "local":
+            return pltpu.make_async_copy(own, at(0, chunk, 0), self.local_sem.at[chunk])
+        kind, source, target, device = {
+            "x": (OUT_X, own, at(0, chunk, 1), side),
+            "y": (OUT_Y, own, at(1, chunk, 0), across),
+            "core": (CORE_OWN, own, at(2, chunk, 0), core),
+            "even": (OUT_CORNER, at(0, chunk, 1), at(1, chunk, 1), across),
+            "odd": (OUT_CORNER, at(1, chunk, 0), at(1, chunk, 1), side),
+            "core_x": (CORE_X, at(0, chunk, 1), at(2, chunk, 1), core),
+            "core_y": (CORE_Y, at(1, chunk, 0), at(3, chunk, 0), core),
+            "core_corner": (CORE_CORNER, at(1, chunk, 1), at(3, chunk, 1), core),
+        }[name]
+        return self.wires.copy(self.base + kind, chunk, source, target, device)
+
+    def send(self, chunk):
+        for name in ("x", "y", "core", "local"):
+            self.copy(name, chunk).start()
+
+    def relay(self):
+        @pl.loop(0, self.count)
+        def _(chunk):
+            even = lax.rem(chunk, 2) == 0
+            self.copy("x", chunk).wait_recv()
+
+            @pl.when(even)
+            def _():
+                self.copy("even", chunk).start()
+
+            self.copy("core_x", chunk).start()
+            self.copy("y", chunk).wait_recv()
+
+            @pl.when(jnp.logical_not(even))
+            def _():
+                self.copy("odd", chunk).start()
+
+            self.copy("core_y", chunk).start()
+
+    def close(self):
+        @pl.loop(0, self.count)
+        def _(chunk):
+            self.copy("even", chunk).wait_recv()
+            self.copy("core_corner", chunk).start()
+
+        @pl.loop(0, self.count)
+        def _(chunk):
+            for name in ("core", "core_x", "core_y", "core_corner"):
+                self.copy(name, chunk).wait_recv()
+            for name in ("x", "y", "core", "even", "core_x", "core_y", "core_corner"):
+                self.copy(name, chunk).wait_send()
+            self.copy("local", chunk).wait()
+
+
+class Share:
+    def __init__(self, wires, base, sources, whole, by_rows, local_sems):
+        self.wires, self.base, self.sources, self.whole, self.by_rows, self.local_sems = (
+            wires,
+            base,
+            sources,
+            whole,
+            by_rows,
+            local_sems,
+        )
+        self.size = (whole.shape[0] // 2 if by_rows else whole.shape[0]) // 4
+
+    def quarter(self, plane):
+        start = plane * self.size
+        if self.by_rows:
+            rows = pl.ds(pl.multiple_of(self.whole.shape[0] // 2 + start, self.size), self.size)
+            return self.whole.at[rows]
+        width = self.whole.shape[1] // 2
+        return self.whole.at[pl.ds(pl.multiple_of(start, self.size), self.size), width:]
+
+    def cross(self, index):
+        side, _, _ = neighbours()
+        plane = lax.axis_index("dp")
+        other = 1 - lax.axis_index("ty")
+        source = self.sources[index]
+        if self.by_rows:
+            rows = pl.ds(pl.multiple_of(plane * self.size, self.size), self.size)
+            columns = source.shape[1] // 2
+            part = source.at[rows, pl.ds(pl.multiple_of(other * columns, columns), columns)]
+            offset = sum(item.shape[1] // 2 for item in self.sources[:index])
+            target = self.quarter(plane).at[:, offset : offset + columns]
+        else:
+            start = pl.multiple_of(other * (source.shape[0] // 2) + plane * self.size, self.size)
+            part = source.at[pl.ds(start, self.size)]
+            target = self.quarter(plane)
+        return self.wires.copy(self.base + SHARE_X, index, part, target, side)
+
+    def local(self, index):
+        mine = lax.axis_index("ty")
+        source = self.sources[index]
+        if self.by_rows:
+            columns = source.shape[1] // 2
+            offset = sum(item.shape[1] // 2 for item in self.sources[:index])
+            part = source.at[:, pl.ds(pl.multiple_of(mine * columns, columns), columns)]
+            target = self.whole.at[: self.whole.shape[0] // 2, offset : offset + columns]
+        else:
+            half = source.shape[0] // 2
+            part = source.at[pl.ds(pl.multiple_of(mine * half, half), half)]
+            target = self.whole.at[:, : self.whole.shape[1] // 2]
+        return pltpu.make_async_copy(part, target, self.local_sems.at[index])
+
+    def over(self, index):
+        near, far = planes()
+        plane = lax.axis_index("dp")
+        owner = lax.rem(plane + 2, 4) if index == 2 else plane
+        place = self.quarter(owner)
+        return self.wires.copy(
+            self.base + SHARE_Z, index, place, place, far if index == 0 else near
+        )
+
+    def start(self):
+        for index in range(len(self.sources)):
+            self.cross(index).start()
+            self.local(index).start()
+
+    def middle(self):
+        for index in range(len(self.sources)):
+            self.cross(index).wait_recv()
+        self.over(0).start()
+        self.over(1).start()
+
+    def late(self):
+        self.over(0).wait_recv()
+        self.over(2).start()
+
+    def close(self):
+        self.over(1).wait_recv()
+        self.over(2).wait_recv()
+        for index in range(3):
+            self.over(index).wait_send()
+        for index in range(len(self.sources)):
+            self.cross(index).wait_send()
+            self.local(index).wait()
+
+
+FOLD_NEAR, FOLD_FAR, FOLD_X = 0, 1, 2
+FOLD_KINDS = 3
+
+
+class Fold:
+    def __init__(self, wires, base, tiles, bufs, mine, theirs):
+        self.wires, self.base, self.tiles, self.mine, self.theirs = (
+            wires,
+            base,
+            tiles,
+            mine,
+            theirs,
+        )
+        self.near_recv, self.far_recv = bufs
+        plane = lax.axis_index("dp")
+        self.low = lax.rem(plane, 2)
+        self.high = lax.div(plane, 2)
+
+    def index(self, half, high, low):
+        return half * 4 + 2 * high + low
+
+    def near(self, half, high):
+        source = self.tiles.at[self.index(half, high, 1 - self.low)]
+        slot = 2 * half + high
+        return self.wires.copy(
+            self.base + FOLD_NEAR, slot, source, self.near_recv.at[slot], planes()[0]
+        )
+
+    def far(self, half):
+        source = self.tiles.at[self.index(half, 1 - self.high, self.low)]
+        return self.wires.copy(
+            self.base + FOLD_FAR, half, source, self.far_recv.at[half], planes()[1]
+        )
+
+    def cross(self):
+        source = self.tiles.at[self.index(1, self.high, self.low)]
+        return self.wires.copy(self.base + FOLD_X, 0, source, self.theirs, neighbours()[0])
+
+    def start(self):
+        for half in range(2):
+            for high in range(2):
+                self.near(half, high).start()
+
+    def add(self, half, high):
+        self.near(half, high).wait_recv()
+        at = self.index(half, high, self.low)
+        came = self.near_recv[2 * half + high].astype(F32)
+        self.tiles[at] = (self.tiles[at].astype(F32) + came).astype(B16)
+
+    def middle(self):
+        @pl.loop(0, 2)
+        def _(turn):
+            half = 1 - turn
+            self.add(half, 1 - self.high)
+            self.far(half).start()
+
+        @pl.loop(0, 2)
+        def _(half):
+            self.add(half, self.high)
+
+    def late(self):
+        at = self.index(1, self.high, self.low)
+        self.far(1).wait_recv()
+        self.tiles[at] = (self.tiles[at].astype(F32) + self.far_recv[1].astype(F32)).astype(B16)
+        self.cross().start()
+        self.far(0).wait_recv()
+        at = self.index(0, self.high, self.low)
+        self.mine[...] = self.tiles[at].astype(F32) + self.far_recv[0].astype(F32)
+
+    def close(self):
+        self.cross().wait_recv()
+        for half in range(2):
+            for high in range(2):
+                self.near(half, high).wait_send()
+            self.far(half).wait_send()
+        self.cross().wait_send()
+
+
+def fold_scratch(rows, columns):
+    return [pltpu.VMEM((4, rows, columns), B16), pltpu.VMEM((2, rows, columns), B16)]
+
+
+def turn_tile(step):
+    low = lax.rem(lax.axis_index("dp"), 2)
+    kept_now = lax.div(step, 4)
+    low = kept_now * low + (1 - kept_now) * (1 - low)
+    return lax.div(lax.rem(step, 4), 2) * 4 + 2 * lax.rem(step, 2) + low
+
+
+class Reduce:
+    def __init__(self, wires, rows_ref, weight_ref, transposed, bufs):
+        self.wires, self.rows_ref, self.weight_ref, self.transposed = (
+            wires,
+            rows_ref,
+            weight_ref,
+            transposed,
+        )
+        (
+            self.sibling_send,
+            self.sibling_recv,
+            self.kept_ref,
+            self.out,
+            self.corner_recv,
+            self.x_recv,
+            self.y_recv,
+        ) = bufs
+        self.rows = rows_ref.shape[1]
+        self.width = (weight_ref.shape[0] if transposed else weight_ref.shape[1]) // 2
+        self.count = self.width // CHUNK
+
+    def product(self, block, chunk, half):
+        left = self.rows_ref[block : block + 2].reshape(2 * self.rows, self.rows_ref.shape[2])
+        at = lanes(chunk, half, self.width)
+        if self.transposed:
+            return rows_dot(left, self.weight_ref[at, :])
+        return jnp.dot(left, self.weight_ref[:, at], preferred_element_type=F32)
+
+    def sibling(self, chunk):
+        return self.wires.copy(
+            SIBLING,
+            chunk,
+            self.sibling_send.at[chunk],
+            self.sibling_recv.at[chunk],
+            neighbours()[2],
+        )
+
+    def corner(self, chunk, device):
+        return self.wires.copy(
+            CORNER, chunk, self.out.at[2, chunk], self.corner_recv.at[chunk], device
+        )
+
+    def final_x(self, chunk):
+        return self.wires.copy(
+            FINAL_X, chunk, self.out.at[0, chunk], self.x_recv.at[chunk], neighbours()[0]
+        )
+
+    def final_y(self, chunk):
+        return self.wires.copy(
+            FINAL_Y, chunk, self.out.at[1, chunk], self.y_recv.at[chunk], neighbours()[1]
+        )
+
+    def start(self):
+        @pl.loop(0, self.count)
+        def _(chunk):
+            @pl.loop(0, 2)
+            def _(half):
+                self.sibling_send[chunk, half] = self.product(2, chunk, half).astype(B16)
+
+            self.sibling(chunk).start()
+
+        rows = self.rows
+
+        @pl.loop(0, self.count)
+        def _(chunk):
+            even = lax.rem(chunk, 2) == 0
+            self.sibling(chunk).wait_recv()
+
+            @pl.loop(0, 2)
+            def _(half):
+                total = self.product(0, chunk, half) + self.sibling_recv[chunk, half].astype(F32)
+
+                @pl.when(half == 1)
+                def _():
+                    self.out[0, chunk] = total[:rows].astype(B16)
+                    self.out[2, chunk] = total[rows:].astype(B16)
+
+                @pl.when(half == 0)
+                def _():
+                    self.kept_ref[chunk] = total[:rows]
+                    self.out[1, chunk] = total[rows:].astype(B16)
+
+            side, across, _ = neighbours()
+
+            @pl.when(even)
+            def _():
+                self.corner(chunk, side).start()
+                self.final_x(chunk).start()
+
+            @pl.when(jnp.logical_not(even))
+            def _():
+                self.corner(chunk, across).start()
+                self.final_y(chunk).start()
+
+    def middle(self):
+        @pl.loop(0, self.count)
+        def _(chunk):
+            even = lax.rem(chunk, 2) == 0
+            self.corner(chunk, neighbours()[0]).wait_recv()
+            came = self.corner_recv[chunk].astype(F32)
+
+            @pl.when(even)
+            def _():
+                self.out[1, chunk] = (self.out[1, chunk].astype(F32) + came).astype(B16)
+                self.final_y(chunk).start()
+
+            @pl.when(jnp.logical_not(even))
+            def _():
+                self.out[0, chunk] = (self.out[0, chunk].astype(F32) + came).astype(B16)
+                self.final_x(chunk).start()
+
+    def total(self, chunk):
+        self.final_x(chunk).wait_recv()
+        self.final_y(chunk).wait_recv()
+        return (
+            self.kept_ref[chunk] + self.x_recv[chunk].astype(F32) + self.y_recv[chunk].astype(F32)
+        )
+
+    def close(self):
+        @pl.loop(0, self.count)
+        def _(chunk):
+            self.sibling(chunk).wait_send()
+            self.corner(chunk, neighbours()[0]).wait_send()
+            self.final_x(chunk).wait_send()
+            self.final_y(chunk).wait_send()
+
+
+def reduce_scratch(rows, width):
+    count = width // CHUNK
+    return [
+        pltpu.VMEM((count, 2, 2 * rows, CHUNK), B16),
+        pltpu.VMEM((count, 2, 2 * rows, CHUNK), B16),
+        pltpu.VMEM((count, rows, CHUNK), F32),
+        pltpu.VMEM((3, count, rows, CHUNK), B16),
+        pltpu.VMEM((count, rows, CHUNK), B16),
+        pltpu.VMEM((count, rows, CHUNK), B16),
+        pltpu.VMEM((count, rows, CHUNK), B16),
+    ]
+
+
+def gather_scratch(rows, width):
+    count = width // CHUNK
+    return [pltpu.VMEM((count, rows, CHUNK), B16), pltpu.SemaphoreType.DMA((count,))]
+
+
+def wire_scratch(kinds, count):
+    return [pltpu.SemaphoreType.DMA((kinds, count))] * 2
+
+
+IN_VMEM = pl.BlockSpec(memory_space=pltpu.VMEM)
+IN_ANY = pl.BlockSpec(memory_space=pl.ANY)
+VMEM_MOST = 60 * 1024 * 1024
+
+
+def remote_params(number):
+    return pltpu.CompilerParams(
+        collective_id=number, has_side_effects=True, vmem_limit_bytes=VMEM_MOST
+    )
+
+
+def cost(flops, size):
+    return pl.CostEstimate(flops=flops, bytes_accessed=size, transcendentals=0)
+
+
+def shape(dims, kind=B16):
+    return jax.ShapeDtypeStruct(dims, kind)
+
+
+def cut(own, block_ref):
+    for chunk in range(own.shape[0]):
+        own[chunk] = block_ref[:, chunk * CHUNK : (chunk + 1) * CHUNK]
+
+
+def open_kernel(
+    tokens_ref, query_ref, key_ref, value_ref, out_ref, whole_ref, project_ref, branch_ref, *scratch
+):
+    own, gather_sem, send_sems, recv_sems, project_sem, branch_sem = scratch
+    cut(own, tokens_ref)
+    greet(neighbours() + planes())
+    wires = Wires(send_sems, recv_sems)
+    gather = Gather(wires, 0, whole_ref, own, gather_sem)
+    shares = [
+        Share(wires, GATHER_KINDS, (query_ref, key_ref, value_ref), project_ref, True, project_sem),
+        Share(wires, GATHER_KINDS + SHARE_KINDS, (out_ref,), branch_ref, False, branch_sem),
+    ]
+    shares[0].start()
+
+    @pl.loop(0, gather.count)
+    def _(chunk):
+        gather.send(chunk)
+
+    shares[1].start()
+    shares[0].middle()
+    gather.relay()
+    shares[1].middle()
+    shares[0].late()
+    shares[1].late()
+    gather.close()
+    shares[0].close()
+    shares[1].close()
+
+
+def open_call(tokens, w_query, w_key, w_value, w_out, number):
+    rows, width = tokens.shape
+    columns = (w_query.shape[1] + w_key.shape[1] + w_value.shape[1]) // 2
+    return pl.pallas_call(
+        open_kernel,
+        out_shape=(
+            shape((4, rows, 2 * width)),
+            shape((2 * width, columns)),
+            shape((w_out.shape[0] // 2, 2 * width)),
+        ),
+        in_specs=[IN_VMEM] + [IN_ANY] * 4,
+        out_specs=(IN_ANY,) * 3,
+        scratch_shapes=gather_scratch(rows, width)
+        + wire_scratch(GATHER_KINDS + 2 * SHARE_KINDS, width // CHUNK)
+        + [pltpu.SemaphoreType.DMA((3,)), pltpu.SemaphoreType.DMA((1,))],
+        compiler_params=remote_params(number),
+        cost_estimate=cost(0, 32 * rows * width),
+    )(tokens, w_query, w_key, w_value, w_out)
+
+
+def front_kernel(
+    most,
+    whole_ref,
+    project_ref,
+    gain_ref,
+    starts_ref,
+    cosine_ref,
+    sine_ref,
+    query_gain_ref,
+    key_gain_ref,
+    grad_ref,
+    down_ref,
+    first_ref,
+    scale_ref,
+    projected_ref,
+    mixed_ref,
+    query_ref,
+    key_ref,
+    value_ref,
+    log_ref,
+    grad_whole_ref,
+    back_ref,
+    *scratch,
+):
+    own, gather_sem, send_sems, recv_sems, back_sem = scratch
+    core = lax.rem(lax.axis_index("tx"), 2)
+    cut(own, grad_ref)
+    greet(neighbours() + planes())
+    wires = Wires(send_sems, recv_sems)
+    gather = Gather(wires, 0, grad_whole_ref, own, gather_sem)
+    back = Share(wires, GATHER_KINDS, (down_ref,), back_ref, False, back_sem)
+
+    @pl.loop(0, gather.count)
+    def _(chunk):
+        gather.send(chunk)
+
+    back.start()
+    rows = whole_ref.shape[1]
+
+    @pl.loop(0, 4 * rows // BLOCK)
+    def _(tile):
+        block = lax.div(tile, rows // BLOCK)
+        at = pl.ds(pl.multiple_of(lax.rem(tile, rows // BLOCK) * BLOCK, BLOCK), BLOCK)
+        value = whole_ref[block, at, :].astype(F32)
+        scale = lax.rsqrt(jnp.mean(value * value, axis=1, keepdims=True) + EPS)
+        first = (value * scale * gain_ref[...]).astype(B16)
+        first_ref[block, at, :] = first
+        projected_ref[block, at, :] = jnp.dot(
+            first, project_ref[...], preferred_element_type=F32
+        )
+
+        @pl.when(block == 0)
+        def _():
+            scale_ref[at, :] = jnp.broadcast_to(scale, (BLOCK, 128))
+
+    gather.relay()
+    back.middle()
+    fixed_refs = (starts_ref, cosine_ref, sine_ref, query_gain_ref, key_gain_ref)
+    saved_refs = (query_ref, key_ref, value_ref, log_ref)
+
+    @pl.loop(0, 2)
+    def _(seq):
+        attend_sequence(core, seq, most, projected_ref, fixed_refs, mixed_ref, saved_refs)
+
+        @pl.when(seq == 0)
+        def _():
+            back.late()
+
+    gather.close()
+    back.close()
+
+
+def front_call(whole, w_project, gain, fixed_args, most, cotangent, w_down, number):
+    starts, cosine, sine, query_gain, key_gain = fixed_args
+    rows, width = cotangent.shape
+    length = cosine.shape[1]
+    depth = query_gain.shape[1]
+    columns = w_project.shape[1]
+    heads = columns // depth - 2
+    outs = (
+        shape((4, rows, 2 * width)),
+        shape((rows, 128), F32),
+        shape((4, rows, columns), F32),
+        shape((4, rows, heads * depth)),
+        shape((2, length, heads * depth)),
+        shape((2, length, depth)),
+        shape((2, length, depth)),
+        shape((2, heads, length, 1), F32),
+        shape((4, rows, 2 * width)),
+        shape((w_down.shape[0] // 2, 2 * width)),
+    )
+    return pl.pallas_call(
+        lambda *refs: front_kernel(most, *refs),
+        out_shape=outs,
+        in_specs=[IN_VMEM] * 9 + [IN_ANY],
+        out_specs=[IN_VMEM] * 8 + [IN_ANY] * 2,
+        scratch_shapes=gather_scratch(rows, width)
+        + wire_scratch(GATHER_KINDS + SHARE_KINDS, width // CHUNK)
+        + [pltpu.SemaphoreType.DMA((1,))],
+        compiler_params=remote_params(number),
+        cost_estimate=cost(16 * rows * width * columns, 64 * rows * width),
+    )(whole, w_project, gain, *fixed_args, cotangent, w_down)
+
+
+def branch_kernel(
+    rows_ref,
+    weight_ref,
+    input_ref,
+    gate_ref,
+    up_ref,
+    residual_ref,
+    whole_ref,
+    both_ref,
+    *scratch,
+):
+    bufs = scratch[:7]
+    own, gather_sem, send_sems, recv_sems, both_sem = scratch[7:]
+    width = input_ref.shape[1]
+    greet(neighbours() + planes())
+    wires = Wires(send_sems, recv_sems)
+    reduce = Reduce(wires, rows_ref, weight_ref, False, bufs)
+    gather = Gather(wires, REDUCE_KINDS, whole_ref, own, gather_sem)
+    both = Share(
+        wires, REDUCE_KINDS + GATHER_KINDS, (gate_ref, up_ref), both_ref, True, both_sem
+    )
+    both.start()
+    reduce.start()
+    both.middle()
+    reduce.middle()
+
+    @pl.loop(0, width // CHUNK)
+    def _(chunk):
+        at = lanes(chunk, 0, width)
+        residual = input_ref[:, at].astype(F32) + reduce.total(chunk)
+        residual_ref[:, at] = residual
+        own[chunk] = residual.astype(B16)
+        gather.send(chunk)
+
+    both.late()
+    gather.relay()
+    gather.close()
+    both.close()
+    reduce.close()
+
+
+def branch_call(rows, weight, inputs, w_gate, w_up, number):
+    height, width = inputs.shape
+    count = width // CHUNK
+    return pl.pallas_call(
+        branch_kernel,
+        out_shape=(
+            shape((height, width), F32),
+            shape((4, height, 2 * width)),
+            shape((2 * width, w_gate.shape[1])),
+        ),
+        in_specs=[IN_VMEM] * 3 + [IN_ANY] * 2,
+        out_specs=(IN_VMEM, IN_ANY, IN_ANY),
+        scratch_shapes=reduce_scratch(height, width)
+        + gather_scratch(height, width)
+        + wire_scratch(REDUCE_KINDS + GATHER_KINDS + SHARE_KINDS, count)
+        + [pltpu.SemaphoreType.DMA((2,))],
+        compiler_params=remote_params(number),
+        cost_estimate=cost(16 * height * rows.shape[2] * width, 64 * height * width),
+    )(rows, weight, inputs, w_gate, w_up)
+
+
+def units_kernel(
+    whole_ref, grad_ref, both_ref, back_ref, gain_ref, second_ref, hidden_ref, unit_ref, scale_ref, stats_ref
+):
+    units = hidden_ref.shape[1]
+    value = whole_ref[...].astype(F32)
+    scale = lax.rsqrt(jnp.mean(value * value, axis=1, keepdims=True) + EPS)
+    second = (value * scale * gain_ref[...]).astype(B16)
+    second_ref[...] = second
+    scale_ref[...] = jnp.broadcast_to(scale, scale_ref.shape)
+    total = jnp.zeros((value.shape[0], 1), F32)
+    for low in range(0, units, CHUNK):
+        at = slice(low, low + CHUNK)
+        beside = slice(units + low, units + low + CHUNK)
+        gate = jnp.dot(second, both_ref[:, at], preferred_element_type=F32)
+        upper = jnp.dot(second, both_ref[:, beside], preferred_element_type=F32)
+        hidden_grad = rows_dot(grad_ref[...], back_ref[at, :])
+        sigma = jax.nn.sigmoid(gate)
+        passed = gate * sigma
+        hidden_ref[:, at] = (passed * upper).astype(B16)
+        gate_grad = (hidden_grad * upper * (sigma + passed * (1.0 - sigma))).astype(B16)
+        up_grad = (hidden_grad * passed).astype(B16)
+        unit_ref[:, at] = gate_grad
+        unit_ref[:, beside] = up_grad
+        total += jnp.sum(
+            gate_grad.astype(F32) * gate + up_grad.astype(F32) * upper, axis=1, keepdims=True
+        )
+    stats_ref[...] = jnp.zeros_like(stats_ref)
+    put_stats(stats_ref, 0, total)
+
+
+def units_call(whole, grad, w_both, w_back, gain):
+    tokens, width = whole.shape
+    units = w_back.shape[0]
+    tiles = tokens // BLOCK
+
+    def tile(columns):
+        return pl.BlockSpec((BLOCK, columns), lambda i: (i, 0))
+
+    def all_of(item):
+        return pl.BlockSpec(item.shape, lambda i: (0, 0))
+
+    return pl.pallas_call(
+        units_kernel,
+        out_shape=(
+            shape((tokens, width)),
+            shape((tokens, units)),
+            shape((tokens, 2 * units)),
+            shape((tokens, 128), F32),
+            shape((tiles, 8, 128), F32),
+        ),
+        grid=(tiles,),
+        in_specs=[tile(width), tile(width), all_of(w_both), all_of(w_back), all_of(gain)],
+        out_specs=(
+            tile(width),
+            tile(units),
+            tile(2 * units),
+            tile(128),
+            pl.BlockSpec((1, 8, 128), lambda i: (i, 0, 0)),
+        ),
+        compiler_params=pltpu.CompilerParams(vmem_limit_bytes=VMEM_MOST),
+        cost_estimate=cost(6 * tokens * width * units, 20 * tokens * width // 2),
+    )(whole, grad, w_both, w_back, gain)
+
+
+def share_stats(wires, base, stats_ref, recv):
+    side, across, core = neighbours()
+    first = wires.copy(base, 0, stats_ref.at[4:8], recv.at[0:4], core)
+    first.start()
+    first.wait()
+    stats_ref[0:4] = stats_ref[0:4] + recv[0:4]
+    second = wires.copy(base, 1, stats_ref.at[2:4], recv.at[4:6], across)
+    second.start()
+    second.wait()
+    stats_ref[0:2] = stats_ref[0:2] + recv[4:6]
+    third = wires.copy(base, 2, stats_ref.at[0:2], recv.at[6:8], side)
+    third.start()
+    third.wait()
+    stats_ref[0:2] = stats_ref[0:2] + recv[6:8]
+
+
+def pull_columns(stats_ref, scale_ref, column_ref, width):
+    for part in range(scale_ref.shape[0] // 128):
+        at = slice(part * 128, (part + 1) * 128)
+        scale = scale_ref[at, :]
+        column_ref[at, :] = (
+            stand(stats_ref[part // 2, part % 2 : part % 2 + 1, :]) * scale * scale / (2 * width)
+        )
+
+
+def pulled(reduce, chunk, refs, column_ref):
+    scale_ref, value_ref, gain_ref, base_ref = refs
+    at = lanes(chunk, 0, value_ref.shape[1])
+    upstream = reduce.total(chunk)
+    value = value_ref[:, at].astype(F32)
+    scale = scale_ref[:, 0:1]
+    back = scale * gain_ref[:, at] * upstream - value * column_ref[:, 0:1]
+    return at, base_ref[:, at].astype(F32) + back, upstream * value * scale
+
+
+def tile_columns(tile):
+    return pl.ds(pl.multiple_of(tile * BLOCK, BLOCK), BLOCK)
+
+
+def middle_kernel(
+    rows_ref,
+    weight_ref,
+    stats_in_ref,
+    scale_ref,
+    value_ref,
+    gain_ref,
+    base_ref,
+    down_in_ref,
+    second_ref,
+    result_ref,
+    gain_grad_ref,
+    whole_ref,
+    down_mine_ref,
+    down_theirs_ref,
+    gate_mine_ref,
+    gate_theirs_ref,
+    up_ref,
+    *scratch,
+):
+    bufs = scratch[:7]
+    stats_ref, stats_recv, column_ref, send_sems, recv_sems, own, gather_sem = scratch[7:14]
+    down_ref, gate_ref, stream, stream_sem, down_sem = scratch[14:19]
+    down_bufs, gate_bufs = scratch[19:21], scratch[21:23]
+    rows, width = value_ref.shape
+    units = up_ref.shape[2]
+    load = pltpu.make_async_copy(down_in_ref, down_ref, down_sem)
+    load.start()
+
+    def fetch(step):
+        return pltpu.make_async_copy(
+            second_ref.at[:, :, tile_columns(turn_tile(step))],
+            stream.at[lax.rem(step, 2)],
+            stream_sem.at[lax.rem(step, 2)],
+        )
+
+    fetch(0).start()
+    stats_ref[...] = stats_in_ref[...]
+    greet(neighbours() + planes())
+    wires = Wires(send_sems, recv_sems)
+    base = REDUCE_KINDS + 1 + GATHER_KINDS
+    down = Fold(wires, base, down_ref, down_bufs, down_mine_ref, down_theirs_ref)
+    gate = Fold(wires, base + FOLD_KINDS, gate_ref, gate_bufs, gate_mine_ref, gate_theirs_ref)
+    load.wait()
+    down.start()
+    reduce = Reduce(wires, rows_ref, weight_ref, True, bufs)
+    reduce.start()
+    share_stats(wires, REDUCE_KINDS, stats_ref, stats_recv)
+    pull_columns(stats_ref, scale_ref, column_ref, width)
+
+    def make(step):
+        @pl.when(step < 7)
+        def _():
+            fetch(step + 1).start()
+
+        fetch(step).wait()
+        left = stream[lax.rem(step, 2)].reshape(4 * rows, BLOCK)
+        tile = turn_tile(step)
+        flat = rows_ref[...].reshape(4 * rows, 2 * units)
+        gate_ref[tile] = weight_grad(left, flat[:, :units]).astype(B16)
+        up_ref[tile] = weight_grad(left, flat[:, units:]).astype(B16)
+
+    @pl.loop(0, 4)
+    def _(step):
+        make(step)
+        gate.near(lax.div(step, 2), lax.rem(step, 2)).start()
+
+    reduce.middle()
+
+    @pl.loop(4, 8)
+    def _(step):
+        make(step)
+
+    down.middle()
+    gather = Gather(wires, REDUCE_KINDS + 1, whole_ref, own, gather_sem)
+
+    @pl.loop(0, width // CHUNK)
+    def _(chunk):
+        at, result, share = pulled(
+            reduce, chunk, (scale_ref, value_ref, gain_ref, base_ref), column_ref
+        )
+        result_ref[:, at] = result
+        own[chunk] = result.astype(B16)
+        gather.send(chunk)
+        gain_grad_ref[:, at] = jnp.sum(share, axis=0, keepdims=True)
+
+    down.late()
+    gather.relay()
+    gate.middle()
+    gather.close()
+    gate.late()
+    down.close()
+    gate.close()
+    reduce.close()
+
+
+def middle_call(rows, weight, stats, scale, value, gain, base, down, second, number):
+    height, width = value.shape
+    count = width // CHUNK
+    units = down.shape[2]
+    quarter = down.shape[1]
+    return pl.pallas_call(
+        middle_kernel,
+        out_shape=(
+            shape((height, width), F32),
+            shape((1, width), F32),
+            shape((4, height, 2 * width)),
+            shape((quarter, units), F32),
+            shape((quarter, units)),
+            shape((quarter, units), F32),
+            shape((quarter, units)),
+            shape((8, quarter, units)),
+        ),
+        in_specs=[IN_VMEM] * 7 + [IN_ANY] * 2,
+        out_specs=(IN_VMEM, IN_VMEM, IN_ANY) + (IN_VMEM, IN_ANY) * 2 + (IN_VMEM,),
+        scratch_shapes=reduce_scratch(height, width)
+        + [
+            pltpu.VMEM((8, 8, 128), F32),
+            pltpu.VMEM((8, 8, 128), F32),
+            pltpu.VMEM((height, 128), F32),
+        ]
+        + wire_scratch(REDUCE_KINDS + 1 + GATHER_KINDS + 2 * FOLD_KINDS, count)
+        + gather_scratch(height, width)
+        + [
+            pltpu.VMEM((8, quarter, units), B16),
+            pltpu.VMEM((8, quarter, units), B16),
+            pltpu.VMEM((2, 4, height, BLOCK), B16),
+            pltpu.SemaphoreType.DMA((2,)),
+            pltpu.SemaphoreType.DMA,
+        ]
+        + fold_scratch(quarter, units) * 2,
+        compiler_params=remote_params(number),
+        cost_estimate=cost(48 * height * units * width, 64 * height * width),
+    )(rows, weight, stats, scale, value, gain, base, down, second)
+
+
+def last_kernel(
+    rows_ref,
+    weight_ref,
+    stats_in_ref,
+    scale_ref,
+    value_ref,
+    gain_ref,
+    base_ref,
+    extra_ref,
+    out_in_ref,
+    first_ref,
+    result_ref,
+    totals_ref,
+    out_mine_ref,
+    out_theirs_ref,
+    project_mine_ref,
+    project_theirs_ref,
+    *scratch,
+):
+    bufs = scratch[:7]
+    stats_ref, stats_recv, column_ref, send_sems, recv_sems = scratch[7:12]
+    out_ref, project_ref, whole, sums_ref, sums_recv, load_sem = scratch[12:18]
+    out_bufs, project_bufs = scratch[18:20], scratch[20:22]
+    rows, width = value_ref.shape
+    loads = [
+        pltpu.make_async_copy(out_in_ref, out_ref, load_sem.at[0]),
+        pltpu.make_async_copy(first_ref, whole, load_sem.at[1]),
+    ]
+    for load in loads:
+        load.start()
+    stats_ref[...] = stats_in_ref[...]
+    sums_ref[...] = jnp.zeros_like(sums_ref)
+    greet(neighbours() + planes())
+    wires = Wires(send_sems, recv_sems)
+    base = REDUCE_KINDS + 1
+    out = Fold(wires, base, out_ref, out_bufs, out_mine_ref, out_theirs_ref)
+    project = Fold(
+        wires, base + FOLD_KINDS, project_ref, project_bufs, project_mine_ref, project_theirs_ref
+    )
+    reduce = Reduce(wires, rows_ref, weight_ref, True, bufs)
+    reduce.start()
+    for load in loads:
+        load.wait()
+
+    def make(step):
+        tile = turn_tile(step)
+        left = whole[:, :, tile_columns(tile)].reshape(4 * rows, BLOCK)
+        grad = weight_grad(left, rows_ref[...].reshape(4 * rows, rows_ref.shape[2]))
+        project_ref[tile] = grad.astype(B16)
+        share = jnp.sum(
+            grad * weight_ref[tile_columns(tile), :].astype(F32), axis=1, keepdims=True
+        )
+        sums_ref[tile, 0:1, :] = lie(share[:128])
+        sums_ref[tile, 1:2, :] = lie(share[128:])
+
+    @pl.loop(0, 4)
+    def _(step):
+        make(step)
+        project.near(lax.div(step, 2), lax.rem(step, 2)).start()
+
+    out.start()
+    share_stats(wires, REDUCE_KINDS, stats_ref, stats_recv)
+    pull_columns(stats_ref, scale_ref, column_ref, width)
+    reduce.middle()
+
+    @pl.loop(4, 8)
+    def _(step):
+        make(step)
+
+    sums_ref[8] = extra_ref[0]
+    sums_ref[9] = extra_ref[1]
+    side, across, core = neighbours()
+    near, far = planes()
+    for hop, device in enumerate((core, across, near, far)):
+        move = wires.copy(base + 2 * FOLD_KINDS, hop, sums_ref, sums_recv.at[hop], device)
+        move.start()
+        move.wait()
+        sums_ref[...] = sums_ref[...] + sums_recv[hop]
+
+    @pl.loop(0, width // CHUNK)
+    def _(chunk):
+        at, result, _ = pulled(
+            reduce, chunk, (scale_ref, value_ref, gain_ref, base_ref), column_ref
+        )
+        result_ref[:, at] = result.astype(B16)
+
+    project.middle()
+    out.middle()
+    move = wires.copy(base + 2 * FOLD_KINDS + 1, 0, sums_ref, sums_recv.at[4], side)
+    move.start()
+    project.late()
+    out.late()
+    move.wait()
+    totals_ref[0:4] = sums_ref[0:4] + sums_recv[4, 4:8]
+    totals_ref[4:8] = sums_ref[4:8] + sums_recv[4, 0:4]
+    totals_ref[8] = sums_ref[8]
+    totals_ref[9] = sums_recv[4, 8]
+    totals_ref[10] = sums_ref[9] + sums_recv[4, 9]
+    project.close()
+    out.close()
+    reduce.close()
+
+
+def last_call(rows, weight, stats, scale, value, gain, base, extra, out, first, number):
+    height, width = value.shape
+    count = width // CHUNK
+    quarter, branch = out.shape[1:]
+    columns = rows.shape[2]
+    return pl.pallas_call(
+        last_kernel,
+        out_shape=(
+            shape((height, width)),
+            shape((11, 8, 128), F32),
+            shape((quarter, branch), F32),
+            shape((quarter, branch)),
+            shape((quarter, columns), F32),
+            shape((quarter, columns)),
+        ),
+        in_specs=[IN_VMEM] * 8 + [IN_ANY] * 2,
+        out_specs=(IN_VMEM, IN_VMEM) + (IN_VMEM, IN_ANY) * 2,
+        scratch_shapes=reduce_scratch(height, width)
+        + [
+            pltpu.VMEM((8, 8, 128), F32),
+            pltpu.VMEM((8, 8, 128), F32),
+            pltpu.VMEM((height, 128), F32),
+        ]
+        + wire_scratch(REDUCE_KINDS + 1 + 2 * FOLD_KINDS + 2, count)
+        + [
+            pltpu.VMEM((8, quarter, branch), B16),
+            pltpu.VMEM((8, quarter, columns), B16),
+            pltpu.VMEM((4, height, 2 * width), B16),
+            pltpu.VMEM((10, 8, 128), F32),
+            pltpu.VMEM((5, 10, 8, 128), F32),
+            pltpu.SemaphoreType.DMA((2,)),
+        ]
+        + fold_scratch(quarter, branch)
+        + fold_scratch(quarter, columns),
+        compiler_params=remote_params(number),
+        cost_estimate=cost(32 * height * columns * width, 64 * height * width),
+    )(rows, weight, stats, scale, value, gain, base, extra, out, first)
+
+
+def back_kernel(
+    most,
+    upstream,
+    hidden_ref,
+    down_ref,
+    residual_ref,
+    starts_ref,
+    cosine_ref,
+    sine_ref,
+    query_gain_ref,
+    key_gain_ref,
+    projected_ref,
+    query_ref,
+    key_ref,
+    value_ref,
+    log_ref,
+    up_in_ref,
+    output_ref,
+    result_ref,
+    stats_ref,
+    gains_ref,
+    up_mine_ref,
+    up_theirs_ref,
+    *scratch,
+):
+    bufs = scratch[:7]
+    query_acc, key_acc, value_acc, send_sems, recv_sems, up_ref, up_sem = scratch[7:14]
+    width = residual_ref.shape[1]
+    core = lax.rem(lax.axis_index("tx"), 2)
+    load = pltpu.make_async_copy(up_in_ref, up_ref, up_sem)
+    load.start()
+    greet(neighbours() + planes())
+    wires = Wires(send_sems, recv_sems)
+    up = Fold(wires, REDUCE_KINDS, up_ref, scratch[14:16], up_mine_ref, up_theirs_ref)
+    load.wait()
+    up.start()
+    reduce = Reduce(wires, hidden_ref, down_ref, False, bufs)
+    reduce.start()
+    stats_ref[...] = jnp.zeros_like(stats_ref)
+    fixed_refs = (starts_ref, cosine_ref, sine_ref, query_gain_ref, key_gain_ref)
+    saved_refs = (query_ref, key_ref, value_ref, log_ref)
+
+    @pl.loop(0, 2)
+    def _(seq):
+        attend_sequence_back(
+            core,
+            seq,
+            most,
+            projected_ref,
+            upstream,
+            fixed_refs,
+            saved_refs,
+            result_ref,
+            stats_ref,
+            gains_ref,
+            (query_acc, key_acc, value_acc),
+        )
+
+        @pl.when(seq == 0)
+        def _():
+            reduce.middle()
+
+    up.middle()
+
+    @pl.loop(0, width // CHUNK)
+    def _(chunk):
+        at = lanes(chunk, 0, width)
+        output_ref[:, at] = (residual_ref[:, at] + reduce.total(chunk)).astype(B16)
+
+    up.late()
+    up.close()
+    reduce.close()
+
+
+def back_call(upstream, hidden, w_back, residual, fixed_args, projected, saved, up, most, number):
+    height, width = residual.shape
+    _, cosine, _, query_gain, _ = fixed_args
+    depth = query_gain.shape[1]
+    length = cosine.shape[1]
+    columns = projected.shape[2]
+    heads = columns // depth - 2
+    return pl.pallas_call(
+        lambda *refs: back_kernel(most, *refs),
+        out_shape=(
+            shape((height, width)),
+            shape((4, height, columns)),
+            shape((8, 8, 128), F32),
+            shape((2, 8, depth), F32),
+            shape(up.shape[1:], F32),
+            shape(up.shape[1:]),
+        ),
+        in_specs=[IN_VMEM] * 14 + [IN_ANY],
+        out_specs=[IN_VMEM] * 5 + [IN_ANY],
+        scratch_shapes=reduce_scratch(height, width)
+        + [
+            pltpu.VMEM((length, heads * depth), F32),
+            pltpu.VMEM((length, depth), F32),
+            pltpu.VMEM((length, depth), F32),
+        ]
+        + wire_scratch(REDUCE_KINDS + FOLD_KINDS, width // CHUNK)
+        + [pltpu.VMEM(up.shape, B16), pltpu.SemaphoreType.DMA]
+        + fold_scratch(*up.shape[1:]),
+        compiler_params=remote_params(number),
+        cost_estimate=cost(16 * height * hidden.shape[2] * width, 64 * height * width),
+    )(upstream, hidden, w_back, residual, *fixed_args, projected, *saved, up)
+
+
+def product_grad(left, right):
+    return weight_grad(left, right).astype(B16)
+
+
+def plane_device(
+    tokens,
+    seg_ids,
+    w_query,
+    w_key,
+    w_value,
+    w_out,
+    w_gate,
+    w_up,
+    w_down,
+    attn_gain,
+    mlp_gain,
+    query_gain,
+    key_gain,
+    cotangent,
+):
+    spot = lax.axis_index("tx")
+    depth = query_gain.shape[0]
+    length = seg_ids.shape[1]
+    most = length // 2
+    rows, width = tokens.shape
+    head_width = w_query.shape[1] // 2
+    kv_width = w_key.shape[1] // 2
+    units = w_gate.shape[1] // 2
+
+    gains = jnp.stack([attn_gain, mlp_gain])
+    gains = jnp.concatenate([gains, swap_x(gains)], axis=1)
+    seg_all = in_order(seg_ids, swap_x(seg_ids), 0)
+    seg_all = jnp.where(lax.div(spot, 2) == 0, seg_all, seg_all[::-1])
+    index = jnp.arange(length, dtype=jnp.int32)[None]
+    edge = jnp.concatenate(
+        [jnp.ones((2, 1), dtype=jnp.bool_), seg_all[:, 1:] != seg_all[:, :-1]], axis=1
+    )
+    starts = lax.cummax(jnp.where(edge, index, 0), axis=1)
+    cosine, sine = rotary(index - starts, depth)
+    cosine = jnp.concatenate([cosine, cosine], axis=-1)
+    sine = jnp.concatenate([-sine, sine], axis=-1)
+    fixed_args = (starts[:, :, None], cosine, sine, query_gain[None], key_gain[None])
+
+    token_whole, w_project, w_branch = open_call(tokens, w_query, w_key, w_value, w_out, 0)
+    first, first_scale, projected, mixed, query, keys, values, logs, grad_whole, w_back = front_call(
+        token_whole, w_project, gains[0:1], fixed_args, most, cotangent, w_down, 1
+    )
+    residual, residual_whole, w_both = branch_call(mixed, w_branch, tokens, w_gate, w_up, 2)
+    flat = (4 * rows, 2 * width)
+    grad_flat = grad_whole.reshape(flat)
+    second, hidden, unit_grads, second_scale, unit_stats = units_call(
+        residual_whole.reshape(flat), grad_flat, w_both, w_back, gains[1:2]
+    )
+    tiles = lambda grad: grad.reshape(8, -1, grad.shape[1])
+    (
+        residual_grad,
+        mlp_gain_part,
+        branch_whole,
+        down_mine,
+        down_theirs,
+        gate_mine,
+        gate_theirs,
+        up_tiles,
+    ) = middle_call(
+        unit_grads.reshape(4, rows, 2 * units),
+        w_both,
+        unit_stats,
+        second_scale[:rows],
+        residual,
+        mlp_gain[None],
+        cotangent,
+        tiles(product_grad(grad_flat, hidden)),
+        second.reshape(4, rows, 2 * width),
+        3,
+    )
+    branch_flat = branch_whole.reshape(flat)
+    upstream = backward_with(w_branch)(branch_flat).astype(B16).reshape(4, rows, head_width)
+    out_tiles = tiles(product_grad(branch_flat, mixed.reshape(4 * rows, head_width)))
+    output, proj_grads, proj_stats, gain_parts, up_mine, up_theirs = back_call(
+        upstream,
+        hidden.reshape(4, rows, units),
+        w_back,
+        residual,
+        fixed_args,
+        projected,
+        (query, keys, values, logs),
+        up_tiles,
+        most,
+        4,
+    )
+    extra = jnp.stack(
+        [
+            mlp_gain_part.reshape(8, 128),
+            jnp.pad(jnp.sum(gain_parts[:, :2], axis=0), ((0, 6), (0, 0))),
+        ]
+    )
+    input_grad, totals, out_mine, out_theirs, project_mine, project_theirs = last_call(
+        proj_grads,
+        w_project,
+        proj_stats,
+        first_scale,
+        tokens,
+        attn_gain[None],
+        residual_grad,
+        extra,
+        out_tiles,
+        first,
+        5,
+    )
+    whole = lambda mine, theirs: in_order(mine, theirs.astype(F32), 1)
+    attn_sums = totals[:8, :2].reshape(-1) / gains[0]
+    attn_total = in_order(attn_sums[:width], attn_sums[width:], 0)
+    mlp_total = in_order(totals[8].reshape(-1), totals[9].reshape(-1), 0)
+    query_total, key_total = totals[10, 0], totals[10, 1]
+    down_share = whole(down_mine, down_theirs).T
+    out_share = whole(out_mine, out_theirs).T
+    gate_share = whole(gate_mine, gate_theirs)
+    up_share = whole(up_mine, up_theirs)
+    ends = (0, head_width, head_width + kv_width, head_width + 2 * kv_width)
+    query_share, key_share, value_share = (
+        whole(project_mine[:, low:high], project_theirs[:, low:high])
+        for low, high in zip(ends[:-1], ends[1:])
+    )
+    return (
+        output,
+        input_grad,
+        query_share,
+        key_share,
+        value_share,
+        out_share,
+        gate_share,
+        up_share,
+        down_share,
+        attn_total,
+        mlp_total,
+        query_total,
+        key_total,
+    )
+
+
 def solution(mesh):
     placed = (
         P(("dp", "tx"), "ty"),
@@ -331,7 +1820,7 @@
         P(("dp", "tx"), "ty"),
     )
     return jax.shard_map(
-        per_device,
+        plane_device if fits(mesh) else general_device,
         mesh=mesh,
         in_specs=placed,
         out_specs=(

time: 1710 us -> 649 us (0.38)
  the two profiles are of different devices: /device:TPU:10 before, /device:TPU:0 now
where the time goes in v2:
time: 649 us; the launch traced here: 639 us
  Pallas kernels  580 us (89%)
  other arithmetic  21.9 us (3%)
  matrix products  21.8 us (3%)
  local copies, waits for them, and re-layouts  11.3 us (2%)
    pallas_call x1, Pallas kernels, middle_call(): pl.pallas_call(middle_kernel, out_shape=(shape((height, width), F32), sha...  139 us
    pallas_call x1, Pallas kernels, branch_call(): pl.pallas_call(branch_kernel, out_shape=(shape((height, width), F32), sha...  104 us
    pallas_call x1, Pallas kernels, last_call(): pl.pallas_call(last_kernel, out_shape=(shape((height, width)), shape((11,...  98.2 us
    pallas_call x1, Pallas kernels, back_call(): pl.pallas_call(lambda *refs: back_kernel(most, *refs), out_shape=(shape((...  80.9 us
    pallas_call x1, Pallas kernels, front_call(): pl.pallas_call(lambda *refs: front_kernel(most, *refs), out_shape=outs, i...  72.8 us
    pallas_call x1, Pallas kernels, open_call(): pl.pallas_call(open_kernel, out_shape=(shape((4, rows, 2 * width)), shape...  54 us
    pallas_call x1, Pallas kernels, units_call(): pl.pallas_call(units_kernel, out_shape=(shape((tokens, width)), shape((to...  31.2 us
    dot_general x2, matrix products, weight_grad(): lax.dot_general(left, right, (((0,), (0,)), ((), ())), preferred_element_...  18.4 us
  transfers between devices with their start and end apart: 2, of which 0 were waited for; matrix products, arithmetic and copies ran while one was open for 2% of the time, Pallas kernels for 8%

profile of v2, /device:TPU:0, one launch (start us, length us, event | category | flops | bytes accessed | tf_op | source)
XLA Modules:
  0.0 639.4 jit_solution(1806190386713744860)
XLA Ops:
  0.7 3.0 collective-permute-start.1
  3.7 0.7 pad_maximum_fusion.8
  4.4 0.1 collective-permute-start
  4.5 54.0 %shard_map.237 = (bf16[4,512,2048]{2,1,0:T(8,128)(2,1)}, bf16[2048,512]{1,0:T(8,128)(2,1)}, bf16[256,2048]{1,0:T(8,128)(2,1)}) custom-call(bf16[512,1024]{1,0:T(8,128)(2,1)} %value_ref.3, bf16[1024,512]{1,0:T(8,128)(2,1)} %query_ref.1, bf16[1024,256]{1,0:T(8,128)(2,1)} %key_ref.1, bf16[1024,256]{1,0:T(8,128)(2,1)} %value_ref.2, bf16[512,1024]{1,0:T(8,128)(2,1)} %out_ref.1), custom_call_target="tpu_custom_call" | custom-call | bytes 16777216 | tf_op jit(solution)/shard_map/pallas_call | solution.py:994
  58.6 0.2 rev.3
  58.8 0.1 slice_compare_fusion
  58.9 0.1 fusion.2
  59.0 0.6 reduce-window.6
  59.6 0.2 slice_reduce_fusion
  59.8 0.2 reduce-window.9
  60.0 0.1 fusion.11
  60.0 0.1 broadcast_maximum_fusion
  60.1 3.7 fusion.1
  63.9 0.0 copy-start.11
  63.9 1.3 pad_maximum_fusion.2.refs_4_.refs_5_
  65.2 1.3 pad_maximum_fusion.3.refs_5_.refs_6_
  66.5 1.8 reduce_window_max.30.refs_3_.refs_4_
  68.4 0.6 fusion.4
  69.0 72.8 %shard_map.238 = (bf16[4,512,2048]{2,1,0:T(8,128)(2,1)}, f32[512,128]{1,0:T(8,128)}, f32[4,512,512]{2,1,0:T(8,128)}, bf16[4,512,256]{2,1,0:T(8,128)(2,1)}, bf16[...) custom-call(bf16[4,512,2048]{2,1,0:T(8,128)(2,1)} %get-tuple-element, ...), custom_call_target="tpu_custom_call" | custom-call | flops 4294967296 | bytes 33554432 | tf_op jit(solution)/shard_map/pallas_call | solution.py:1102
  141.8 104.1 %shard_map.239 = (f32[512,1024]{1,0:T(8,128)}, bf16[4,512,2048]{2,1,0:T(8,128)(2,1)}, bf16[2048,1536]{1,0:T(8,128)(2,1)}) custom-call(bf16[4,512,256]{2,1,0:T(8,128)(2,1)} %get-tuple-element.56.rows_ref, bf16[256,2048]{1,0:T(8,128)(2,1)} %get-tuple-element.57.weight_ref, bf16[512,1024]{1,0:T(8,128)(2,1)} %value_ref.3, bf16[1024,1536]{1,0:T(8,128)(2,1)} %gate_ref.1, ...), custom_call_target="tpu_custom_call" | custom-call | flops 2147483648 | bytes 33554432 | tf_op jit(solution)/shard_map/pallas_call | solution.py:1159
  246.0 31.2 %shard_map.240 = (bf16[2048,2048]{1,0:T(8,128)(2,1)}, bf16[2048,768]{1,0:T(8,128)(2,1)}, bf16[2048,1536]{1,0:T(8,128)(2,1)}, f32[2048,128]{1,0:T(8,128)}, f32[8,8,128]{2,1,0:T(8,128)}) custom-call(bf16[2048,2048]{1,0:T(8,128)(2,1)} %bitcast.72, bf16[2048,2048]{1,0:T(8,128)(2,1)} %bitcast.70, bf16[2048,1536]{1,0:T(8,128)(2,1)} %get-tuple-element.60.both_ref.weight_ref, ...), custom_call_target="tpu_custom_call" | custom-call | flops 19327352832 | bytes 41943040 | tf_op jit(solution)/shard_map/pallas_call | solution.py:1218
  277.2 11.4 %convolution_convert_fusion = bf16[2048,768]{1,0:T(8,128)(2,1)} fusion(bf16[2048,2048]{1,0:T(8,128)(2,1)} %bitcast.71, bf16[2048,768]{1,0:T(8,128)(2,1)} %get-tuple-element.66), kind=kOutput, calls=%fused_computation | convolution fusion | flops 6444023808 | bytes 14680064 | tf_op jit(solution)/shard_map/dot_general | solution.py:49
  288.5 1.7 slice.70.scale_ref
  290.2 139.1 %shard_map.241 = (f32[512,1024]{1,0:T(8,128)}, f32[1,1024]{1,0:T(1,128)}, bf16[4,512,2048]{2,1,0:T(8,128)(2,1)}, f32[256,768]{1,0:T(8,128)}, bf16[256,768]{1,0:T...) custom-call(bf16[4,512,1536]{2,1,0:T(8,128)(2,1)} %bitcast.75, ...), custom_call_target="tpu_custom_call" | custom-call | flops 19327352832 | bytes 33554432 | tf_op jit(solution)/shard_map/pallas_call | solution.py:1381
  429.3 7.0 %fusion = bf16[2048,256]{1,0:T(8,128)(2,1)} fusion(bf16[4,512,2048]{2,1,0:T(8,128)(2,1)} %get-tuple-element.68, bf16[4,512,256]{2,1,0:T(8,128)(2,1)S(1)} %copy-done.1), kind=kOutput, calls=%fused_computation.2 | convolution fusion | flops 2148007936 | bytes 10485760 | tf_op jit(solution)/shard_map/dot_general | solution.py:49
  436.3 3.4 convolution_convert_fusion.1
  439.7 80.9 %shard_map.242 = (bf16[512,1024]{1,0:T(8,128)(2,1)}, bf16[4,512,512]{2,1,0:T(8,128)(2,1)}, f32[8,8,128]{2,1,0:T(8,128)}, f32[2,8,128]{2,1,0:T(8,128)}, f32[256,768]{1,0:T(8,128)}, /*index=5*/bf16[256,768]{1,0:T(8,128)(2,1)}) custom-call(bf16[4,512,256]{2,1,0:T(8,128)(2,1)} %bitcast.53, bf16[4,512,768]{2,1,0:T(8,128)(2,1)} %bitcast.52, ...), custom_call_target="tpu_custom_call" | custom-call | flops 6442450944 | bytes 33554432 | tf_op jit(solution)/shard_map/pallas_call | solution.py:1639
  520.6 0.7 slice_reduce_fusion.1
  521.3 0.6 pad_maximum_fusion.9.extra_ref
  521.9 98.2 %shard_map.243 = (bf16[512,1024]{1,0:T(8,128)(2,1)}, f32[11,8,128]{2,1,0:T(8,128)}, f32[256,256]{1,0:T(8,128)}, bf16[256,256]{1,0:T(8,128)(2,1)}, f32[256,512]{1,0:T(8,128)}, /*index=5*/bf16[256,512]{1,0:T(8,128)(2,1)}) custom-call(bf16[4,512,512]{2,1,0:T(8,128)(2,1)} %get-tuple-element.76.rows_ref, bf16[2048,512]{1,0:T(8,128)(2,1)} %get-tuple-element.55.refs_1_.weight_ref, ...), custom_call_target="tpu_custom_call" | custom-call | flops 8589934592 | bytes 33554432 | tf_op jit(solution)/shard_map/pallas_call | solution.py:1524
  620.1 1.3 slice_bitcast_fusion
  621.4 0.8 slice.78
  622.2 0.7 select_bitcast_fusion.1
  622.9 1.8 convert_select_fusion.11
  624.6 1.9 convert_select_fusion.7
  626.6 0.1 maximum_bitcast_fusion.1
  626.6 1.0 copy.33
  627.6 1.4 convert_select_fusion.1
  629.0 0.2 maximum_bitcast_fusion
  629.2 1.6 copy.34
  630.9 1.4 convert_select_fusion.5
  632.3 1.3 pad_maximum_fusion
  633.6 0.9 pad_maximum_fusion.4
  634.5 1.4 pad_maximum_fusion.1
  635.9 0.6 pad_maximum_fusion.10
  636.5 0.8 pad_maximum_fusion.5
  637.3 1.0 copy.43
  638.3 1.0 copy.44
  (43 shorter events, 0.2 us)
Async XLA Ops:
  0.6 57.9 %copy-start.13 = (s32[1,1024]{1,0:T(1,128)S(1)}, s32[1,1024]{1,0:T(1,128)}, u32[]{:S(2)}) copy-start(s32[1,1024]{1,0:T(1,128)} %param.15) | copy-start | bytes 12292
  0.7 57.9 %collective-permute-start.1 = (s32[1,1024]{1,0:T(1,128)}, s32[1,1024]{1,0:T(1,128)S(1)}, u32[]{:S(2)}, u32[]{:S(2)}) collective-permute-start(s32[1,1024]{1,0:T(1,128)} %param.15), channel_id=1, source_target_pairs={{0,1},{1,0},{2,3},{3,2},{4,5},{5,4},{6,7},{7,6},{8,9},{9,8},{10,11... | collective-permute-start | bytes 12296 | tf_op jit(solution)/shard_map/ppermute | solution.py:324
  4.4 64.0 %collective-permute-start = (f32[2,1024]{1,0:T(2,128)S(1)}, f32[2,1024]{1,0:T(2,128)S(1)}, u32[]{:S(2)}, u32[]{:S(2)}) collective-permute-start(f32[2,1024]{1,0:T(2,128)S(1)} %pad_maximum_fusion.8), channel_id=1, source_target_pairs={{0,1},{1,0},{2,3},{3,2},{4,5},{5,4},{6,7},{7,6},{8,9},{9,8},{10,11... | collective-permute-start | bytes 24584 | tf_op jit(solution)/shard_map/ppermute | solution.py:324
  63.9 4.5 copy-start.11
  63.9 4.5 copy-start.12
  290.2 139.1 %copy-start.1 = (bf16[4,512,256]{2,1,0:T(8,128)(2,1)S(1)}, bf16[4,512,256]{2,1,0:T(8,128)(2,1)}, u32[]{:S(2)}) copy-start(bf16[4,512,256]{2,1,0:T(8,128)(2,1)} %get-tuple-element.56.rows_ref) | copy-start | bytes 3145732
  429.3 7.1 %copy-start = (bf16[256,2048]{1,0:T(8,128)(2,1)S(1)}, bf16[256,2048]{1,0:T(8,128)(2,1)}, u32[]{:S(2)}) copy-start(bf16[256,2048]{1,0:T(8,128)(2,1)} %get-tuple-element.57.weight_ref) | copy-start | bytes 3145732
  429.3 7.0 %copy-start.15 = (bf16[4,512,2048]{2,1,0:T(8,128)(2,1)S(1)}, bf16[4,512,2048]{2,1,0:T(8,128)(2,1)}, u32[]{:S(2)}) copy-start(bf16[4,512,2048]{2,1,0:T(8,128)(2,1)} %get-tuple-element.68) | copy-start | bytes 25165828
  439.7 81.6 %copy-start.14 = (f32[1,1024]{1,0:T(1,128)S(1)}, f32[1,1024]{1,0:T(1,128)}, u32[]{:S(2)}) copy-start(f32[1,1024]{1,0:T(1,128)} %get-tuple-element.80) | copy-start | bytes 12292
  521.9 101.0 %copy-start.10 = (f32[1,2048]{1,0:T(1,128)S(1)}, f32[1,2048]{1,0:T(1,128)}, u32[]{:S(2)}) copy-start(f32[1,2048]{1,0:T(1,128)} %get-tuple-element.140.refs_2_) | copy-start | bytes 24580
  620.1 7.6 %copy-start.5 = (f32[256,768]{1,0:T(8,128)S(1)}, f32[256,768]{1,0:T(8,128)}, u32[]{:S(2)}) copy-start(f32[256,768]{1,0:T(8,128)} %get-tuple-element.92) | copy-start | bytes 2359300
  620.1 7.6 %copy-start.6 = (f32[256,768]{1,0:T(8,128)S(1)}, f32[256,768]{1,0:T(8,128)}, u32[]{:S(2)}) copy-start(f32[256,768]{1,0:T(8,128)} %get-tuple-element.90) | copy-start | bytes 2359300
  630.9 2.8 copy-start.4
  632.3 4.2 copy-start.7
  632.3 4.2 copy-start.8
  632.3 4.2 copy-start.9
  633.6 3.7 copy-start.2
  634.5 3.8 copy-start.3

commit v3 on v2

--- a/solution.py
+++ b/solution.py
@@ -374,7 +374,7 @@
 BLOCK = 256
 
 
-def attend_sequence(core, seq, most, projected, fixed_refs, mixed, saved_refs):
+def attend_sequence(core, seq, most, projected, fixed_refs, mixed, saved_refs, between):
     starts_ref, cosine_ref, sine_ref, query_gain_ref, key_gain_ref = fixed_refs
     query_ref, key_ref, value_ref, log_ref = saved_refs
     rows = projected.shape[1]
@@ -400,6 +400,7 @@
                 else:
                     value_ref[seq, at : at + BLOCK, :] = value.astype(B16)
     for first in range(0, length, BLOCK):
+        between(first // BLOCK)
         low, high = window(first, BLOCK, most)
         mask = kept(first, BLOCK, low, high, starts_ref[seq, first : first + BLOCK, :])
         half, inner = divmod(first, rows)
@@ -530,7 +531,7 @@
 
 CHUNK = 256
 SIBLING, CORNER, FINAL_X, FINAL_Y = 0, 1, 2, 3
-REDUCE_KINDS = 4
+REDUCE_KINDS = 5
 OUT_X, OUT_Y, OUT_CORNER, CORE_OWN, CORE_X, CORE_Y, CORE_CORNER = range(7)
 GATHER_KINDS = 7
 SHARE_X, SHARE_Z = 0, 1
@@ -542,7 +543,7 @@
 
 
 class Gather:
-    def __init__(self, wires, base, whole, own, local_sem):
+    def __init__(self, wires, base, whole, own, local_sem, most=4):
         self.wires, self.base, self.whole, self.own, self.local_sem = (
             wires,
             base,
@@ -550,6 +551,7 @@
             own,
             local_sem,
         )
+        self.most = most
         self.width = whole.shape[2] // 2
         self.count = self.width // CHUNK
 
@@ -578,10 +580,10 @@
         for name in ("x", "y", "core", "local"):
             self.copy(name, chunk).start()
 
-    def relay(self):
-        @pl.loop(0, self.count)
+    def relay(self, low=0, high=None):
+        @pl.loop(low, self.count if high is None else high)
         def _(chunk):
-            even = lax.rem(chunk, 2) == 0
+            even = (lax.rem(chunk, 2) == 0) | (chunk >= self.most)
             self.copy("x", chunk).wait_recv()
 
             @pl.when(even)
@@ -613,7 +615,7 @@
 
 
 class Share:
-    def __init__(self, wires, base, sources, whole, by_rows, local_sems):
+    def __init__(self, wires, base, sources, whole, by_rows, local_sems, held=None):
         self.wires, self.base, self.sources, self.whole, self.by_rows, self.local_sems = (
             wires,
             base,
@@ -622,6 +624,7 @@
             by_rows,
             local_sems,
         )
+        self.held = held or sources
         self.size = (whole.shape[0] // 2 if by_rows else whole.shape[0]) // 4
 
     def quarter(self, plane):
@@ -651,7 +654,7 @@
 
     def local(self, index):
         mine = lax.axis_index("ty")
-        source = self.sources[index]
+        source = self.held[index]
         if self.by_rows:
             columns = source.shape[1] // 2
             offset = sum(item.shape[1] // 2 for item in self.sources[:index])
@@ -697,12 +700,49 @@
             self.local(index).wait()
 
 
+class Spread(Share):
+    def __init__(self, wires, base, source, whole, local_sems, quarter):
+        super().__init__(wires, base, (source,), whole, True, local_sems)
+        self.piece = quarter
+
+    def over(self, index):
+        if index == 2:
+            return super().over(index)
+        near, far = planes()
+        return self.wires.copy(
+            self.base + SHARE_Z,
+            index,
+            self.piece,
+            self.quarter(lax.axis_index("dp")),
+            far if index == 0 else near,
+        )
+
+    def own(self):
+        return pltpu.make_async_copy(
+            self.piece, self.quarter(lax.axis_index("dp")), self.local_sems.at[1]
+        )
+
+    def start(self):
+        self.over(0).start()
+        self.over(1).start()
+        self.local(0).start()
+        self.own().start()
+
+    def close(self):
+        self.over(1).wait_recv()
+        self.over(2).wait_recv()
+        for index in range(3):
+            self.over(index).wait_send()
+        self.local(0).wait()
+        self.own().wait()
+
+
 FOLD_NEAR, FOLD_FAR, FOLD_X = 0, 1, 2
 FOLD_KINDS = 3
 
 
 class Fold:
-    def __init__(self, wires, base, tiles, bufs, mine, theirs):
+    def __init__(self, wires, base, tiles, bufs, mine, theirs, first=None):
         self.wires, self.base, self.tiles, self.mine, self.theirs = (
             wires,
             base,
@@ -710,6 +750,7 @@
             mine,
             theirs,
         )
+        self.first = tiles if first is None else first
         self.near_recv, self.far_recv = bufs
         plane = lax.axis_index("dp")
         self.low = lax.rem(plane, 2)
@@ -719,7 +760,7 @@
         return half * 4 + 2 * high + low
 
     def near(self, half, high):
-        source = self.tiles.at[self.index(half, high, 1 - self.low)]
+        source = self.first.at[self.index(half, high, 1 - self.low)]
         slot = 2 * half + high
         return self.wires.copy(
             self.base + FOLD_NEAR, slot, source, self.near_recv.at[slot], planes()[0]
@@ -814,12 +855,12 @@
             return rows_dot(left, self.weight_ref[at, :])
         return jnp.dot(left, self.weight_ref[:, at], preferred_element_type=F32)
 
-    def sibling(self, chunk):
+    def sibling(self, chunk, half):
         return self.wires.copy(
-            SIBLING,
+            SIBLING + half * (REDUCE_KINDS - 1),
             chunk,
-            self.sibling_send.at[chunk],
-            self.sibling_recv.at[chunk],
+            self.sibling_send.at[lax.rem(chunk, 2), half],
+            self.sibling_recv.at[chunk, half],
             neighbours()[2],
         )
 
@@ -838,47 +879,63 @@
             FINAL_Y, chunk, self.out.at[1, chunk], self.y_recv.at[chunk], neighbours()[1]
         )
 
-    def start(self):
-        @pl.loop(0, self.count)
+    def give(self, chunk):
+        @pl.loop(0, 2)
+        def _(turn):
+            half = 1 - turn
+            self.sibling_send[lax.rem(chunk, 2), half] = self.product(2, chunk, half).astype(B16)
+            self.sibling(chunk, half).start()
+
+    def take(self, chunk):
+        rows = self.rows
+        even = lax.rem(chunk, 2) == 0
+        side, across, _ = neighbours()
+
+        @pl.loop(0, 2)
+        def _(turn):
+            half = 1 - turn
+            own = self.product(0, chunk, half)
+            self.sibling(chunk, half).wait_recv()
+            total = own + self.sibling_recv[chunk, half].astype(F32)
+
+            @pl.when(half == 1)
+            def _():
+                self.out[2, chunk] = total[rows:].astype(B16)
+                self.out[0, chunk] = total[:rows].astype(B16)
+
+                @pl.when(even)
+                def _():
+                    self.corner(chunk, side).start()
+                    self.final_x(chunk).start()
+
+                @pl.when(jnp.logical_not(even))
+                def _():
+                    self.corner(chunk, across).start()
+
+            @pl.when(half == 0)
+            def _():
+                self.kept_ref[chunk] = total[:rows]
+                self.out[1, chunk] = total[rows:].astype(B16)
+
+                @pl.when(jnp.logical_not(even))
+                def _():
+                    self.final_y(chunk).start()
+
+    def start(self, between=(lambda: None, lambda: None)):
+        self.give(0)
+        self.take(0)
+        self.give(1)
+        self.take(1)
+        between[0]()
+
+        @pl.loop(2, self.count)
         def _(chunk):
-            @pl.loop(0, 2)
-            def _(half):
-                self.sibling_send[chunk, half] = self.product(2, chunk, half).astype(B16)
-
-            self.sibling(chunk).start()
-
-        rows = self.rows
-
-        @pl.loop(0, self.count)
-        def _(chunk):
-            even = lax.rem(chunk, 2) == 0
-            self.sibling(chunk).wait_recv()
-
-            @pl.loop(0, 2)
-            def _(half):
-                total = self.product(0, chunk, half) + self.sibling_recv[chunk, half].astype(F32)
-
-                @pl.when(half == 1)
-                def _():
-                    self.out[0, chunk] = total[:rows].astype(B16)
-                    self.out[2, chunk] = total[rows:].astype(B16)
-
-                @pl.when(half == 0)
-                def _():
-                    self.kept_ref[chunk] = total[:rows]
-                    self.out[1, chunk] = total[rows:].astype(B16)
-
-            side, across, _ = neighbours()
-
-            @pl.when(even)
-            def _():
-                self.corner(chunk, side).start()
-                self.final_x(chunk).start()
-
-            @pl.when(jnp.logical_not(even))
-            def _():
-                self.corner(chunk, across).start()
-                self.final_y(chunk).start()
+            for half in range(2):
+                self.sibling(chunk - 2, half).wait_send()
+            self.give(chunk)
+            self.take(chunk)
+
+        between[1]()
 
     def middle(self):
         @pl.loop(0, self.count)
@@ -905,9 +962,13 @@
         )
 
     def close(self):
+        @pl.loop(self.count - 2, self.count)
+        def _(chunk):
+            for half in range(2):
+                self.sibling(chunk, half).wait_send()
+
         @pl.loop(0, self.count)
         def _(chunk):
-            self.sibling(chunk).wait_send()
             self.corner(chunk, neighbours()[0]).wait_send()
             self.final_x(chunk).wait_send()
             self.final_y(chunk).wait_send()
@@ -916,7 +977,7 @@
 def reduce_scratch(rows, width):
     count = width // CHUNK
     return [
-        pltpu.VMEM((count, 2, 2 * rows, CHUNK), B16),
+        pltpu.VMEM((2, 2, 2 * rows, CHUNK), B16),
         pltpu.VMEM((count, 2, 2 * rows, CHUNK), B16),
         pltpu.VMEM((count, rows, CHUNK), F32),
         pltpu.VMEM((3, count, rows, CHUNK), B16),
@@ -960,52 +1021,117 @@
 
 
 def open_kernel(
-    tokens_ref, query_ref, key_ref, value_ref, out_ref, whole_ref, project_ref, branch_ref, *scratch
+    tokens_ref,
+    query_ref,
+    key_ref,
+    value_ref,
+    out_ref,
+    gains_ref,
+    seg_ref,
+    rate_ref,
+    gains_all_ref,
+    starts_ref,
+    cosine_ref,
+    sine_ref,
+    whole_ref,
+    project_ref,
+    branch_ref,
+    *scratch,
 ):
-    own, gather_sem, send_sems, recv_sems, project_sem, branch_sem = scratch
+    own, gather_sem, send_sems, recv_sems, project_sem, branch_sem = scratch[:6]
+    gains_recv, seg_recv, seg_all = scratch[6:]
+    width = gains_ref.shape[1]
+    length = seg_ref.shape[1]
     cut(own, tokens_ref)
     greet(neighbours() + planes())
     wires = Wires(send_sems, recv_sems)
-    gather = Gather(wires, 0, whole_ref, own, gather_sem)
+    gather = Gather(wires, 0, whole_ref, own, gather_sem, 2)
+    base = GATHER_KINDS + 2 * SHARE_KINDS
+    side = neighbours()[0]
+    gains = wires.copy(base, 0, gains_ref, gains_recv, side)
+    segs = wires.copy(base, 1, seg_ref, seg_recv, side)
     shares = [
         Share(wires, GATHER_KINDS, (query_ref, key_ref, value_ref), project_ref, True, project_sem),
         Share(wires, GATHER_KINDS + SHARE_KINDS, (out_ref,), branch_ref, False, branch_sem),
     ]
+    gains.start()
+    segs.start()
     shares[0].start()
+    shares[1].start()
 
     @pl.loop(0, gather.count)
     def _(chunk):
         gather.send(chunk)
 
-    shares[1].start()
+    gains.wait()
+    segs.wait()
+    gains_all_ref[:, :width] = gains_ref[...]
+    gains_all_ref[:, width:] = gains_recv[...]
+    mine = lax.rem(lax.axis_index("ty") + lax.div(lax.axis_index("tx"), 2), 2)
+    seg_all[pl.ds(mine, 1)] = seg_ref[...].astype(F32)[None]
+    seg_all[pl.ds(1 - mine, 1)] = seg_recv[...].astype(F32)[None]
+
     shares[0].middle()
-    gather.relay()
     shares[1].middle()
-    shares[0].late()
-    shares[1].late()
+
+    @pl.loop(0, 2)
+    def _(seq):
+        for low in range(0, length, 128):
+            here = stand(seg_all[seq, :, low : low + 128])
+            before = jnp.zeros((128, 128), F32)
+            for other in range(0, length, 128):
+                before += (seg_all[seq, :, other : other + 128] < here).astype(F32)
+            start = jnp.sum(before, axis=1, keepdims=True)
+            at = slice(low, low + 128)
+            starts_ref[seq, at, :] = start.astype(jnp.int32)
+            row = lax.broadcasted_iota(jnp.int32, (128, 128), 0) + low
+            lane = lax.broadcasted_iota(jnp.int32, (128, 128), 1)
+            angle = (row.astype(F32) - start) * rate_ref[...]
+            cosine_ref[seq, at, :] = jnp.cos(angle)
+            sine = jnp.sin(angle)
+            sine_ref[seq, at, :] = jnp.where(lane < 64, -sine, sine)
+
+        @pl.when(seq == 0)
+        def _():
+            shares[0].late()
+            shares[1].late()
+            gather.relay(0, 2)
+
+    gather.relay(2)
     gather.close()
     shares[0].close()
     shares[1].close()
 
 
-def open_call(tokens, w_query, w_key, w_value, w_out, number):
+def open_call(tokens, w_query, w_key, w_value, w_out, gains, seg_ids, rate, number):
     rows, width = tokens.shape
     columns = (w_query.shape[1] + w_key.shape[1] + w_value.shape[1]) // 2
+    length = seg_ids.shape[1]
     return pl.pallas_call(
         open_kernel,
         out_shape=(
+            shape((2, 2 * width), F32),
+            shape((2, length, 1), jnp.int32),
+            shape((2, length, 128), F32),
+            shape((2, length, 128), F32),
             shape((4, rows, 2 * width)),
             shape((2 * width, columns)),
             shape((w_out.shape[0] // 2, 2 * width)),
         ),
-        in_specs=[IN_VMEM] + [IN_ANY] * 4,
-        out_specs=(IN_ANY,) * 3,
+        in_specs=[IN_VMEM] * 8,
+        out_specs=(IN_VMEM,) * 4 + (IN_ANY,) * 3,
         scratch_shapes=gather_scratch(rows, width)
-        + wire_scratch(GATHER_KINDS + 2 * SHARE_KINDS, width // CHUNK)
-        + [pltpu.SemaphoreType.DMA((3,)), pltpu.SemaphoreType.DMA((1,))],
+        + wire_scratch(GATHER_KINDS + 2 * SHARE_KINDS + 1, width // CHUNK)
+        + [
+            pltpu.SemaphoreType.DMA((3,)),
+            pltpu.SemaphoreType.DMA((1,)),
+            pltpu.VMEM((2, width), F32),
+            pltpu.VMEM((1, length), jnp.int32),
+            pltpu.VMEM((2, 1, length), F32),
+        ],
         compiler_params=remote_params(number),
         cost_estimate=cost(0, 32 * rows * width),
-    )(tokens, w_query, w_key, w_value, w_out)
+    )(tokens, w_query, w_key, w_value, w_out, gains, seg_ids, rate)
 
 
 def front_kernel(
@@ -1020,6 +1146,7 @@
     key_gain_ref,
     grad_ref,
     down_ref,
+    gate_in_ref,
     first_ref,
     scale_ref,
     projected_ref,
@@ -1030,31 +1157,72 @@
     log_ref,
     grad_whole_ref,
     back_ref,
+    gate_ref,
     *scratch,
 ):
-    own, gather_sem, send_sems, recv_sems, back_sem = scratch
+    own, gather_sem, send_sems, recv_sems, back_sem, tokens, firsts, tile_sem = scratch
     core = lax.rem(lax.axis_index("tx"), 2)
     cut(own, grad_ref)
+    rows = whole_ref.shape[1]
+
+    def spot(ref, tile):
+        at = pl.ds(pl.multiple_of(lax.rem(tile, rows // BLOCK) * BLOCK, BLOCK), BLOCK)
+        return ref.at[lax.div(tile, rows // BLOCK), at, :]
+
+    def fetch(tile):
+        slot = lax.rem(tile, 2)
+        return pltpu.make_async_copy(spot(whole_ref, tile), tokens.at[slot], tile_sem.at[0, slot])
+
+    def store(tile):
+        slot = lax.rem(tile, 2)
+        return pltpu.make_async_copy(firsts.at[slot], spot(first_ref, tile), tile_sem.at[1, slot])
+
+    fetch(0).start()
     greet(neighbours() + planes())
     wires = Wires(send_sems, recv_sems)
-    gather = Gather(wires, 0, grad_whole_ref, own, gather_sem)
+    gather = Gather(wires, 0, grad_whole_ref, own, gather_sem, 0)
     back = Share(wires, GATHER_KINDS, (down_ref,), back_ref, False, back_sem)
+    size, columns = gate_ref.shape
+    gate = wires.copy(
+        GATHER_KINDS + SHARE_KINDS,
+        0,
+        gate_in_ref.at[
+            pl.ds(pl.multiple_of(lax.axis_index("dp") * size, size), size),
+            pl.ds(pl.multiple_of((1 - lax.axis_index("ty")) * columns, columns), columns),
+        ],
+        gate_ref,
+        neighbours()[0],
+    )
+    back.start()
+    gate.start()
 
     @pl.loop(0, gather.count)
     def _(chunk):
         gather.send(chunk)
 
-    back.start()
-    rows = whole_ref.shape[1]
-
-    @pl.loop(0, 4 * rows // BLOCK)
+    count = 4 * rows // BLOCK
+
+    @pl.loop(0, count)
     def _(tile):
+        slot = lax.rem(tile, 2)
         block = lax.div(tile, rows // BLOCK)
         at = pl.ds(pl.multiple_of(lax.rem(tile, rows // BLOCK) * BLOCK, BLOCK), BLOCK)
-        value = whole_ref[block, at, :].astype(F32)
+
+        @pl.when(tile < count - 1)
+        def _():
+            fetch(tile + 1).start()
+
+        fetch(tile).wait()
+
+        @pl.when(tile >= 2)
+        def _():
+            store(tile - 2).wait()
+
+        value = tokens[slot].astype(F32)
         scale = lax.rsqrt(jnp.mean(value * value, axis=1, keepdims=True) + EPS)
         first = (value * scale * gain_ref[...]).astype(B16)
-        first_ref[block, at, :] = first
+        firsts[slot] = first
+        store(tile).start()
         projected_ref[block, at, :] = jnp.dot(
             first, project_ref[...], preferred_element_type=F32
         )
@@ -1063,24 +1231,34 @@
         def _():
             scale_ref[at, :] = jnp.broadcast_to(scale, (BLOCK, 128))
 
-    gather.relay()
-    back.middle()
+        @pl.when(tile == count // 2)
+        def _():
+            back.middle()
+
     fixed_refs = (starts_ref, cosine_ref, sine_ref, query_gain_ref, key_gain_ref)
     saved_refs = (query_ref, key_ref, value_ref, log_ref)
 
     @pl.loop(0, 2)
     def _(seq):
-        attend_sequence(core, seq, most, projected_ref, fixed_refs, mixed_ref, saved_refs)
-
-        @pl.when(seq == 0)
-        def _():
-            back.late()
-
+        def between(turn):
+            @pl.when(seq == 0)
+            def _():
+                if turn == 0:
+                    back.late()
+                gather.relay(turn, turn + 1)
+
+        attend_sequence(
+            core, seq, most, projected_ref, fixed_refs, mixed_ref, saved_refs, between
+        )
+
+    for tile in range(count - 2, count):
+        store(tile).wait()
     gather.close()
     back.close()
-
-
-def front_call(whole, w_project, gain, fixed_args, most, cotangent, w_down, number):
+    gate.wait()
+
+
+def front_call(whole, w_project, gain, fixed_args, most, cotangent, w_down, w_gate, number):
     starts, cosine, sine, query_gain, key_gain = fixed_args
     rows, width = cotangent.shape
     length = cosine.shape[1]
@@ -1098,45 +1276,73 @@
         shape((2, heads, length, 1), F32),
         shape((4, rows, 2 * width)),
         shape((w_down.shape[0] // 2, 2 * width)),
+        shape((width // 4, w_gate.shape[1] // 2)),
     )
     return pl.pallas_call(
         lambda *refs: front_kernel(most, *refs),
         out_shape=outs,
-        in_specs=[IN_VMEM] * 9 + [IN_ANY],
-        out_specs=[IN_VMEM] * 8 + [IN_ANY] * 2,
+        in_specs=[IN_ANY] + [IN_VMEM] * 10,
+        out_specs=[IN_ANY] + [IN_VMEM] * 7 + [IN_ANY] * 3,
         scratch_shapes=gather_scratch(rows, width)
-        + wire_scratch(GATHER_KINDS + SHARE_KINDS, width // CHUNK)
-        + [pltpu.SemaphoreType.DMA((1,))],
+        + wire_scratch(GATHER_KINDS + SHARE_KINDS + 1, width // CHUNK)
+        + [
+            pltpu.SemaphoreType.DMA((1,)),
+            pltpu.VMEM((2, BLOCK, 2 * width), B16),
+            pltpu.VMEM((2, BLOCK, 2 * width), B16),
+            pltpu.SemaphoreType.DMA((2, 2)),
+        ],
         compiler_params=remote_params(number),
         cost_estimate=cost(16 * rows * width * columns, 64 * rows * width),
-    )(whole, w_project, gain, *fixed_args, cotangent, w_down)
+    )(whole, w_project, gain, *fixed_args, cotangent, w_down, w_gate)
 
 
 def branch_kernel(
-    rows_ref,
-    weight_ref,
-    input_ref,
-    gate_ref,
-    up_ref,
+    rows_in_ref,
+    weight_in_ref,
+    input_in_ref,
+    up_in_ref,
+    gate_in_ref,
+    quarter_ref,
     residual_ref,
     whole_ref,
-    both_ref,
+    up_ref,
+    gate_ref,
     *scratch,
 ):
     bufs = scratch[:7]
-    own, gather_sem, send_sems, recv_sems, both_sem = scratch[7:]
+    own, gather_sem, send_sems, recv_sems, up_sem = scratch[7:12]
+    held, load_sem, gate_sem = scratch[12:17], scratch[17], scratch[18]
+    rows_ref, weight_ref, input_ref, up_held, gate_held = held
+    loads = Loads(
+        (rows_in_ref, weight_in_ref, input_in_ref, up_in_ref, gate_in_ref), held, load_sem
+    )
+    loads.start()
     width = input_ref.shape[1]
     greet(neighbours() + planes())
     wires = Wires(send_sems, recv_sems)
     reduce = Reduce(wires, rows_ref, weight_ref, False, bufs)
-    gather = Gather(wires, REDUCE_KINDS, whole_ref, own, gather_sem)
-    both = Share(
-        wires, REDUCE_KINDS + GATHER_KINDS, (gate_ref, up_ref), both_ref, True, both_sem
-    )
-    both.start()
-    reduce.start()
-    both.middle()
+    gather = Gather(wires, REDUCE_KINDS, whole_ref, own, gather_sem, 0)
+    up = Share(
+        wires, REDUCE_KINDS + GATHER_KINDS, (up_in_ref,), up_ref, True, up_sem, (up_held,)
+    )
+    gate = Spread(
+        wires,
+        REDUCE_KINDS + GATHER_KINDS + SHARE_KINDS,
+        gate_held,
+        gate_ref,
+        gate_sem,
+        quarter_ref,
+    )
+    loads.wait(0, 2)
+
+    def between():
+        loads.wait(2, 5)
+        up.start()
+        gate.start()
+
+    reduce.start((between, gate.late))
     reduce.middle()
+    up.middle()
 
     @pl.loop(0, width // CHUNK)
     def _(chunk):
@@ -1146,36 +1352,41 @@
         own[chunk] = residual.astype(B16)
         gather.send(chunk)
 
-    both.late()
+    up.late()
     gather.relay()
     gather.close()
-    both.close()
+    up.close()
+    gate.close()
     reduce.close()
 
 
-def branch_call(rows, weight, inputs, w_gate, w_up, number):
+def branch_call(rows, weight, inputs, w_up, w_gate, quarter, number):
     height, width = inputs.shape
     count = width // CHUNK
+    loaded = (rows, weight, inputs, w_up, w_gate)
     return pl.pallas_call(
         branch_kernel,
         out_shape=(
             shape((height, width), F32),
             shape((4, height, 2 * width)),
-            shape((2 * width, w_gate.shape[1])),
+            shape((2 * width, w_up.shape[1] // 2)),
+            shape((2 * width, w_gate.shape[1] // 2)),
         ),
-        in_specs=[IN_VMEM] * 3 + [IN_ANY] * 2,
-        out_specs=(IN_VMEM, IN_ANY, IN_ANY),
+        in_specs=[IN_ANY] * 6,
+        out_specs=(IN_VMEM, IN_ANY, IN_ANY, IN_ANY),
         scratch_shapes=reduce_scratch(height, width)
         + gather_scratch(height, width)
-        + wire_scratch(REDUCE_KINDS + GATHER_KINDS + SHARE_KINDS, count)
+        + wire_scratch(REDUCE_KINDS + GATHER_KINDS + 2 * SHARE_KINDS, count)
+        + [pltpu.SemaphoreType.DMA((1,))]
+        + load_scratch(loaded)
         + [pltpu.SemaphoreType.DMA((2,))],
         compiler_params=remote_params(number),
         cost_estimate=cost(16 * height * rows.shape[2] * width, 64 * height * width),
-    )(rows, weight, inputs, w_gate, w_up)
+    )(*loaded, quarter)
 
 
 def units_kernel(
-    whole_ref, grad_ref, both_ref, back_ref, gain_ref, second_ref, hidden_ref, unit_ref, scale_ref, stats_ref
+    whole_ref, grad_ref, gates_ref, uppers_ref, back_ref, gain_ref, second_ref, hidden_ref, unit_ref, scale_ref, stats_ref
 ):
     units = hidden_ref.shape[1]
     value = whole_ref[...].astype(F32)
@@ -1187,8 +1398,8 @@
     for low in range(0, units, CHUNK):
         at = slice(low, low + CHUNK)
         beside = slice(units + low, units + low + CHUNK)
-        gate = jnp.dot(second, both_ref[:, at], preferred_element_type=F32)
-        upper = jnp.dot(second, both_ref[:, beside], preferred_element_type=F32)
+        gate = jnp.dot(second, gates_ref[:, at], preferred_element_type=F32)
+        upper = jnp.dot(second, uppers_ref[:, at], preferred_element_type=F32)
         hidden_grad = rows_dot(grad_ref[...], back_ref[at, :])
         sigma = jax.nn.sigmoid(gate)
         passed = gate * sigma
@@ -1201,16 +1412,18 @@
             gate_grad.astype(F32) * gate + up_grad.astype(F32) * upper, axis=1, keepdims=True
         )
     stats_ref[...] = jnp.zeros_like(stats_ref)
-    put_stats(stats_ref, 0, total)
-
-
-def units_call(whole, grad, w_both, w_back, gain):
+    for tile in range(stats_ref.shape[0]):
+        put_stats(stats_ref, tile, total[tile * BLOCK : (tile + 1) * BLOCK])
+
+
+def units_call(whole, grad, w_gates, w_uppers, w_back, gain):
     tokens, width = whole.shape
     units = w_back.shape[0]
-    tiles = tokens // BLOCK
+    size = 2 * BLOCK
+    tiles = tokens // size
 
     def tile(columns):
-        return pl.BlockSpec((BLOCK, columns), lambda i: (i, 0))
+        return pl.BlockSpec((size, columns), lambda i: (i, 0))
 
     def all_of(item):
         return pl.BlockSpec(item.shape, lambda i: (0, 0))
@@ -1222,36 +1435,67 @@
             shape((tokens, units)),
             shape((tokens, 2 * units)),
             shape((tokens, 128), F32),
-            shape((tiles, 8, 128), F32),
+            shape((2 * tiles, 8, 128), F32),
         ),
         grid=(tiles,),
-        in_specs=[tile(width), tile(width), all_of(w_both), all_of(w_back), all_of(gain)],
+        in_specs=[tile(width), tile(width)]
+        + [all_of(item) for item in (w_gates, w_uppers, w_back, gain)],
         out_specs=(
             tile(width),
             tile(units),
             tile(2 * units),
             tile(128),
-            pl.BlockSpec((1, 8, 128), lambda i: (i, 0, 0)),
+            pl.BlockSpec((2, 8, 128), lambda i: (i, 0, 0)),
         ),
         compiler_params=pltpu.CompilerParams(vmem_limit_bytes=VMEM_MOST),
         cost_estimate=cost(6 * tokens * width * units, 20 * tokens * width // 2),
-    )(whole, grad, w_both, w_back, gain)
-
-
-def share_stats(wires, base, stats_ref, recv):
-    side, across, core = neighbours()
-    first = wires.copy(base, 0, stats_ref.at[4:8], recv.at[0:4], core)
-    first.start()
-    first.wait()
-    stats_ref[0:4] = stats_ref[0:4] + recv[0:4]
-    second = wires.copy(base, 1, stats_ref.at[2:4], recv.at[4:6], across)
-    second.start()
-    second.wait()
-    stats_ref[0:2] = stats_ref[0:2] + recv[4:6]
-    third = wires.copy(base, 2, stats_ref.at[0:2], recv.at[6:8], side)
-    third.start()
-    third.wait()
-    stats_ref[0:2] = stats_ref[0:2] + recv[6:8]
+    )(whole, grad, w_gates, w_uppers, w_back, gain)
+
+
+class Loads:
+    def __init__(self, sources, targets, sems):
+        self.copies = [
+            pltpu.make_async_copy(source, target, sems.at[index])
+            for index, (source, target) in enumerate(zip(sources, targets))
+        ]
+
+    def start(self):
+        for copy in self.copies:
+            copy.start()
+
+    def wait(self, low, high):
+        for copy in self.copies[low:high]:
+            copy.wait()
+
+
+def load_scratch(items):
+    return [pltpu.VMEM(item.shape, item.dtype) for item in items] + [
+        pltpu.SemaphoreType.DMA((len(items),))
+    ]
+
+
+class Stats:
+    def __init__(self, wires, base, ref, recv):
+        self.ref, self.recv = ref, recv
+        side, across, core = neighbours()
+        self.hops = (
+            lambda: wires.copy(base, 0, ref.at[4:8], recv.at[0:4], core),
+            lambda: wires.copy(base, 1, ref.at[2:4], recv.at[4:6], across),
+            lambda: wires.copy(base, 2, ref.at[0:2], recv.at[6:8], side),
+        )
+        self.spans = ((4, 0), (2, 4), (2, 6))
+
+    def start(self, hop):
+        self.hops[hop]().start()
+
+    def finish(self, hop):
+        self.hops[hop]().wait()
+        size, at = self.spans[hop]
+        self.ref[0:size] = self.ref[0:size] + self.recv[at : at + size]
+
+    def step(self, hop):
+        self.finish(hop)
+        self.start(hop + 1)
 
 
 def pull_columns(stats_ref, scale_ref, column_ref, width):
@@ -1277,80 +1521,149 @@
     return pl.ds(pl.multiple_of(tile * BLOCK, BLOCK), BLOCK)
 
 
+SPLIT = 512
+
+
 def middle_kernel(
-    rows_ref,
-    weight_ref,
+    rows_in_ref,
+    gates_in_ref,
+    uppers_in_ref,
+    value_in_ref,
+    base_in_ref,
+    branch_in_ref,
+    mixed_in_ref,
     stats_in_ref,
     scale_ref,
-    value_ref,
     gain_ref,
-    base_ref,
     down_in_ref,
     second_ref,
     result_ref,
     gain_grad_ref,
+    upstream_ref,
+    out_ref,
     whole_ref,
-    down_mine_ref,
-    down_theirs_ref,
-    gate_mine_ref,
-    gate_theirs_ref,
-    up_ref,
-    *scratch,
+    rest_ref,
+    *refs,
 ):
+    ends, scratch = refs[:6], refs[6:]
     bufs = scratch[:7]
     stats_ref, stats_recv, column_ref, send_sems, recv_sems, own, gather_sem = scratch[7:14]
-    down_ref, gate_ref, stream, stream_sem, down_sem = scratch[14:19]
-    down_bufs, gate_bufs = scratch[19:21], scratch[21:23]
+    stream, stream_sem, down_sem, stage, stage_sem, upstream = scratch[14:20]
+    tiles = scratch[20:29]
+    weight_ref, rows_ref, value_ref, base_ref, branch_ref, mixed_ref = scratch[29:35]
+    load_sem = scratch[35]
     rows, width = value_ref.shape
-    units = up_ref.shape[2]
-    load = pltpu.make_async_copy(down_in_ref, down_ref, down_sem)
-    load.start()
-
-    def fetch(step):
+    columns = rows_ref.shape[2]
+    half = tiles[0].shape[2]
+    parts = [down_in_ref.at[:, :, index * half : (index + 1) * half] for index in range(2)]
+    downs = [
+        pltpu.make_async_copy(parts[index], tiles[3 * index], down_sem.at[index])
+        for index in range(2)
+    ]
+    units = gates_in_ref.shape[1]
+    loads = Loads(
+        (
+            rows_in_ref,
+            gates_in_ref,
+            uppers_in_ref,
+            value_in_ref,
+            base_in_ref,
+            branch_in_ref,
+            mixed_in_ref,
+        ),
+        (
+            rows_ref,
+            weight_ref.at[:, :units],
+            weight_ref.at[:, units:],
+            value_ref,
+            base_ref,
+            branch_ref,
+            mixed_ref,
+        ),
+        load_sem,
+    )
+
+    def fetch(ref, step, tile):
+        slot = lax.rem(step, 2)
         return pltpu.make_async_copy(
-            second_ref.at[:, :, tile_columns(turn_tile(step))],
-            stream.at[lax.rem(step, 2)],
-            stream_sem.at[lax.rem(step, 2)],
-        )
-
-    fetch(0).start()
+            ref.at[:, :, tile_columns(tile)], stream.at[slot], stream_sem.at[slot]
+        )
+
+    loads.start()
+    for load in downs:
+        load.start()
+    fetch(second_ref, 0, turn_tile(0)).start()
     stats_ref[...] = stats_in_ref[...]
     greet(neighbours() + planes())
     wires = Wires(send_sems, recv_sems)
     base = REDUCE_KINDS + 1 + GATHER_KINDS
-    down = Fold(wires, base, down_ref, down_bufs, down_mine_ref, down_theirs_ref)
-    gate = Fold(wires, base + FOLD_KINDS, gate_ref, gate_bufs, gate_mine_ref, gate_theirs_ref)
-    load.wait()
-    down.start()
+    folds = [
+        Fold(
+            wires,
+            base + index * FOLD_KINDS,
+            tiles[3 * index],
+            tiles[3 * index + 1 : 3 * index + 3],
+            ends[2 * index],
+            ends[2 * index + 1],
+            parts[index] if index < 2 else None,
+        )
+        for index in range(3)
+    ]
+    stats = Stats(wires, REDUCE_KINDS, stats_ref, stats_recv)
+    folds[0].start()
+    folds[1].start()
+    stats.start(0)
     reduce = Reduce(wires, rows_ref, weight_ref, True, bufs)
-    reduce.start()
-    share_stats(wires, REDUCE_KINDS, stats_ref, stats_recv)
-    pull_columns(stats_ref, scale_ref, column_ref, width)
+    loads.wait(0, 3)
+    reduce.start((lambda: stats.step(0), lambda: stats.step(1)))
+    made = folds[2]
+
+    def store(step):
+        slot = lax.rem(step, 2)
+        return pltpu.make_async_copy(
+            stage.at[slot], rest_ref.at[turn_tile(step)], stage_sem.at[slot]
+        )
 
     def make(step):
+        slot = lax.rem(step, 2)
+
         @pl.when(step < 7)
         def _():
-            fetch(step + 1).start()
-
-        fetch(step).wait()
-        left = stream[lax.rem(step, 2)].reshape(4 * rows, BLOCK)
-        tile = turn_tile(step)
-        flat = rows_ref[...].reshape(4 * rows, 2 * units)
-        gate_ref[tile] = weight_grad(left, flat[:, :units]).astype(B16)
-        up_ref[tile] = weight_grad(left, flat[:, units:]).astype(B16)
+            fetch(second_ref, step + 1, turn_tile(step + 1)).start()
+
+        fetch(second_ref, step, turn_tile(step)).wait()
+
+        @pl.when(step >= 2)
+        def _():
+            store(step - 2).wait()
+
+        left = stream[slot].reshape(4 * rows, BLOCK)
+        flat = rows_ref[...].reshape(4 * rows, columns)
+        made.tiles[turn_tile(step)] = weight_grad(left, flat[:, :SPLIT]).astype(B16)
+        for low in range(SPLIT, columns, SPLIT):
+            stage[slot, :, low - SPLIT : low] = weight_grad(
+                left, flat[:, low : low + SPLIT]
+            ).astype(B16)
+        store(step).start()
 
     @pl.loop(0, 4)
     def _(step):
         make(step)
-        gate.near(lax.div(step, 2), lax.rem(step, 2)).start()
+        made.near(lax.div(step, 2), lax.rem(step, 2)).start()
 
     reduce.middle()
+    stats.finish(2)
+    pull_columns(stats_ref, scale_ref, column_ref, width)
 
     @pl.loop(4, 8)
     def _(step):
         make(step)
 
-    down.middle()
+    for load in downs:
+        load.wait()
+    folds[0].middle()
+    folds[1].middle()
+    loads.wait(3, 7)
     gather = Gather(wires, REDUCE_KINDS + 1, whole_ref, own, gather_sem)
 
     @pl.loop(0, width // CHUNK)
@@ -1363,64 +1676,94 @@
         gather.send(chunk)
         gain_grad_ref[:, at] = jnp.sum(share, axis=0, keepdims=True)
 
-    down.late()
+    for step in (6, 7):
+        store(step).wait()
+    folds[2].middle()
     gather.relay()
-    gate.middle()
+    folds[0].late()
+    folds[1].late()
     gather.close()
-    gate.late()
-    down.close()
-    gate.close()
+    folds[2].late()
+    fetch(whole_ref, 0, 0).start()
+    upstream[...] = jnp.zeros_like(upstream)
+
+    @pl.loop(0, 8)
+    def _(tile):
+        @pl.when(tile < 7)
+        def _():
+            fetch(whole_ref, tile + 1, tile + 1).start()
+
+        fetch(whole_ref, tile, tile).wait()
+        left = stream[lax.rem(tile, 2)].reshape(4 * rows, BLOCK)
+        upstream[...] += rows_dot(left, branch_ref[:, tile_columns(tile)])
+        out_ref[tile] = weight_grad(left, mixed_ref[...].reshape(4 * rows, -1)).astype(B16)
+
+    upstream_ref[...] = upstream[...].astype(B16).reshape(upstream_ref.shape)
+    for fold in folds:
+        fold.close()
     reduce.close()
 
 
-def middle_call(rows, weight, stats, scale, value, gain, base, down, second, number):
+def middle_call(
+    rows, w_gates, w_uppers, stats, scale, value, gain, base, down, second, w_branch, mixed, number
+):
     height, width = value.shape
     count = width // CHUNK
-    units = down.shape[2]
-    quarter = down.shape[1]
+    columns = rows.shape[2]
+    quarter, units = down.shape[1:]
+    heads = mixed.shape[2]
+    sizes = (units // 2, units // 2, SPLIT)
+    ends, tiles = [], []
+    for size in sizes:
+        ends += [shape((quarter, size), F32), shape((quarter, size))]
+        tiles += [pltpu.VMEM((8, quarter, size), B16)] + fold_scratch(quarter, size)
+    loaded = (rows, w_gates, w_uppers, value, base, w_branch, mixed)
     return pl.pallas_call(
         middle_kernel,
-        out_shape=(
+        out_shape=[
             shape((height, width), F32),
             shape((1, width), F32),
+            shape((4, height, heads)),
+            shape((8, quarter, heads)),
             shape((4, height, 2 * width)),
-            shape((quarter, units), F32),
-            shape((quarter, units)),
-            shape((quarter, units), F32),
-            shape((quarter, units)),
-            shape((8, quarter, units)),
-        ),
-        in_specs=[IN_VMEM] * 7 + [IN_ANY] * 2,
-        out_specs=(IN_VMEM, IN_VMEM, IN_ANY) + (IN_VMEM, IN_ANY) * 2 + (IN_VMEM,),
+            shape((8, quarter, columns - SPLIT)),
+        ]
+        + ends,
+        in_specs=[IN_ANY] * 7 + [IN_VMEM] * 3 + [IN_ANY] * 2,
+        out_specs=[IN_VMEM] * 4 + [IN_ANY] * 2 + [IN_VMEM, IN_ANY] * 3,
         scratch_shapes=reduce_scratch(height, width)
         + [
             pltpu.VMEM((8, 8, 128), F32),
             pltpu.VMEM((8, 8, 128), F32),
             pltpu.VMEM((height, 128), F32),
         ]
-        + wire_scratch(REDUCE_KINDS + 1 + GATHER_KINDS + 2 * FOLD_KINDS, count)
+        + wire_scratch(REDUCE_KINDS + 1 + GATHER_KINDS + 3 * FOLD_KINDS, count)
         + gather_scratch(height, width)
         + [
-            pltpu.VMEM((8, quarter, units), B16),
-            pltpu.VMEM((8, quarter, units), B16),
             pltpu.VMEM((2, 4, height, BLOCK), B16),
             pltpu.SemaphoreType.DMA((2,)),
-            pltpu.SemaphoreType.DMA,
+            pltpu.SemaphoreType.DMA((2,)),
+            pltpu.VMEM((2, quarter, columns - SPLIT), B16),
+            pltpu.SemaphoreType.DMA((2,)),
+            pltpu.VMEM((4 * height, heads), F32),
         ]
-        + fold_scratch(quarter, units) * 2,
+        + tiles
+        + [pltpu.VMEM((2 * width, columns), B16)]
+        + load_scratch((rows,) + loaded[3:])[:-1]
+        + [pltpu.SemaphoreType.DMA((len(loaded),))],
         compiler_params=remote_params(number),
         cost_estimate=cost(48 * height * units * width, 64 * height * width),
-    )(rows, weight, stats, scale, value, gain, base, down, second)
+    )(*loaded, stats, scale, gain, down, second)
 
 
 def last_kernel(
-    rows_ref,
-    weight_ref,
+    rows_in_ref,
+    weight_in_ref,
+    value_in_ref,
+    base_in_ref,
     stats_in_ref,
     scale_ref,
-    value_ref,
     gain_ref,
-    base_ref,
     extra_ref,
     out_in_ref,
     first_ref,
@@ -1436,26 +1779,29 @@
     stats_ref, stats_recv, column_ref, send_sems, recv_sems = scratch[7:12]
     out_ref, project_ref, whole, sums_ref, sums_recv, load_sem = scratch[12:18]
     out_bufs, project_bufs = scratch[18:20], scratch[20:22]
+    rows_ref, weight_ref, value_ref, base_ref = scratch[22:26]
     rows, width = value_ref.shape
-    loads = [
-        pltpu.make_async_copy(out_in_ref, out_ref, load_sem.at[0]),
-        pltpu.make_async_copy(first_ref, whole, load_sem.at[1]),
-    ]
-    for load in loads:
-        load.start()
+    loads = Loads(
+        (rows_in_ref, weight_in_ref, first_ref, value_in_ref, base_in_ref, out_in_ref),
+        (rows_ref, weight_ref, whole, value_ref, base_ref, out_ref),
+        load_sem,
+    )
+    loads.start()
     stats_ref[...] = stats_in_ref[...]
     sums_ref[...] = jnp.zeros_like(sums_ref)
+    sums_ref[8] = extra_ref[0]
+    sums_ref[9] = extra_ref[1]
     greet(neighbours() + planes())
     wires = Wires(send_sems, recv_sems)
     base = REDUCE_KINDS + 1
-    out = Fold(wires, base, out_ref, out_bufs, out_mine_ref, out_theirs_ref)
+    out = Fold(wires, base, out_ref, out_bufs, out_mine_ref, out_theirs_ref, out_in_ref)
     project = Fold(
         wires, base + FOLD_KINDS, project_ref, project_bufs, project_mine_ref, project_theirs_ref
     )
-    reduce = Reduce(wires, rows_ref, weight_ref, True, bufs)
-    reduce.start()
-    for load in loads:
-        load.wait()
+    stats = Stats(wires, REDUCE_KINDS, stats_ref, stats_recv)
+    stats.start(0)
+    out.start()
+    loads.wait(0, 2)
 
     def make(step):
         tile = turn_tile(step)
@@ -1468,29 +1814,45 @@
         sums_ref[tile, 0:1, :] = lie(share[:128])
         sums_ref[tile, 1:2, :] = lie(share[128:])
 
+    side, across, core = neighbours()
+    near, far = planes()
+    hops = [
+        lambda hop=hop, device=device: wires.copy(
+            base + 2 * FOLD_KINDS, hop, sums_ref, sums_recv.at[hop], device
+        )
+        for hop, device in enumerate((core, across, near, far))
+    ]
+
+    def add(hop):
+        hops[hop]().wait()
+        sums_ref[...] = sums_ref[...] + sums_recv[hop]
+
+    reduce = Reduce(wires, rows_ref, weight_ref, True, bufs)
+    reduce.start((lambda: stats.step(0), lambda: stats.step(1)))
+    loads.wait(2, 3)
+
     @pl.loop(0, 4)
     def _(step):
         make(step)
         project.near(lax.div(step, 2), lax.rem(step, 2)).start()
 
-    out.start()
-    share_stats(wires, REDUCE_KINDS, stats_ref, stats_recv)
-    pull_columns(stats_ref, scale_ref, column_ref, width)
-    reduce.middle()
-
     @pl.loop(4, 8)
     def _(step):
         make(step)
 
-    sums_ref[8] = extra_ref[0]
-    sums_ref[9] = extra_ref[1]
-    side, across, core = neighbours()
-    near, far = planes()
-    for hop, device in enumerate((core, across, near, far)):
-        move = wires.copy(base + 2 * FOLD_KINDS, hop, sums_ref, sums_recv.at[hop], device)
-        move.start()
-        move.wait()
-        sums_ref[...] = sums_ref[...] + sums_recv[hop]
+    hops[0]().start()
+    loads.wait(3, 6)
+    add(0)
+    hops[1]().start()
+    reduce.middle()
+    out.middle()
+    stats.finish(2)
+    pull_columns(stats_ref, scale_ref, column_ref, width)
+    add(1)
+    hops[2]().start()
+    project.middle()
+    add(2)
+    hops[3]().start()
 
     @pl.loop(0, width // CHUNK)
     def _(chunk):
@@ -1499,12 +1861,11 @@
         )
         result_ref[:, at] = result.astype(B16)
 
-    project.middle()
-    out.middle()
+    out.late()
+    project.late()
+    add(3)
     move = wires.copy(base + 2 * FOLD_KINDS + 1, 0, sums_ref, sums_recv.at[4], side)
     move.start()
-    project.late()
-    out.late()
     move.wait()
     totals_ref[0:4] = sums_ref[0:4] + sums_recv[4, 4:8]
     totals_ref[4:8] = sums_ref[4:8] + sums_recv[4, 0:4]
@@ -1531,7 +1892,7 @@
             shape((quarter, columns), F32),
             shape((quarter, columns)),
         ),
-        in_specs=[IN_VMEM] * 8 + [IN_ANY] * 2,
+        in_specs=[IN_ANY] * 4 + [IN_VMEM] * 4 + [IN_ANY] * 2,
         out_specs=(IN_VMEM, IN_VMEM) + (IN_VMEM, IN_ANY) * 2,
         scratch_shapes=reduce_scratch(height, width)
         + [
@@ -1546,53 +1907,65 @@
             pltpu.VMEM((4, height, 2 * width), B16),
             pltpu.VMEM((10, 8, 128), F32),
             pltpu.VMEM((5, 10, 8, 128), F32),
-            pltpu.SemaphoreType.DMA((2,)),
+            pltpu.SemaphoreType.DMA((6,)),
         ]
         + fold_scratch(quarter, branch)
-        + fold_scratch(quarter, columns),
+        + fold_scratch(quarter, columns)
+        + load_scratch((rows, weight, value, base))[:4],
         compiler_params=remote_params(number),
         cost_estimate=cost(32 * height * columns * width, 64 * height * width),
-    )(rows, weight, stats, scale, value, gain, base, extra, out, first)
+    )(rows, weight, value, base, stats, scale, gain, extra, out, first)
 
 
 def back_kernel(
     most,
-    upstream,
-    hidden_ref,
-    down_ref,
-    residual_ref,
-    starts_ref,
-    cosine_ref,
-    sine_ref,
     query_gain_ref,
     key_gain_ref,
-    projected_ref,
-    query_ref,
-    key_ref,
-    value_ref,
-    log_ref,
-    up_in_ref,
-    output_ref,
-    result_ref,
-    stats_ref,
-    gains_ref,
-    up_mine_ref,
-    up_theirs_ref,
-    *scratch,
+    *refs,
 ):
+    operands, refs = refs[:12], refs[12:]
+    rest_ref, refs = refs[0], refs[1:]
+    output_ref, result_ref, stats_ref, gains_ref = refs[:4]
+    ends, scratch = refs[4:8], refs[8:]
     bufs = scratch[:7]
-    query_acc, key_acc, value_acc, send_sems, recv_sems, up_ref, up_sem = scratch[7:14]
+    query_acc, key_acc, value_acc, send_sems, recv_sems, rest_sem = scratch[7:13]
+    tiles = scratch[13:19]
+    held, load_sem = scratch[19:31], scratch[31]
+    hidden_ref, down_ref, upstream, starts_ref, cosine_ref, sine_ref = held[:6]
+    projected_ref, query_ref, key_ref, value_ref, log_ref, residual_ref = held[6:]
+    attend_loads = Loads(operands, held, load_sem)
+    attend_loads.start()
     width = residual_ref.shape[1]
     core = lax.rem(lax.axis_index("tx"), 2)
-    load = pltpu.make_async_copy(up_in_ref, up_ref, up_sem)
-    load.start()
+    parts = [rest_ref.at[:, :, index * SPLIT : (index + 1) * SPLIT] for index in range(2)]
+    loads = [
+        pltpu.make_async_copy(parts[index], tiles[3 * index], rest_sem.at[index])
+        for index in range(2)
+    ]
+    for load in loads:
+        load.start()
     greet(neighbours() + planes())
     wires = Wires(send_sems, recv_sems)
-    up = Fold(wires, REDUCE_KINDS, up_ref, scratch[14:16], up_mine_ref, up_theirs_ref)
-    load.wait()
-    up.start()
+    folds = [
+        Fold(
+            wires,
+            REDUCE_KINDS + index * FOLD_KINDS,
+            tiles[3 * index],
+            tiles[3 * index + 1 : 3 * index + 3],
+            ends[2 * index],
+            ends[2 * index + 1],
+            parts[index],
+        )
+        for index in range(2)
+    ]
+    for fold in folds:
+        fold.start()
     reduce = Reduce(wires, hidden_ref, down_ref, False, bufs)
+    attend_loads.wait(0, 2)
     reduce.start()
+    attend_loads.wait(2, 12)
+    for load in loads:
+        load.wait()
     stats_ref[...] = jnp.zeros_like(stats_ref)
     fixed_refs = (starts_ref, cosine_ref, sine_ref, query_gain_ref, key_gain_ref)
     saved_refs = (query_ref, key_ref, value_ref, log_ref)
@@ -1616,26 +1989,31 @@
         @pl.when(seq == 0)
         def _():
             reduce.middle()
-
-    up.middle()
+            folds[0].middle()
+
 
     @pl.loop(0, width // CHUNK)
     def _(chunk):
         at = lanes(chunk, 0, width)
         output_ref[:, at] = (residual_ref[:, at] + reduce.total(chunk)).astype(B16)
 
-    up.late()
-    up.close()
+    folds[1].middle()
+    folds[0].late()
+    folds[1].late()
+    for fold in folds:
+        fold.close()
     reduce.close()
 
 
-def back_call(upstream, hidden, w_back, residual, fixed_args, projected, saved, up, most, number):
+def back_call(upstream, hidden, w_back, residual, fixed_args, projected, saved, rest, most, number):
     height, width = residual.shape
     _, cosine, _, query_gain, _ = fixed_args
     depth = query_gain.shape[1]
     length = cosine.shape[1]
     columns = projected.shape[2]
     heads = columns // depth - 2
+    quarter = rest.shape[1]
+    loaded = (hidden, w_back, upstream) + fixed_args[:3] + (projected,) + saved + (residual,)
     return pl.pallas_call(
         lambda *refs: back_kernel(most, *refs),
         out_shape=(
@@ -1643,23 +2021,101 @@
             shape((4, height, columns)),
             shape((8, 8, 128), F32),
             shape((2, 8, depth), F32),
-            shape(up.shape[1:], F32),
-            shape(up.shape[1:]),
-        ),
-        in_specs=[IN_VMEM] * 14 + [IN_ANY],
-        out_specs=[IN_VMEM] * 5 + [IN_ANY],
+        )
+        + (shape((quarter, SPLIT), F32), shape((quarter, SPLIT))) * 2,
+        in_specs=[IN_VMEM] * 2 + [IN_ANY] * 13,
+        out_specs=[IN_VMEM] * 4 + [IN_VMEM, IN_ANY] * 2,
         scratch_shapes=reduce_scratch(height, width)
         + [
             pltpu.VMEM((length, heads * depth), F32),
             pltpu.VMEM((length, depth), F32),
             pltpu.VMEM((length, depth), F32),
         ]
-        + wire_scratch(REDUCE_KINDS + FOLD_KINDS, width // CHUNK)
-        + [pltpu.VMEM(up.shape, B16), pltpu.SemaphoreType.DMA]
-        + fold_scratch(*up.shape[1:]),
+        + wire_scratch(REDUCE_KINDS + 2 * FOLD_KINDS, width // CHUNK)
+        + [pltpu.SemaphoreType.DMA((2,))]
+        + ([pltpu.VMEM((8, quarter, SPLIT), B16)] + fold_scratch(quarter, SPLIT)) * 2
+        + load_scratch(loaded),
         compiler_params=remote_params(number),
         cost_estimate=cost(16 * height * hidden.shape[2] * width, 64 * height * width),
-    )(upstream, hidden, w_back, residual, *fixed_args, projected, *saved, up)
+    )(*fixed_args[3:], *loaded, rest)
+
+
+def finish_kernel(place_ref, *refs):
+    downs, both, out, project = refs[0:4], refs[4:10], refs[10:12], refs[12:14]
+    totals_ref, gain_ref = refs[14:16]
+    query_ref, key_ref, value_ref, out_ref, gate_ref, up_ref, down_ref = refs[16:23]
+    attn_ref, mlp_ref = refs[23:]
+    first = place_ref[0] == 0
+
+    def ordered(mine, theirs):
+        theirs = theirs.astype(F32)
+        return jnp.where(first, mine, theirs), jnp.where(first, theirs, mine)
+
+    def put(target, at, mine, theirs):
+        half = target.shape[1] // 2
+        low, high = ordered(mine, theirs)
+        target[:, at : at + mine.shape[1]] = low
+        target[:, half + at : half + at + mine.shape[1]] = high
+
+    def put_turned(target, at, mine, theirs):
+        half = target.shape[0] // 2
+        low, high = ordered(mine, theirs)
+        target[at : at + mine.shape[1], :] = low.T
+        target[half + at : half + at + mine.shape[1], :] = high.T
+
+    at = 0
+    for index in (0, 2):
+        put_turned(down_ref, at, downs[index][...], downs[index + 1][...])
+        at += downs[index].shape[1]
+    put_turned(out_ref, 0, out[0][...], out[1][...])
+    at = 0
+    for target in (query_ref, key_ref, value_ref):
+        size = target.shape[1] // 2
+        put(target, 0, project[0][:, at : at + size], project[1][:, at : at + size])
+        at += size
+    units = gate_ref.shape[1] // 2
+    at = 0
+    for index in (0, 2, 4):
+        low = 0
+        while low < both[index].shape[1]:
+            size = min(both[index].shape[1] - low, units - at % units)
+            put(
+                gate_ref if at < units else up_ref,
+                at % units,
+                both[index][:, low : low + size],
+                both[index + 1][:, low : low + size],
+            )
+            low += size
+            at += size
+    mine = jnp.concatenate([totals_ref[tile, 0:2] for tile in range(4)], axis=0)
+    theirs = jnp.concatenate([totals_ref[tile, 0:2] for tile in range(4, 8)], axis=0)
+    low, high = ordered(mine / gain_ref[0:8], theirs / gain_ref[8:16])
+    attn_ref[0:8], attn_ref[8:16] = low, high
+    low, high = ordered(totals_ref[8], totals_ref[9])
+    mlp_ref[0:8], mlp_ref[8:16] = low, high
+
+
+def finish_call(place, parts, totals, gain, sizes):
+    quarter = parts[0].shape[0]
+    queries, keys, branch, units = sizes
+    return pl.pallas_call(
+        finish_kernel,
+        out_shape=(
+            shape((quarter, queries), F32),
+            shape((quarter, keys), F32),
+            shape((quarter, keys), F32),
+            shape((branch, quarter), F32),
+            shape((quarter, units), F32),
+            shape((quarter, units), F32),
+            shape((units, quarter), F32),
+            shape((16, 128), F32),
+            shape((16, 128), F32),
+        ),
+        in_specs=[pl.BlockSpec(memory_space=pltpu.SMEM)] + [IN_VMEM] * (len(parts) + 2),
+        out_specs=[IN_VMEM] * 9,
+        compiler_params=pltpu.CompilerParams(vmem_limit_bytes=VMEM_MOST),
+        cost_estimate=cost(0, 16 * 1024 * 1024),
+    )(place, *parts, totals, gain)
 
 
 def product_grad(left, right):
@@ -1682,52 +2138,56 @@
     key_gain,
     cotangent,
 ):
-    spot = lax.axis_index("tx")
     depth = query_gain.shape[0]
-    length = seg_ids.shape[1]
-    most = length // 2
+    most = seg_ids.shape[1] // 2
     rows, width = tokens.shape
     head_width = w_query.shape[1] // 2
     kv_width = w_key.shape[1] // 2
     units = w_gate.shape[1] // 2
 
-    gains = jnp.stack([attn_gain, mlp_gain])
-    gains = jnp.concatenate([gains, swap_x(gains)], axis=1)
-    seg_all = in_order(seg_ids, swap_x(seg_ids), 0)
-    seg_all = jnp.where(lax.div(spot, 2) == 0, seg_all, seg_all[::-1])
-    index = jnp.arange(length, dtype=jnp.int32)[None]
-    edge = jnp.concatenate(
-        [jnp.ones((2, 1), dtype=jnp.bool_), seg_all[:, 1:] != seg_all[:, :-1]], axis=1
-    )
-    starts = lax.cummax(jnp.where(edge, index, 0), axis=1)
-    cosine, sine = rotary(index - starts, depth)
-    cosine = jnp.concatenate([cosine, cosine], axis=-1)
-    sine = jnp.concatenate([-sine, sine], axis=-1)
-    fixed_args = (starts[:, :, None], cosine, sine, query_gain[None], key_gain[None])
-
-    token_whole, w_project, w_branch = open_call(tokens, w_query, w_key, w_value, w_out, 0)
-    first, first_scale, projected, mixed, query, keys, values, logs, grad_whole, w_back = front_call(
-        token_whole, w_project, gains[0:1], fixed_args, most, cotangent, w_down, 1
-    )
-    residual, residual_whole, w_both = branch_call(mixed, w_branch, tokens, w_gate, w_up, 2)
+    half = jnp.arange(depth // 2, dtype=F32)
+    rate = THETA ** (-half * 2.0 / depth)
+    rate = jnp.concatenate([rate, rate])[None]
+    gains, starts, cosine, sine, token_whole, w_project, w_branch = open_call(
+        tokens, w_query, w_key, w_value, w_out, jnp.stack([attn_gain, mlp_gain]), seg_ids, rate, 0
+    )
+    fixed_args = (starts, cosine, sine, query_gain[None], key_gain[None])
+    (
+        first,
+        first_scale,
+        projected,
+        mixed,
+        query,
+        keys,
+        values,
+        logs,
+        grad_whole,
+        w_back,
+        gate_quarter,
+    ) = front_call(
+        token_whole, w_project, gains[0:1], fixed_args, most, cotangent, w_down, w_gate, 1
+    )
+    residual, residual_whole, w_uppers, w_gates = branch_call(
+        mixed, w_branch, tokens, w_up, w_gate, gate_quarter, 2
+    )
     flat = (4 * rows, 2 * width)
     grad_flat = grad_whole.reshape(flat)
     second, hidden, unit_grads, second_scale, unit_stats = units_call(
-        residual_whole.reshape(flat), grad_flat, w_both, w_back, gains[1:2]
+        residual_whole.reshape(flat), grad_flat, w_gates, w_uppers, w_back, gains[1:2]
     )
     tiles = lambda grad: grad.reshape(8, -1, grad.shape[1])
     (
         residual_grad,
         mlp_gain_part,
-        branch_whole,
-        down_mine,
-        down_theirs,
-        gate_mine,
-        gate_theirs,
-        up_tiles,
+        upstream,
+        out_tiles,
+        _,
+        rest_tiles,
+        *ends,
     ) = middle_call(
         unit_grads.reshape(4, rows, 2 * units),
-        w_both,
+        w_gates,
+        w_uppers,
         unit_stats,
         second_scale[:rows],
         residual,
@@ -1735,12 +2195,11 @@
         cotangent,
         tiles(product_grad(grad_flat, hidden)),
         second.reshape(4, rows, 2 * width),
+        w_branch,
+        mixed,
         3,
     )
-    branch_flat = branch_whole.reshape(flat)
-    upstream = backward_with(w_branch)(branch_flat).astype(B16).reshape(4, rows, head_width)
-    out_tiles = tiles(product_grad(branch_flat, mixed.reshape(4 * rows, head_width)))
-    output, proj_grads, proj_stats, gain_parts, up_mine, up_theirs = back_call(
+    output, proj_grads, proj_stats, gain_parts, *rest_ends = back_call(
         upstream,
         hidden.reshape(4, rows, units),
         w_back,
@@ -1748,7 +2207,7 @@
         fixed_args,
         projected,
         (query, keys, values, logs),
-        up_tiles,
+        rest_tiles,
         most,
         4,
     )
@@ -1771,20 +2230,26 @@
         first,
         5,
     )
-    whole = lambda mine, theirs: in_order(mine, theirs.astype(F32), 1)
-    attn_sums = totals[:8, :2].reshape(-1) / gains[0]
-    attn_total = in_order(attn_sums[:width], attn_sums[width:], 0)
-    mlp_total = in_order(totals[8].reshape(-1), totals[9].reshape(-1), 0)
+    place = lax.axis_index("ty").reshape(1).astype(jnp.int32)
+    (
+        query_share,
+        key_share,
+        value_share,
+        out_share,
+        gate_share,
+        up_share,
+        down_share,
+        attn_total,
+        mlp_total,
+    ) = finish_call(
+        place,
+        (*ends, *rest_ends, out_mine, out_theirs, project_mine, project_theirs),
+        totals,
+        gains[0].reshape(16, 128),
+        (2 * head_width, 2 * kv_width, 2 * head_width, 2 * units),
+    )
+    attn_total, mlp_total = attn_total.reshape(-1), mlp_total.reshape(-1)
     query_total, key_total = totals[10, 0], totals[10, 1]
-    down_share = whole(down_mine, down_theirs).T
-    out_share = whole(out_mine, out_theirs).T
-    gate_share = whole(gate_mine, gate_theirs)
-    up_share = whole(up_mine, up_theirs)
-    ends = (0, head_width, head_width + kv_width, head_width + 2 * kv_width)
-    query_share, key_share, value_share = (
-        whole(project_mine[:, low:high], project_theirs[:, low:high])
-        for low, high in zip(ends[:-1], ends[1:])
-    )
     return (
         output,
         input_grad,

time: 649 us -> 561 us (0.86)
  Pallas kernels: 580 us -> 530 us
  other arithmetic: 21.9 us -> 3.22 us
  matrix products: 21.8 us -> 11.4 us
    pallas_call x2 -> x3, Pallas kernels: 193 us -> 174 us  [the longest x1 113 us: middle_call(): pl.pallas_call(middle_kernel, out_shape=[shape((height, width), F32), sha...]
    pallas_call x1, Pallas kernels: 98.2 us -> 80 us  [last_call(): pl.pallas_call(last_kernel, out_shape=(shape((height, width)), shape((11,...]
    pallas_call x1, Pallas kernels: 104 us -> 93.3 us  [branch_call(): pl.pallas_call(branch_kernel, out_shape=(shape((height, width), F32), sha...]
    concatenate x9 -> x0, other arithmetic: 7.63 us -> none  [the longest x6 4.99 us: in_order(): jnp.concatenate([jnp.where(first, mine, theirs), jnp.where(first, theirs,...]
    select_n x8 -> x0, other arithmetic: 7.19 us -> none  [the longest x7 7.18 us: in_order(): jnp.where(first, mine, theirs)]
    dot_general x2 -> x1, matrix products: 18.4 us -> 11.4 us  [weight_grad(): lax.dot_general(left, right, (((0,), (0,)), ((), ())), preferred_element_...]
    pallas_call x1, Pallas kernels: 72.8 us -> 66 us  [front_call(): pl.pallas_call(lambda *refs: front_kernel(most, *refs), out_shape=outs, i...]
  transfers between devices with their start and end apart: 2 -> 0, of which waited for: 0 -> 0; matrix products, arithmetic and copies ran while one was open for 2% -> 0% of each run, Pallas kernels for 8% -> 0%
where the time goes in v3:
time: 561 us; the launch traced here: 552 us
  Pallas kernels  530 us (94%)
  matrix products  11.4 us (2%)
  local copies, waits for them, and re-layouts  6.31 us (1%)
    pallas_call x1, Pallas kernels, middle_call(): pl.pallas_call(middle_kernel, out_shape=[shape((height, width), F32), sha...  113 us
    pallas_call x1, Pallas kernels, branch_call(): pl.pallas_call(branch_kernel, out_shape=(shape((height, width), F32), sha...  93.3 us
    pallas_call x1, Pallas kernels, back_call(): pl.pallas_call(lambda *refs: back_kernel(most, *refs), out_shape=(shape((...  85.4 us
    pallas_call x1, Pallas kernels, last_call(): pl.pallas_call(last_kernel, out_shape=(shape((height, width)), shape((11,...  80 us
    pallas_call x1, Pallas kernels, front_call(): pl.pallas_call(lambda *refs: front_kernel(most, *refs), out_shape=outs, i...  66 us
    pallas_call x1, Pallas kernels, open_call(): pl.pallas_call(open_kernel, out_shape=(shape((2, 2 * width), F32), shape(...  54.5 us
    pallas_call x1, Pallas kernels, units_call(): pl.pallas_call(units_kernel, out_shape=(shape((tokens, width)), shape((to...  31.5 us
    dot_general x1, matrix products, weight_grad(): lax.dot_general(left, right, (((0,), (0,)), ((), ())), preferred_element_...  11.4 us

profile of v3, /device:TPU:0, one launch (start us, length us, event | category | flops | bytes accessed | tf_op | source)
XLA Modules:
  0.0 551.9 jit_solution(7200339799285895911)
XLA Ops:
  0.6 1.3 pad_maximum_fusion.gains_ref
  2.0 0.6 maximum_bitcast_fusion.rate_ref
  2.6 54.5 %shard_map.237 = (f32[2,2048]{1,0:T(2,128)}, s32[2,1024,1]{2,1,0:T(8,128)}, f32[2,1024,128]{2,1,0:T(8,128)}, f32[2,1024,128]{2,1,0:T(8,128)}, bf16[4,512,2048]{2...) custom-call(bf16[512,1024]{1,0:T(8,128)(2,1)} %value_in_ref.1, bf16[1024,512]{1,0:T(8,128)(2,1)} %query_ref.1, ...), custom_call_target="tpu_custom_call" | custom-call | bytes 16777216 | tf_op jit(solution)/shard_map/pallas_call | solution.py:1110
  57.1 1.4 fusion
  58.5 66.0 %shard_map.238 = (bf16[4,512,2048]{2,1,0:T(8,128)(2,1)}, f32[512,128]{1,0:T(8,128)}, f32[4,512,512]{2,1,0:T(8,128)}, bf16[4,512,256]{2,1,0:T(8,128)(2,1)}, bf16[...) custom-call(bf16[4,512,2048]{2,1,0:T(8,128)(2,1)} %get-tuple-element, ...), custom_call_target="tpu_custom_call" | custom-call | flops 4294967296 | bytes 33554432 | tf_op jit(solution)/shard_map/pallas_call | solution.py:1281
  124.5 93.3 %shard_map.239 = (f32[512,1024]{1,0:T(8,128)}, bf16[4,512,2048]{2,1,0:T(8,128)(2,1)}, bf16[2048,768]{1,0:T(8,128)(2,1)}, bf16[2048,768]{1,0:T(8,128)(2,1)}) custom-call(bf16[4,512,256]{2,1,0:T(8,128)(2,1)} %get-tuple-element.80.rows_in_ref.mixed_in_ref, bf16[256,2048]{1,0:T(8,128)(2,1)} %get-tuple-element.81.weight_in_ref.branch_in_ref, ...), custom_call_target="tpu_custom_call" | custom-call | flops 2147483648 | bytes 33554432 | tf_op jit(solution)/shard_map/pallas_call | solution.py:1367
  217.8 31.5 %shard_map.240 = (bf16[2048,2048]{1,0:T(8,128)(2,1)}, bf16[2048,768]{1,0:T(8,128)(2,1)}, bf16[2048,1536]{1,0:T(8,128)(2,1)}, f32[2048,128]{1,0:T(8,128)}, f32[8,8,128]{2,1,0:T(8,128)}) custom-call(bf16[2048,2048]{1,0:T(8,128)(2,1)} %bitcast.38, bf16[2048,2048]{1,0:T(8,128)(2,1)} %bitcast.36, bf16[2048,768]{1,0:T(8,128)(2,1)} %get-tuple-element.85.gates_ref.gates_in_ref, ...), custom_call_target="tpu_custom_call" | custom-call | flops 19327352832 | bytes 41943040 | tf_op jit(solution)/shard_map/pallas_call | solution.py:1431
  249.3 11.4 %convolution_convert_fusion = bf16[2048,768]{1,0:T(8,128)(2,1)} fusion(bf16[2048,2048]{1,0:T(8,128)(2,1)} %bitcast.37, bf16[2048,768]{1,0:T(8,128)(2,1)} %get-tuple-element.88), kind=kOutput, calls=%fused_computation | convolution fusion | flops 6444023808 | bytes 14680064 | tf_op jit(solution)/shard_map/dot_general | solution.py:49
  260.7 1.7 slice.21.scale_ref
  262.3 113.3 %shard_map.241 = (f32[512,1024]{1,0:T(8,128)}, f32[1,1024]{1,0:T(1,128)}, bf16[4,512,256]{2,1,0:T(8,128)(2,1)}, bf16[8,256,256]{2,1,0:T(8,128)(2,1)}, bf16[4,512...) custom-call(bf16[4,512,1536]{2,1,0:T(8,128)(2,1)} %bitcast.42, ...), custom_call_target="tpu_custom_call" | custom-call | flops 19327352832 | bytes 33554432 | tf_op jit(solution)/shard_map/pallas_call | solution.py:1721
  375.7 0.0 copy-start.2
  375.7 85.4 %shard_map.242 = (bf16[512,1024]{1,0:T(8,128)(2,1)}, bf16[4,512,512]{2,1,0:T(8,128)(2,1)}, f32[8,8,128]{2,1,0:T(8,128)}, f32[2,8,128]{2,1,0:T(8,128)}, f32[256,5...) custom-call(f32[1,128]{1,0:T(1,128)} %bitcast.33, f32[1,128]{1,0:T(1,128)} %bitcast.35, ...), custom_call_target="tpu_custom_call" | custom-call | flops 6442450944 | bytes 33554432 | tf_op jit(solution)/shard_map/pallas_call | solution.py:2017
  461.1 0.7 slice_reduce_fusion
  461.9 0.0 copy-done.2
  461.9 0.6 pad_maximum_fusion.1.extra_ref
  462.5 80.0 %shard_map.243 = (bf16[512,1024]{1,0:T(8,128)(2,1)}, f32[11,8,128]{2,1,0:T(8,128)}, f32[256,256]{1,0:T(8,128)}, bf16[256,256]{1,0:T(8,128)(2,1)}, f32[256,512]{1,0:T(8,128)}, /*index=5*/bf16[256,512]{1,0:T(8,128)(2,1)}) custom-call(bf16[4,512,512]{2,1,0:T(8,128)(2,1)} %get-tuple-element.102.rows_in_ref, ...), custom_call_target="tpu_custom_call" | custom-call | flops 8589934592 | bytes 33554432 | tf_op jit(solution)/shard_map/pallas_call | solution.py:1885
  542.4 0.0 copy-start
  542.5 0.0 copy-start.1
  542.5 5.8 %shard_map.244 = (f32[256,512]{1,0:T(8,128)}, f32[256,256]{1,0:T(8,128)}, f32[256,256]{1,0:T(8,128)}, f32[512,256]{1,0:T(8,128)}, f32[256,1536]{1,0:T(8,128)}, /...) custom-call(s32[1]{0:T(128)} %bitcast.13.place_ref, ...), custom_call_target="tpu_custom_call" | custom-call | bytes 16777216 | tf_op jit(solution)/shard_map/pallas_call | solution.py:2101
  548.3 1.3 slice_bitcast_fusion
  549.6 0.0 copy-done
  549.6 1.0 copy.29
  550.5 0.0 copy-done.1
  550.5 1.0 copy.30
  (2 shorter events, 0.0 us)
Async XLA Ops:
  375.7 86.2 %copy-start.2 = (f32[1,1024]{1,0:T(1,128)S(1)}, f32[1,1024]{1,0:T(1,128)}, u32[]{:S(2)}) copy-start(f32[1,1024]{1,0:T(1,128)} %get-tuple-element.106) | copy-start | bytes 12292
  542.4 7.1 %copy-start = (bf16[512,1024]{1,0:T(8,128)(2,1)S(1)}, bf16[512,1024]{1,0:T(8,128)(2,1)}, u32[]{:S(2)}) copy-start(bf16[512,1024]{1,0:T(8,128)(2,1)} %get-tuple-element.152) | copy-start | bytes 3145732
  542.5 8.1 %copy-start.1 = (bf16[512,1024]{1,0:T(8,128)(2,1)S(1)}, bf16[512,1024]{1,0:T(8,128)(2,1)}, u32[]{:S(2)}) copy-start(bf16[512,1024]{1,0:T(8,128)(2,1)} %get-tuple-element.153) | copy-start | bytes 3145732

commit v4 on v3

--- a/solution.py
+++ b/solution.py
@@ -503,7 +503,12 @@
 
 def planes():
     plane = lax.axis_index("dp")
-    return {"dp": plane + 1 - 2 * lax.rem(plane, 2)}, {"dp": lax.rem(plane + 2, 4)}
+    return {"dp": plane + 1 - 2 * lax.rem(plane, 2)}, {"dp": 3 - plane}
+
+
+def inner():
+    plane = lax.axis_index("dp")
+    return (plane == 1) | (plane == 2)
 
 
 def greet(targets):
@@ -534,8 +539,8 @@
 REDUCE_KINDS = 5
 OUT_X, OUT_Y, OUT_CORNER, CORE_OWN, CORE_X, CORE_Y, CORE_CORNER = range(7)
 GATHER_KINDS = 7
-SHARE_X, SHARE_Z = 0, 1
-SHARE_KINDS = 2
+SHARE_X, SHARE_NEAR, SHARE_MIDDLE = 0, 1, 2
+SHARE_KINDS = 3
 
 
 def lanes(chunk, half, width):
@@ -666,35 +671,78 @@
             target = self.whole.at[:, : self.whole.shape[1] // 2]
         return pltpu.make_async_copy(part, target, self.local_sems.at[index])
 
-    def over(self, index):
-        near, far = planes()
+    def piece_of(self, owner):
+        place = self.quarter(owner)
+        return place, place
+
+    def over(self, near, index):
+        beside, mirror = planes()
         plane = lax.axis_index("dp")
-        owner = lax.rem(plane + 2, 4) if index == 2 else plane
-        place = self.quarter(owner)
+        other = 3 - plane
+        if near:
+            owner = (plane, other, other + 1 - 2 * lax.rem(other, 2))[index]
+        else:
+            owner = (plane, plane + 1 - 2 * lax.rem(plane, 2))[index]
+        source, target = self.piece_of(owner) if index else self.own_piece()
         return self.wires.copy(
-            self.base + SHARE_Z, index, place, place, far if index == 0 else near
-        )
+            self.base + (SHARE_NEAR if near else SHARE_MIDDLE),
+            index,
+            source,
+            target,
+            beside if near else mirror,
+        )
+
+    def own_piece(self):
+        return self.piece_of(lax.axis_index("dp"))
 
     def start(self):
         for index in range(len(self.sources)):
             self.cross(index).start()
             self.local(index).start()
 
+    def send_own(self):
+        self.over(True, 0).start()
+
+        @pl.when(inner())
+        def _():
+            self.over(False, 0).start()
+
     def middle(self):
         for index in range(len(self.sources)):
             self.cross(index).wait_recv()
-        self.over(0).start()
-        self.over(1).start()
+        self.send_own()
 
     def late(self):
-        self.over(0).wait_recv()
-        self.over(2).start()
+        @pl.when(inner())
+        def _():
+            self.over(True, 0).wait_recv()
+            self.over(False, 1).start()
+            self.over(False, 0).wait_recv()
+            self.over(True, 1).start()
+
+    def later(self):
+        @pl.when(inner())
+        def _():
+            self.over(False, 1).wait_recv()
+            self.over(True, 2).start()
+
+    def close_planes(self):
+        self.over(True, 0).wait_send()
+
+        @pl.when(inner())
+        def _():
+            self.over(True, 1).wait_send()
+            self.over(True, 2).wait_send()
+            self.over(False, 0).wait_send()
+            self.over(False, 1).wait_send()
+
+        @pl.when(jnp.logical_not(inner()))
+        def _():
+            for index in range(3):
+                self.over(True, index).wait_recv()
 
     def close(self):
-        self.over(1).wait_recv()
-        self.over(2).wait_recv()
-        for index in range(3):
-            self.over(index).wait_send()
+        self.close_planes()
         for index in range(len(self.sources)):
             self.cross(index).wait_send()
             self.local(index).wait()
@@ -705,17 +753,8 @@
         super().__init__(wires, base, (source,), whole, True, local_sems)
         self.piece = quarter
 
-    def over(self, index):
-        if index == 2:
-            return super().over(index)
-        near, far = planes()
-        return self.wires.copy(
-            self.base + SHARE_Z,
-            index,
-            self.piece,
-            self.quarter(lax.axis_index("dp")),
-            far if index == 0 else near,
-        )
+    def own_piece(self):
+        return self.piece, self.quarter(lax.axis_index("dp"))
 
     def own(self):
         return pltpu.make_async_copy(
@@ -723,22 +762,26 @@
         )
 
     def start(self):
-        self.over(0).start()
-        self.over(1).start()
+        self.send_own()
         self.local(0).start()
         self.own().start()
 
     def close(self):
-        self.over(1).wait_recv()
-        self.over(2).wait_recv()
-        for index in range(3):
-            self.over(index).wait_send()
+        self.close_planes()
         self.local(0).wait()
         self.own().wait()
 
 
-FOLD_NEAR, FOLD_FAR, FOLD_X = 0, 1, 2
-FOLD_KINDS = 3
+FOLD_END, FOLD_MIDDLE, FOLD_BACK, FOLD_X = 0, 2, 4, 5
+FOLD_KINDS = 6
+
+
+def side():
+    return lax.div(lax.axis_index("dp"), 2)
+
+
+def turn_shard(turn):
+    return 3 * (1 - side()) + turn * (2 * side() - 1)
 
 
 class Fold:
@@ -751,80 +794,132 @@
             theirs,
         )
         self.first = tiles if first is None else first
-        self.near_recv, self.far_recv = bufs
+        (self.recv,) = bufs
+        self.near, self.mirror = planes()
+
+    def send(self, kind, half, slot, source, target, device):
+        target = self.recv.at[2 * target + half]
+        return self.wires.copy(self.base + kind, slot, source, target, device)
+
+    def end(self, half, turn):
+        source = self.first.at[4 * half + turn_shard(turn)]
+        return self.send(FOLD_END + half, half, turn, source, turn, self.near)
+
+    def across(self, half, turn):
+        source = self.recv.at[2 * turn + half]
+        return self.send(FOLD_MIDDLE + half, half, turn, source, 3 + turn, self.mirror)
+
+    def back(self, half):
+        return self.send(FOLD_BACK, half, half, self.recv.at[6 + half], 0, self.near)
+
+    def cross(self):
+        source = self.tiles.at[4 + lax.axis_index("dp")]
+        return self.wires.copy(self.base + FOLD_X, 0, source, self.theirs, neighbours()[0])
+
+    def add(self, slot, half, shard):
+        self.recv[2 * slot + half] = (
+            self.recv[2 * slot + half].astype(F32) + self.tiles[4 * half + shard].astype(F32)
+        ).astype(B16)
+
+    def begin(self, turn, half):
+        @pl.when(jnp.logical_not(inner()))
+        def _():
+            self.end(half, turn).start()
+
+    def start(self):
+        for turn in range(3):
+            for half in (1, 0):
+                self.begin(turn, half)
+
+    def pass_on(self, turn):
+        @pl.when(inner())
+        def _():
+            for half in (1, 0):
+                self.end(half, turn).wait_recv()
+                self.add(turn, half, turn_shard(turn))
+                self.across(half, turn).start()
+
+    def step(self):
+        self.pass_on(0)
+
+    def middle(self):
+        self.pass_on(1)
+
+        @pl.when(inner())
+        def _():
+            for half in (1, 0):
+                self.across(half, 0).wait_recv()
+                self.add(3, half, 3 * side())
+                self.back(half).start()
+
+    def late(self):
         plane = lax.axis_index("dp")
-        self.low = lax.rem(plane, 2)
-        self.high = lax.div(plane, 2)
-
-    def index(self, half, high, low):
-        return half * 4 + 2 * high + low
-
-    def near(self, half, high):
-        source = self.first.at[self.index(half, high, 1 - self.low)]
-        slot = 2 * half + high
-        return self.wires.copy(
-            self.base + FOLD_NEAR, slot, source, self.near_recv.at[slot], planes()[0]
-        )
-
-    def far(self, half):
-        source = self.tiles.at[self.index(half, 1 - self.high, self.low)]
-        return self.wires.copy(
-            self.base + FOLD_FAR, half, source, self.far_recv.at[half], planes()[1]
-        )
-
-    def cross(self):
-        source = self.tiles.at[self.index(1, self.high, self.low)]
-        return self.wires.copy(self.base + FOLD_X, 0, source, self.theirs, neighbours()[0])
-
-    def start(self):
-        for half in range(2):
-            for high in range(2):
-                self.near(half, high).start()
-
-    def add(self, half, high):
-        self.near(half, high).wait_recv()
-        at = self.index(half, high, self.low)
-        came = self.near_recv[2 * half + high].astype(F32)
-        self.tiles[at] = (self.tiles[at].astype(F32) + came).astype(B16)
-
-    def middle(self):
-        @pl.loop(0, 2)
-        def _(turn):
-            half = 1 - turn
-            self.add(half, 1 - self.high)
-            self.far(half).start()
-
-        @pl.loop(0, 2)
-        def _(half):
-            self.add(half, self.high)
-
-    def late(self):
-        at = self.index(1, self.high, self.low)
-        self.far(1).wait_recv()
-        self.tiles[at] = (self.tiles[at].astype(F32) + self.far_recv[1].astype(F32)).astype(B16)
-        self.cross().start()
-        self.far(0).wait_recv()
-        at = self.index(0, self.high, self.low)
-        self.mine[...] = self.tiles[at].astype(F32) + self.far_recv[0].astype(F32)
+        for half in (1, 0):
+
+            @pl.when(inner())
+            def _():
+                self.end(half, 2).wait_recv()
+                self.across(half, 1).wait_recv()
+                self.add(2, half, plane)
+
+            @pl.when(jnp.logical_not(inner()))
+            def _():
+                self.back(half).wait_recv()
+
+            at = 4 * half + plane
+            middle = inner().astype(jnp.int32)
+            total = self.recv[4 * middle + half].astype(F32)
+            other = jnp.where(
+                inner(), self.recv[8 * middle + half].astype(F32), self.tiles[at].astype(F32)
+            )
+            total = total + other
+            if half == 1:
+                self.tiles[at] = total.astype(B16)
+                self.cross().start()
+            else:
+                self.mine[...] = total
 
     def close(self):
         self.cross().wait_recv()
-        for half in range(2):
-            for high in range(2):
-                self.near(half, high).wait_send()
-            self.far(half).wait_send()
+
+        @pl.when(inner())
+        def _():
+            for half in range(2):
+                self.across(half, 0).wait_send()
+                self.across(half, 1).wait_send()
+                self.back(half).wait_send()
+
+        @pl.when(jnp.logical_not(inner()))
+        def _():
+            for half in range(2):
+                for turn in range(3):
+                    self.end(half, turn).wait_send()
+
         self.cross().wait_send()
 
 
 def fold_scratch(rows, columns):
-    return [pltpu.VMEM((4, rows, columns), B16), pltpu.VMEM((2, rows, columns), B16)]
+    return [pltpu.VMEM((10, rows, columns), B16)]
 
 
 def turn_tile(step):
-    low = lax.rem(lax.axis_index("dp"), 2)
-    kept_now = lax.div(step, 4)
-    low = kept_now * low + (1 - kept_now) * (1 - low)
-    return lax.div(lax.rem(step, 4), 2) * 4 + 2 * lax.rem(step, 2) + low
+    return 4 * (1 - lax.rem(step, 2)) + turn_shard(lax.div(step, 2))
+
+
+def make_tiles(fold, make, low, high):
+    @pl.loop(low, high)
+    def _(step):
+        make(step)
+
+        @pl.when(step < 6)
+        def _():
+            half = 1 - lax.rem(step, 2)
+            turn = lax.div(step, 2)
+            for side_half in range(2):
+
+                @pl.when(half == side_half)
+                def _():
+                    fold.begin(turn, side_half)
 
 
 class Reduce:
@@ -1096,6 +1191,8 @@
             shares[0].late()
             shares[1].late()
             gather.relay(0, 2)
+            shares[0].later()
+            shares[1].later()
 
     gather.relay(2)
     gather.close()
@@ -1245,6 +1342,8 @@
             def _():
                 if turn == 0:
                     back.late()
+                elif turn == 2:
+                    back.later()
                 gather.relay(turn, turn + 1)
 
         attend_sequence(
@@ -1341,8 +1440,9 @@
         gate.start()
 
     reduce.start((between, gate.late))
+    up.middle()
     reduce.middle()
-    up.middle()
+    gate.later()
 
     @pl.loop(0, width // CHUNK)
     def _(chunk):
@@ -1354,6 +1454,7 @@
 
     up.late()
     gather.relay()
+    up.later()
     gather.close()
     up.close()
     gate.close()
@@ -1545,21 +1646,16 @@
     rest_ref,
     *refs,
 ):
-    ends, scratch = refs[:6], refs[6:]
+    ends, scratch = refs[:4], refs[4:]
     bufs = scratch[:7]
     stats_ref, stats_recv, column_ref, send_sems, recv_sems, own, gather_sem = scratch[7:14]
     stream, stream_sem, down_sem, stage, stage_sem, upstream = scratch[14:20]
-    tiles = scratch[20:29]
-    weight_ref, rows_ref, value_ref, base_ref, branch_ref, mixed_ref = scratch[29:35]
-    load_sem = scratch[35]
+    down_tiles, down_recv, made_tiles, made_recv = scratch[20:24]
+    weight_ref, rows_ref, value_ref, base_ref, branch_ref, mixed_ref = scratch[24:30]
+    load_sem = scratch[30]
     rows, width = value_ref.shape
     columns = rows_ref.shape[2]
-    half = tiles[0].shape[2]
-    parts = [down_in_ref.at[:, :, index * half : (index + 1) * half] for index in range(2)]
-    downs = [
-        pltpu.make_async_copy(parts[index], tiles[3 * index], down_sem.at[index])
-        for index in range(2)
-    ]
+    load = pltpu.make_async_copy(down_in_ref, down_tiles, down_sem)
     units = gates_in_ref.shape[1]
     loads = Loads(
         (
@@ -1590,33 +1686,22 @@
         )
 
     loads.start()
-    for load in downs:
-        load.start()
+    load.start()
     fetch(second_ref, 0, turn_tile(0)).start()
     stats_ref[...] = stats_in_ref[...]
     greet(neighbours() + planes())
     wires = Wires(send_sems, recv_sems)
     base = REDUCE_KINDS + 1 + GATHER_KINDS
-    folds = [
-        Fold(
-            wires,
-            base + index * FOLD_KINDS,
-            tiles[3 * index],
-            tiles[3 * index + 1 : 3 * index + 3],
-            ends[2 * index],
-            ends[2 * index + 1],
-            parts[index] if index < 2 else None,
-        )
-        for index in range(3)
-    ]
+    down = Fold(wires, base, down_tiles, (down_recv,), ends[0], ends[1], down_in_ref)
+    made = Fold(wires, base + FOLD_KINDS, made_tiles, (made_recv,), ends[2], ends[3])
     stats = Stats(wires, REDUCE_KINDS, stats_ref, stats_recv)
-    folds[0].start()
-    folds[1].start()
+    down.start()
     stats.start(0)
     reduce = Reduce(wires, rows_ref, weight_ref, True, bufs)
     loads.wait(0, 3)
     reduce.start((lambda: stats.step(0), lambda: stats.step(1)))
-    made = folds[2]
+    load.wait()
+    down.step()
 
     def store(step):
         slot = lax.rem(step, 2)
@@ -1646,23 +1731,12 @@
             ).astype(B16)
         store(step).start()
 
-    @pl.loop(0, 4)
-    def _(step):
-        make(step)
-        made.near(lax.div(step, 2), lax.rem(step, 2)).start()
-
+    make_tiles(made, make, 0, 4)
     reduce.middle()
     stats.finish(2)
     pull_columns(stats_ref, scale_ref, column_ref, width)
-
-    @pl.loop(4, 8)
-    def _(step):
-        make(step)
-
-    for load in downs:
-        load.wait()
-    folds[0].middle()
-    folds[1].middle()
+    down.middle()
+    make_tiles(made, make, 4, 8)
     loads.wait(3, 7)
     gather = Gather(wires, REDUCE_KINDS + 1, whole_ref, own, gather_sem)
 
@@ -1678,12 +1752,13 @@
 
     for step in (6, 7):
         store(step).wait()
-    folds[2].middle()
-    gather.relay()
-    folds[0].late()
-    folds[1].late()
+    down.late()
+    gather.relay(0, 2)
+    made.step()
+    gather.relay(2)
+    made.middle()
     gather.close()
-    folds[2].late()
+    made.late()
     fetch(whole_ref, 0, 0).start()
     upstream[...] = jnp.zeros_like(upstream)
 
@@ -1699,8 +1774,8 @@
         out_ref[tile] = weight_grad(left, mixed_ref[...].reshape(4 * rows, -1)).astype(B16)
 
     upstream_ref[...] = upstream[...].astype(B16).reshape(upstream_ref.shape)
-    for fold in folds:
-        fold.close()
+    down.close()
+    made.close()
     reduce.close()
 
 
@@ -1712,7 +1787,7 @@
     columns = rows.shape[2]
     quarter, units = down.shape[1:]
     heads = mixed.shape[2]
-    sizes = (units // 2, units // 2, SPLIT)
+    sizes = (units, SPLIT)
     ends, tiles = [], []
     for size in sizes:
         ends += [shape((quarter, size), F32), shape((quarter, size))]
@@ -1730,19 +1805,19 @@
         ]
         + ends,
         in_specs=[IN_ANY] * 7 + [IN_VMEM] * 3 + [IN_ANY] * 2,
-        out_specs=[IN_VMEM] * 4 + [IN_ANY] * 2 + [IN_VMEM, IN_ANY] * 3,
+        out_specs=[IN_VMEM] * 4 + [IN_ANY] * 2 + [IN_VMEM, IN_ANY] * 2,
         scratch_shapes=reduce_scratch(height, width)
         + [
             pltpu.VMEM((8, 8, 128), F32),
             pltpu.VMEM((8, 8, 128), F32),
             pltpu.VMEM((height, 128), F32),
         ]
-        + wire_scratch(REDUCE_KINDS + 1 + GATHER_KINDS + 3 * FOLD_KINDS, count)
+        + wire_scratch(REDUCE_KINDS + 1 + GATHER_KINDS + 2 * FOLD_KINDS, count)
         + gather_scratch(height, width)
         + [
             pltpu.VMEM((2, 4, height, BLOCK), B16),
             pltpu.SemaphoreType.DMA((2,)),
-            pltpu.SemaphoreType.DMA((2,)),
+            pltpu.SemaphoreType.DMA,
             pltpu.VMEM((2, quarter, columns - SPLIT), B16),
             pltpu.SemaphoreType.DMA((2,)),
             pltpu.VMEM((4 * height, heads), F32),
@@ -1778,8 +1853,8 @@
     bufs = scratch[:7]
     stats_ref, stats_recv, column_ref, send_sems, recv_sems = scratch[7:12]
     out_ref, project_ref, whole, sums_ref, sums_recv, load_sem = scratch[12:18]
-    out_bufs, project_bufs = scratch[18:20], scratch[20:22]
-    rows_ref, weight_ref, value_ref, base_ref = scratch[22:26]
+    out_bufs, project_bufs = scratch[18:19], scratch[19:20]
+    rows_ref, weight_ref, value_ref, base_ref = scratch[20:24]
     rows, width = value_ref.shape
     loads = Loads(
         (rows_in_ref, weight_in_ref, first_ref, value_in_ref, base_in_ref, out_in_ref),
@@ -1830,22 +1905,15 @@
     reduce = Reduce(wires, rows_ref, weight_ref, True, bufs)
     reduce.start((lambda: stats.step(0), lambda: stats.step(1)))
     loads.wait(2, 3)
-
-    @pl.loop(0, 4)
-    def _(step):
-        make(step)
-        project.near(lax.div(step, 2), lax.rem(step, 2)).start()
-
-    @pl.loop(4, 8)
-    def _(step):
-        make(step)
-
+    make_tiles(project, make, 0, 8)
     hops[0]().start()
     loads.wait(3, 6)
+    out.step()
     add(0)
     hops[1]().start()
     reduce.middle()
     out.middle()
+    project.step()
     stats.finish(2)
     pull_columns(stats_ref, scale_ref, column_ref, width)
     add(1)
@@ -1926,46 +1994,28 @@
     operands, refs = refs[:12], refs[12:]
     rest_ref, refs = refs[0], refs[1:]
     output_ref, result_ref, stats_ref, gains_ref = refs[:4]
-    ends, scratch = refs[4:8], refs[8:]
+    ends, scratch = refs[4:6], refs[6:]
     bufs = scratch[:7]
     query_acc, key_acc, value_acc, send_sems, recv_sems, rest_sem = scratch[7:13]
-    tiles = scratch[13:19]
-    held, load_sem = scratch[19:31], scratch[31]
+    tiles, fold_recv = scratch[13:15]
+    held, load_sem = scratch[15:27], scratch[27]
     hidden_ref, down_ref, upstream, starts_ref, cosine_ref, sine_ref = held[:6]
     projected_ref, query_ref, key_ref, value_ref, log_ref, residual_ref = held[6:]
     attend_loads = Loads(operands, held, load_sem)
     attend_loads.start()
     width = residual_ref.shape[1]
     core = lax.rem(lax.axis_index("tx"), 2)
-    parts = [rest_ref.at[:, :, index * SPLIT : (index + 1) * SPLIT] for index in range(2)]
-    loads = [
-        pltpu.make_async_copy(parts[index], tiles[3 * index], rest_sem.at[index])
-        for index in range(2)
-    ]
-    for load in loads:
-        load.start()
+    load = pltpu.make_async_copy(rest_ref, tiles, rest_sem)
+    load.start()
     greet(neighbours() + planes())
     wires = Wires(send_sems, recv_sems)
-    folds = [
-        Fold(
-            wires,
-            REDUCE_KINDS + index * FOLD_KINDS,
-            tiles[3 * index],
-            tiles[3 * index + 1 : 3 * index + 3],
-            ends[2 * index],
-            ends[2 * index + 1],
-            parts[index],
-        )
-        for index in range(2)
-    ]
-    for fold in folds:
-        fold.start()
+    fold = Fold(wires, REDUCE_KINDS, tiles, (fold_recv,), ends[0], ends[1], rest_ref)
+    fold.start()
     reduce = Reduce(wires, hidden_ref, down_ref, False, bufs)
     attend_loads.wait(0, 2)
     reduce.start()
     attend_loads.wait(2, 12)
-    for load in loads:
-        load.wait()
+    load.wait()
     stats_ref[...] = jnp.zeros_like(stats_ref)
     fixed_refs = (starts_ref, cosine_ref, sine_ref, query_gain_ref, key_gain_ref)
     saved_refs = (query_ref, key_ref, value_ref, log_ref)
@@ -1989,7 +2039,9 @@
         @pl.when(seq == 0)
         def _():
             reduce.middle()
-            folds[0].middle()
+            fold.step()
+
+    fold.middle()
 
 
     @pl.loop(0, width // CHUNK)
@@ -1997,11 +2049,8 @@
         at = lanes(chunk, 0, width)
         output_ref[:, at] = (residual_ref[:, at] + reduce.total(chunk)).astype(B16)
 
-    folds[1].middle()
-    folds[0].late()
-    folds[1].late()
-    for fold in folds:
-        fold.close()
+    fold.late()
+    fold.close()
     reduce.close()
 
 
@@ -2012,7 +2061,7 @@
     length = cosine.shape[1]
     columns = projected.shape[2]
     heads = columns // depth - 2
-    quarter = rest.shape[1]
+    quarter, columns_left = rest.shape[1:]
     loaded = (hidden, w_back, upstream) + fixed_args[:3] + (projected,) + saved + (residual,)
     return pl.pallas_call(
         lambda *refs: back_kernel(most, *refs),
@@ -2022,18 +2071,18 @@
             shape((8, 8, 128), F32),
             shape((2, 8, depth), F32),
         )
-        + (shape((quarter, SPLIT), F32), shape((quarter, SPLIT))) * 2,
+        + (shape((quarter, columns_left), F32), shape((quarter, columns_left))),
         in_specs=[IN_VMEM] * 2 + [IN_ANY] * 13,
-        out_specs=[IN_VMEM] * 4 + [IN_VMEM, IN_ANY] * 2,
+        out_specs=[IN_VMEM] * 5 + [IN_ANY],
         scratch_shapes=reduce_scratch(height, width)
         + [
             pltpu.VMEM((length, heads * depth), F32),
             pltpu.VMEM((length, depth), F32),
             pltpu.VMEM((length, depth), F32),
         ]
-        + wire_scratch(REDUCE_KINDS + 2 * FOLD_KINDS, width // CHUNK)
-        + [pltpu.SemaphoreType.DMA((2,))]
-        + ([pltpu.VMEM((8, quarter, SPLIT), B16)] + fold_scratch(quarter, SPLIT)) * 2
+        + wire_scratch(REDUCE_KINDS + FOLD_KINDS, width // CHUNK)
+        + [pltpu.SemaphoreType.DMA, pltpu.VMEM(rest.shape, B16)]
+        + fold_scratch(quarter, columns_left)
         + load_scratch(loaded),
         compiler_params=remote_params(number),
         cost_estimate=cost(16 * height * hidden.shape[2] * width, 64 * height * width),
@@ -2041,10 +2090,10 @@
 
 
 def finish_kernel(place_ref, *refs):
-    downs, both, out, project = refs[0:4], refs[4:10], refs[10:12], refs[12:14]
-    totals_ref, gain_ref = refs[14:16]
-    query_ref, key_ref, value_ref, out_ref, gate_ref, up_ref, down_ref = refs[16:23]
-    attn_ref, mlp_ref = refs[23:]
+    downs, both, out, project = refs[0:2], refs[2:6], refs[6:8], refs[8:10]
+    totals_ref, gain_ref = refs[10:12]
+    query_ref, key_ref, value_ref, out_ref, gate_ref, up_ref, down_ref = refs[12:19]
+    attn_ref, mlp_ref = refs[19:]
     first = place_ref[0] == 0
 
     def ordered(mine, theirs):
@@ -2063,10 +2112,7 @@
         target[at : at + mine.shape[1], :] = low.T
         target[half + at : half + at + mine.shape[1], :] = high.T
 
-    at = 0
-    for index in (0, 2):
-        put_turned(down_ref, at, downs[index][...], downs[index + 1][...])
-        at += downs[index].shape[1]
+    put_turned(down_ref, 0, downs[0][...], downs[1][...])
     put_turned(out_ref, 0, out[0][...], out[1][...])
     at = 0
     for target in (query_ref, key_ref, value_ref):
@@ -2075,7 +2121,7 @@
         at += size
     units = gate_ref.shape[1] // 2
     at = 0
-    for index in (0, 2, 4):
+    for index in (0, 2):
         low = 0
         while low < both[index].shape[1]:
             size = min(both[index].shape[1] - low, units - at % units)

time: 561 us -> 538 us (0.959)
  the two profiles are of different devices: /device:TPU:0 before, /device:TPU:10 now
where the time goes in v4:
time: 538 us; the launch traced here: 529 us
  Pallas kernels  507 us (94%)
  matrix products  11.4 us (2%)
  local copies, waits for them, and re-layouts  6.3 us (1%)
    pallas_call x1, Pallas kernels, middle_call(): pl.pallas_call(middle_kernel, out_shape=[shape((height, width), F32), sha...  113 us
    pallas_call x1, Pallas kernels, branch_call(): pl.pallas_call(branch_kernel, out_shape=(shape((height, width), F32), sha...  92.2 us
    pallas_call x1, Pallas kernels, back_call(): pl.pallas_call(lambda *refs: back_kernel(most, *refs), out_shape=(shape((...  79.8 us
    pallas_call x1, Pallas kernels, last_call(): pl.pallas_call(last_kernel, out_shape=(shape((height, width)), shape((11,...  71.8 us
    pallas_call x1, Pallas kernels, front_call(): pl.pallas_call(lambda *refs: front_kernel(most, *refs), out_shape=outs, i...  63.2 us
    pallas_call x1, Pallas kernels, open_call(): pl.pallas_call(open_kernel, out_shape=(shape((2, 2 * width), F32), shape(...  49.5 us
    pallas_call x1, Pallas kernels, units_call(): pl.pallas_call(units_kernel, out_shape=(shape((tokens, width)), shape((to...  31.1 us
    dot_general x1, matrix products, weight_grad(): lax.dot_general(left, right, (((0,), (0,)), ((), ())), preferred_element_...  11.4 us

profile of v4, /device:TPU:10, one launch (start us, length us, event | category | flops | bytes accessed | tf_op | source)
XLA Modules:
  0.0 528.9 jit_solution(3028199078771409002)
XLA Ops:
  0.6 1.3 pad_maximum_fusion.gains_ref
  2.0 0.6 maximum_bitcast_fusion.rate_ref
  2.6 49.5 %shard_map.237 = (f32[2,2048]{1,0:T(2,128)}, s32[2,1024,1]{2,1,0:T(8,128)}, f32[2,1024,128]{2,1,0:T(8,128)}, f32[2,1024,128]{2,1,0:T(8,128)}, bf16[4,512,2048]{2...) custom-call(bf16[512,1024]{1,0:T(8,128)(2,1)} %value_in_ref.1, bf16[1024,512]{1,0:T(8,128)(2,1)} %query_ref.1, ...), custom_call_target="tpu_custom_call" | custom-call | bytes 16777216 | tf_op jit(solution)/shard_map/pallas_call | solution.py:1207
  52.0 1.4 fusion
  53.5 63.2 %shard_map.238 = (bf16[4,512,2048]{2,1,0:T(8,128)(2,1)}, f32[512,128]{1,0:T(8,128)}, f32[4,512,512]{2,1,0:T(8,128)}, bf16[4,512,256]{2,1,0:T(8,128)(2,1)}, bf16[...) custom-call(bf16[4,512,2048]{2,1,0:T(8,128)(2,1)} %get-tuple-element, ...), custom_call_target="tpu_custom_call" | custom-call | flops 4294967296 | bytes 33554432 | tf_op jit(solution)/shard_map/pallas_call | solution.py:1380
  116.7 92.2 %shard_map.239 = (f32[512,1024]{1,0:T(8,128)}, bf16[4,512,2048]{2,1,0:T(8,128)(2,1)}, bf16[2048,768]{1,0:T(8,128)(2,1)}, bf16[2048,768]{1,0:T(8,128)(2,1)}) custom-call(bf16[4,512,256]{2,1,0:T(8,128)(2,1)} %get-tuple-element.76.rows_in_ref.mixed_in_ref, bf16[256,2048]{1,0:T(8,128)(2,1)} %get-tuple-element.77.weight_in_ref.branch_in_ref, ...), custom_call_target="tpu_custom_call" | custom-call | flops 2147483648 | bytes 33554432 | tf_op jit(solution)/shard_map/pallas_call | solution.py:1468
  208.9 31.1 %shard_map.240 = (bf16[2048,2048]{1,0:T(8,128)(2,1)}, bf16[2048,768]{1,0:T(8,128)(2,1)}, bf16[2048,1536]{1,0:T(8,128)(2,1)}, f32[2048,128]{1,0:T(8,128)}, f32[8,8,128]{2,1,0:T(8,128)}) custom-call(bf16[2048,2048]{1,0:T(8,128)(2,1)} %bitcast.38, bf16[2048,2048]{1,0:T(8,128)(2,1)} %bitcast.36, bf16[2048,768]{1,0:T(8,128)(2,1)} %get-tuple-element.81.gates_ref.gates_in_ref, ...), custom_call_target="tpu_custom_call" | custom-call | flops 19327352832 | bytes 41943040 | tf_op jit(solution)/shard_map/pallas_call | solution.py:1532
  240.0 11.4 %convolution_convert_fusion = bf16[2048,768]{1,0:T(8,128)(2,1)} fusion(bf16[2048,2048]{1,0:T(8,128)(2,1)} %bitcast.37, bf16[2048,768]{1,0:T(8,128)(2,1)} %get-tuple-element.84), kind=kOutput, calls=%fused_computation | convolution fusion | flops 6444023808 | bytes 14680064 | tf_op jit(solution)/shard_map/dot_general | solution.py:49
  251.3 1.7 slice.21.scale_ref
  253.0 113.4 %shard_map.241 = (f32[512,1024]{1,0:T(8,128)}, f32[1,1024]{1,0:T(1,128)}, bf16[4,512,256]{2,1,0:T(8,128)(2,1)}, bf16[8,256,256]{2,1,0:T(8,128)(2,1)}, bf16[4,512...) custom-call(bf16[4,512,1536]{2,1,0:T(8,128)(2,1)} %bitcast.42, ...), custom_call_target="tpu_custom_call" | custom-call | flops 19327352832 | bytes 33554432 | tf_op jit(solution)/shard_map/pallas_call | solution.py:1796
  366.5 0.0 copy-start.2
  366.5 79.8 %shard_map.242 = (bf16[512,1024]{1,0:T(8,128)(2,1)}, bf16[4,512,512]{2,1,0:T(8,128)(2,1)}, f32[8,8,128]{2,1,0:T(8,128)}, f32[2,8,128]{2,1,0:T(8,128)}, f32[256,1024]{1,0:T(8,128)}, /*index=5*/bf16[256,1024]{1,0:T(8,128)(2,1)}) custom-call(f32[1,128]{1,0:T(1,128)} %bitcast.33, f32[1,128]{1,0:T(1,128)} %bitcast.35, bf16[4,512,768]{2,1,0:T(8,128)(2,1)} %bitcast.25, ...), custom_call_target="tpu_custom_call" | custom-call | flops 6442450944 | bytes 33554432 | tf_op jit(solution)/shard_map/pallas_call | solution.py:2066
  446.3 0.7 slice_reduce_fusion
  447.0 0.0 copy-done.2
  447.0 0.6 pad_maximum_fusion.1.extra_ref
  447.6 71.8 %shard_map.243 = (bf16[512,1024]{1,0:T(8,128)(2,1)}, f32[11,8,128]{2,1,0:T(8,128)}, f32[256,256]{1,0:T(8,128)}, bf16[256,256]{1,0:T(8,128)(2,1)}, f32[256,512]{1,0:T(8,128)}, /*index=5*/bf16[256,512]{1,0:T(8,128)(2,1)}) custom-call(bf16[4,512,512]{2,1,0:T(8,128)(2,1)} %get-tuple-element.98.rows_in_ref, ...), custom_call_target="tpu_custom_call" | custom-call | flops 8589934592 | bytes 33554432 | tf_op jit(solution)/shard_map/pallas_call | solution.py:1953
  519.5 0.0 copy-start
  519.5 0.0 copy-start.1
  519.5 5.7 %shard_map.244 = (f32[256,512]{1,0:T(8,128)}, f32[256,256]{1,0:T(8,128)}, f32[256,256]{1,0:T(8,128)}, f32[512,256]{1,0:T(8,128)}, f32[256,1536]{1,0:T(8,128)}, /...) custom-call(s32[1]{0:T(128)} %bitcast.13.place_ref, ...), custom_call_target="tpu_custom_call" | custom-call | bytes 16777216 | tf_op jit(solution)/shard_map/pallas_call | solution.py:2147
  525.2 1.3 slice_bitcast_fusion
  526.5 0.0 copy-done
  526.5 1.0 copy.29
  527.5 0.0 copy-done.1
  527.5 1.0 copy.30
  (2 shorter events, 0.0 us)
Async XLA Ops:
  366.5 80.6 %copy-start.2 = (f32[1,1024]{1,0:T(1,128)S(1)}, f32[1,1024]{1,0:T(1,128)}, u32[]{:S(2)}) copy-start(f32[1,1024]{1,0:T(1,128)} %get-tuple-element.102) | copy-start | bytes 12292
  519.5 7.0 %copy-start = (bf16[512,1024]{1,0:T(8,128)(2,1)S(1)}, bf16[512,1024]{1,0:T(8,128)(2,1)}, u32[]{:S(2)}) copy-start(bf16[512,1024]{1,0:T(8,128)(2,1)} %get-tuple-element.144) | copy-start | bytes 3145732
  519.5 8.0 %copy-start.1 = (bf16[512,1024]{1,0:T(8,128)(2,1)S(1)}, bf16[512,1024]{1,0:T(8,128)(2,1)}, u32[]{:S(2)}) copy-start(bf16[512,1024]{1,0:T(8,128)(2,1)} %get-tuple-element.145) | copy-start | bytes 3145732

commit v5 on v4

--- a/solution.py
+++ b/solution.py
@@ -1018,6 +1018,9 @@
 
     def start(self, between=(lambda: None, lambda: None)):
         self.give(0)
+        self.rest(between)
+
+    def rest(self, between):
         self.take(0)
         self.give(1)
         self.take(1)
@@ -1121,10 +1124,12 @@
     key_ref,
     value_ref,
     out_ref,
-    gains_ref,
+    attn_ref,
+    mlp_ref,
     seg_ref,
     rate_ref,
-    gains_all_ref,
+    attn_all_ref,
+    mlp_all_ref,
     starts_ref,
     cosine_ref,
     sine_ref,
@@ -1134,8 +1139,8 @@
     *scratch,
 ):
     own, gather_sem, send_sems, recv_sems, project_sem, branch_sem = scratch[:6]
-    gains_recv, seg_recv, seg_all = scratch[6:]
-    width = gains_ref.shape[1]
+    attn_recv, mlp_recv, seg_recv, seg_all = scratch[6:]
+    width = attn_ref.shape[1]
     length = seg_ref.shape[1]
     cut(own, tokens_ref)
     greet(neighbours() + planes())
@@ -1143,14 +1148,18 @@
     gather = Gather(wires, 0, whole_ref, own, gather_sem, 2)
     base = GATHER_KINDS + 2 * SHARE_KINDS
     side = neighbours()[0]
-    gains = wires.copy(base, 0, gains_ref, gains_recv, side)
-    segs = wires.copy(base, 1, seg_ref, seg_recv, side)
+    small = [
+        wires.copy(base, index, source, target, side)
+        for index, (source, target) in enumerate(
+            ((attn_ref, attn_recv), (mlp_ref, mlp_recv), (seg_ref, seg_recv))
+        )
+    ]
     shares = [
         Share(wires, GATHER_KINDS, (query_ref, key_ref, value_ref), project_ref, True, project_sem),
         Share(wires, GATHER_KINDS + SHARE_KINDS, (out_ref,), branch_ref, False, branch_sem),
     ]
-    gains.start()
-    segs.start()
+    for copy in small:
+        copy.start()
     shares[0].start()
     shares[1].start()
 
@@ -1158,10 +1167,12 @@
     def _(chunk):
         gather.send(chunk)
 
-    gains.wait()
-    segs.wait()
-    gains_all_ref[:, :width] = gains_ref[...]
-    gains_all_ref[:, width:] = gains_recv[...]
+    for copy in small:
+        copy.wait()
+    attn_all_ref[:, :width] = attn_ref[...]
+    attn_all_ref[:, width:] = attn_recv[...]
+    mlp_all_ref[:, :width] = mlp_ref[...]
+    mlp_all_ref[:, width:] = mlp_recv[...]
     mine = lax.rem(lax.axis_index("ty") + lax.div(lax.axis_index("tx"), 2), 2)
     seg_all[pl.ds(mine, 1)] = seg_ref[...].astype(F32)[None]
     seg_all[pl.ds(1 - mine, 1)] = seg_recv[...].astype(F32)[None]
@@ -1200,14 +1211,15 @@
     shares[1].close()
 
 
-def open_call(tokens, w_query, w_key, w_value, w_out, gains, seg_ids, rate, number):
+def open_call(tokens, w_query, w_key, w_value, w_out, attn_gain, mlp_gain, seg_ids, rate, number):
     rows, width = tokens.shape
     columns = (w_query.shape[1] + w_key.shape[1] + w_value.shape[1]) // 2
     length = seg_ids.shape[1]
     return pl.pallas_call(
         open_kernel,
         out_shape=(
-            shape((2, 2 * width), F32),
+            shape((1, 2 * width), F32),
+            shape((1, 2 * width), F32),
             shape((2, length, 1), jnp.int32),
             shape((2, length, 128), F32),
             shape((2, length, 128), F32),
@@ -1215,20 +1227,21 @@
             shape((2 * width, columns)),
             shape((w_out.shape[0] // 2, 2 * width)),
         ),
-        in_specs=[IN_VMEM] * 8,
-        out_specs=(IN_VMEM,) * 4 + (IN_ANY,) * 3,
+        in_specs=[IN_VMEM] * 9,
+        out_specs=(IN_VMEM,) * 5 + (IN_ANY,) * 3,
         scratch_shapes=gather_scratch(rows, width)
         + wire_scratch(GATHER_KINDS + 2 * SHARE_KINDS + 1, width // CHUNK)
         + [
             pltpu.SemaphoreType.DMA((3,)),
             pltpu.SemaphoreType.DMA((1,)),
-            pltpu.VMEM((2, width), F32),
+            pltpu.VMEM((1, width), F32),
+            pltpu.VMEM((1, width), F32),
             pltpu.VMEM((1, length), jnp.int32),
             pltpu.VMEM((2, 1, length), F32),
         ],
         compiler_params=remote_params(number),
         cost_estimate=cost(0, 32 * rows * width),
-    )(tokens, w_query, w_key, w_value, w_out, gains, seg_ids, rate)
+    )(tokens, w_query, w_key, w_value, w_out, attn_gain, mlp_gain, seg_ids, rate)
 
 
 def front_kernel(
@@ -1236,13 +1249,13 @@
     whole_ref,
     project_ref,
     gain_ref,
-    starts_ref,
-    cosine_ref,
-    sine_ref,
     query_gain_ref,
     key_gain_ref,
     grad_ref,
-    down_ref,
+    starts_in_ref,
+    cosine_in_ref,
+    sine_in_ref,
+    down_in_ref,
     gate_in_ref,
     first_ref,
     scale_ref,
@@ -1257,7 +1270,11 @@
     gate_ref,
     *scratch,
 ):
-    own, gather_sem, send_sems, recv_sems, back_sem, tokens, firsts, tile_sem = scratch
+    own, gather_sem, send_sems, recv_sems, back_sem, tokens, firsts, tile_sem = scratch[:8]
+    down_ref, starts_ref, cosine_ref, sine_ref = scratch[8:12]
+    loads = Loads(
+        (down_in_ref, starts_in_ref, cosine_in_ref, sine_in_ref), scratch[8:12], scratch[12]
+    )
     core = lax.rem(lax.axis_index("tx"), 2)
     cut(own, grad_ref)
     rows = whole_ref.shape[1]
@@ -1275,10 +1292,11 @@
         return pltpu.make_async_copy(firsts.at[slot], spot(first_ref, tile), tile_sem.at[1, slot])
 
     fetch(0).start()
+    loads.start()
     greet(neighbours() + planes())
     wires = Wires(send_sems, recv_sems)
     gather = Gather(wires, 0, grad_whole_ref, own, gather_sem, 0)
-    back = Share(wires, GATHER_KINDS, (down_ref,), back_ref, False, back_sem)
+    back = Share(wires, GATHER_KINDS, (down_in_ref,), back_ref, False, back_sem, (down_ref,))
     size, columns = gate_ref.shape
     gate = wires.copy(
         GATHER_KINDS + SHARE_KINDS,
@@ -1290,13 +1308,15 @@
         gate_ref,
         neighbours()[0],
     )
-    back.start()
+    back.cross(0).start()
     gate.start()
 
     @pl.loop(0, gather.count)
     def _(chunk):
         gather.send(chunk)
 
+    loads.wait(0, 1)
+    back.local(0).start()
     count = 4 * rows // BLOCK
 
     @pl.loop(0, count)
@@ -1332,6 +1352,7 @@
         def _():
             back.middle()
 
+    loads.wait(1, 4)
     fixed_refs = (starts_ref, cosine_ref, sine_ref, query_gain_ref, key_gain_ref)
     saved_refs = (query_ref, key_ref, value_ref, log_ref)
 
@@ -1380,7 +1401,7 @@
     return pl.pallas_call(
         lambda *refs: front_kernel(most, *refs),
         out_shape=outs,
-        in_specs=[IN_ANY] + [IN_VMEM] * 10,
+        in_specs=[IN_ANY] + [IN_VMEM] * 5 + [IN_ANY] * 5,
         out_specs=[IN_ANY] + [IN_VMEM] * 7 + [IN_ANY] * 3,
         scratch_shapes=gather_scratch(rows, width)
         + wire_scratch(GATHER_KINDS + SHARE_KINDS + 1, width // CHUNK)
@@ -1389,10 +1410,11 @@
             pltpu.VMEM((2, BLOCK, 2 * width), B16),
             pltpu.VMEM((2, BLOCK, 2 * width), B16),
             pltpu.SemaphoreType.DMA((2, 2)),
-        ],
+        ]
+        + load_scratch((w_down, starts, cosine, sine)),
         compiler_params=remote_params(number),
         cost_estimate=cost(16 * rows * width * columns, 64 * rows * width),
-    )(whole, w_project, gain, *fixed_args, cotangent, w_down, w_gate)
+    )(whole, w_project, gain, query_gain, key_gain, cotangent, starts, cosine, sine, w_down, w_gate)
 
 
 def branch_kernel(
@@ -1631,17 +1653,14 @@
     uppers_in_ref,
     value_in_ref,
     base_in_ref,
-    branch_in_ref,
-    mixed_in_ref,
+    hidden_in_ref,
+    scale_in_ref,
     stats_in_ref,
-    scale_ref,
     gain_ref,
-    down_in_ref,
+    grad_ref,
     second_ref,
     result_ref,
     gain_grad_ref,
-    upstream_ref,
-    out_ref,
     whole_ref,
     rest_ref,
     *refs,
@@ -1649,32 +1668,31 @@
     ends, scratch = refs[:4], refs[4:]
     bufs = scratch[:7]
     stats_ref, stats_recv, column_ref, send_sems, recv_sems, own, gather_sem = scratch[7:14]
-    stream, stream_sem, down_sem, stage, stage_sem, upstream = scratch[14:20]
-    down_tiles, down_recv, made_tiles, made_recv = scratch[20:24]
-    weight_ref, rows_ref, value_ref, base_ref, branch_ref, mixed_ref = scratch[24:30]
-    load_sem = scratch[30]
+    stream, stream_sem, stage, stage_sem = scratch[14:18]
+    down_tiles, down_recv, made_tiles, made_recv = scratch[18:22]
+    weight_ref, hidden_ref, rows_ref, value_ref, base_ref, scale_ref = scratch[22:28]
+    load_sem = scratch[28]
     rows, width = value_ref.shape
     columns = rows_ref.shape[2]
-    load = pltpu.make_async_copy(down_in_ref, down_tiles, down_sem)
     units = gates_in_ref.shape[1]
     loads = Loads(
         (
+            hidden_in_ref,
             rows_in_ref,
             gates_in_ref,
             uppers_in_ref,
+            scale_in_ref.at[pl.ds(0, rows)],
             value_in_ref,
             base_in_ref,
-            branch_in_ref,
-            mixed_in_ref,
         ),
         (
+            hidden_ref,
             rows_ref,
             weight_ref.at[:, :units],
             weight_ref.at[:, units:],
+            scale_ref,
             value_ref,
             base_ref,
-            branch_ref,
-            mixed_ref,
         ),
         load_sem,
     )
@@ -1685,22 +1703,42 @@
             ref.at[:, :, tile_columns(tile)], stream.at[slot], stream_sem.at[slot]
         )
 
+    fetch(grad_ref, 0, turn_tile(0)).start()
     loads.start()
-    load.start()
-    fetch(second_ref, 0, turn_tile(0)).start()
     stats_ref[...] = stats_in_ref[...]
     greet(neighbours() + planes())
     wires = Wires(send_sems, recv_sems)
     base = REDUCE_KINDS + 1 + GATHER_KINDS
-    down = Fold(wires, base, down_tiles, (down_recv,), ends[0], ends[1], down_in_ref)
+    down = Fold(wires, base, down_tiles, (down_recv,), ends[0], ends[1])
     made = Fold(wires, base + FOLD_KINDS, made_tiles, (made_recv,), ends[2], ends[3])
     stats = Stats(wires, REDUCE_KINDS, stats_ref, stats_recv)
-    down.start()
+    def make_down(step):
+        @pl.when(step < 7)
+        def _():
+            fetch(grad_ref, step + 1, turn_tile(step + 1)).start()
+
+        fetch(grad_ref, step, turn_tile(step)).wait()
+        left = stream[lax.rem(step, 2)].reshape(4 * rows, BLOCK)
+        down_tiles[turn_tile(step)] = weight_grad(
+            left, hidden_ref[...].reshape(4 * rows, units)
+        ).astype(B16)
+
     stats.start(0)
+    loads.wait(0, 1)
+    make_tiles(down, make_down, 0, 2)
     reduce = Reduce(wires, rows_ref, weight_ref, True, bufs)
-    loads.wait(0, 3)
-    reduce.start((lambda: stats.step(0), lambda: stats.step(1)))
-    load.wait()
+    loads.wait(1, 4)
+
+    def first_part():
+        stats.step(0)
+        make_tiles(down, make_down, 2, 4)
+
+    def second_part():
+        stats.step(1)
+        make_tiles(down, make_down, 4, 8)
+
+    reduce.start((first_part, second_part))
+    fetch(second_ref, 0, turn_tile(0)).start()
     down.step()
 
     def store(step):
@@ -1733,11 +1771,11 @@
 
     make_tiles(made, make, 0, 4)
     reduce.middle()
+    loads.wait(4, 7)
     stats.finish(2)
     pull_columns(stats_ref, scale_ref, column_ref, width)
     down.middle()
     make_tiles(made, make, 4, 8)
-    loads.wait(3, 7)
     gather = Gather(wires, REDUCE_KINDS + 1, whole_ref, own, gather_sem)
 
     @pl.loop(0, width // CHUNK)
@@ -1759,53 +1797,35 @@
     made.middle()
     gather.close()
     made.late()
-    fetch(whole_ref, 0, 0).start()
-    upstream[...] = jnp.zeros_like(upstream)
-
-    @pl.loop(0, 8)
-    def _(tile):
-        @pl.when(tile < 7)
-        def _():
-            fetch(whole_ref, tile + 1, tile + 1).start()
-
-        fetch(whole_ref, tile, tile).wait()
-        left = stream[lax.rem(tile, 2)].reshape(4 * rows, BLOCK)
-        upstream[...] += rows_dot(left, branch_ref[:, tile_columns(tile)])
-        out_ref[tile] = weight_grad(left, mixed_ref[...].reshape(4 * rows, -1)).astype(B16)
-
-    upstream_ref[...] = upstream[...].astype(B16).reshape(upstream_ref.shape)
     down.close()
     made.close()
     reduce.close()
 
 
 def middle_call(
-    rows, w_gates, w_uppers, stats, scale, value, gain, base, down, second, w_branch, mixed, number
+    rows, w_gates, w_uppers, stats, scale, value, gain, base, hidden, grad, second, number
 ):
     height, width = value.shape
     count = width // CHUNK
     columns = rows.shape[2]
-    quarter, units = down.shape[1:]
-    heads = mixed.shape[2]
+    quarter, units = width // 4, hidden.shape[2]
     sizes = (units, SPLIT)
     ends, tiles = [], []
     for size in sizes:
         ends += [shape((quarter, size), F32), shape((quarter, size))]
         tiles += [pltpu.VMEM((8, quarter, size), B16)] + fold_scratch(quarter, size)
-    loaded = (rows, w_gates, w_uppers, value, base, w_branch, mixed)
+    loaded = (rows, w_gates, w_uppers, value, base, hidden, scale)
     return pl.pallas_call(
         middle_kernel,
         out_shape=[
             shape((height, width), F32),
             shape((1, width), F32),
-            shape((4, height, heads)),
-            shape((8, quarter, heads)),
             shape((4, height, 2 * width)),
             shape((8, quarter, columns - SPLIT)),
         ]
         + ends,
-        in_specs=[IN_ANY] * 7 + [IN_VMEM] * 3 + [IN_ANY] * 2,
-        out_specs=[IN_VMEM] * 4 + [IN_ANY] * 2 + [IN_VMEM, IN_ANY] * 2,
+        in_specs=[IN_ANY] * 7 + [IN_VMEM] * 2 + [IN_ANY] * 2,
+        out_specs=[IN_VMEM] * 2 + [IN_ANY] * 2 + [IN_VMEM, IN_ANY] * 2,
         scratch_shapes=reduce_scratch(height, width)
         + [
             pltpu.VMEM((8, 8, 128), F32),
@@ -1817,18 +1837,17 @@
         + [
             pltpu.VMEM((2, 4, height, BLOCK), B16),
             pltpu.SemaphoreType.DMA((2,)),
-            pltpu.SemaphoreType.DMA,
             pltpu.VMEM((2, quarter, columns - SPLIT), B16),
             pltpu.SemaphoreType.DMA((2,)),
-            pltpu.VMEM((4 * height, heads), F32),
         ]
         + tiles
         + [pltpu.VMEM((2 * width, columns), B16)]
-        + load_scratch((rows,) + loaded[3:])[:-1]
+        + load_scratch((hidden, rows, value, base))[:-1]
+        + [pltpu.VMEM((height, 128), F32)]
         + [pltpu.SemaphoreType.DMA((len(loaded),))],
         compiler_params=remote_params(number),
         cost_estimate=cost(48 * height * units * width, 64 * height * width),
-    )(*loaded, stats, scale, gain, down, second)
+    )(*loaded, stats, gain, grad, second)
 
 
 def last_kernel(
@@ -1841,7 +1860,7 @@
     gain_ref,
     extra_ref,
     out_in_ref,
-    first_ref,
+    project_in_ref,
     result_ref,
     totals_ref,
     out_mine_ref,
@@ -1852,13 +1871,13 @@
 ):
     bufs = scratch[:7]
     stats_ref, stats_recv, column_ref, send_sems, recv_sems = scratch[7:12]
-    out_ref, project_ref, whole, sums_ref, sums_recv, load_sem = scratch[12:18]
-    out_bufs, project_bufs = scratch[18:19], scratch[19:20]
-    rows_ref, weight_ref, value_ref, base_ref = scratch[20:24]
+    out_ref, project_ref, sums_ref, sums_recv, load_sem = scratch[12:17]
+    out_bufs, project_bufs = scratch[17:18], scratch[18:19]
+    rows_ref, weight_ref, value_ref, base_ref = scratch[19:23]
     rows, width = value_ref.shape
     loads = Loads(
-        (rows_in_ref, weight_in_ref, first_ref, value_in_ref, base_in_ref, out_in_ref),
-        (rows_ref, weight_ref, whole, value_ref, base_ref, out_ref),
+        (project_in_ref, weight_in_ref, rows_in_ref, value_in_ref, base_in_ref, out_in_ref),
+        (project_ref, weight_ref, rows_ref, value_ref, base_ref, out_ref),
         load_sem,
     )
     loads.start()
@@ -1871,56 +1890,86 @@
     base = REDUCE_KINDS + 1
     out = Fold(wires, base, out_ref, out_bufs, out_mine_ref, out_theirs_ref, out_in_ref)
     project = Fold(
-        wires, base + FOLD_KINDS, project_ref, project_bufs, project_mine_ref, project_theirs_ref
+        wires,
+        base + FOLD_KINDS,
+        project_ref,
+        project_bufs,
+        project_mine_ref,
+        project_theirs_ref,
+        project_in_ref,
     )
     stats = Stats(wires, REDUCE_KINDS, stats_ref, stats_recv)
     stats.start(0)
     out.start()
     loads.wait(0, 2)
 
-    def make(step):
-        tile = turn_tile(step)
-        left = whole[:, :, tile_columns(tile)].reshape(4 * rows, BLOCK)
-        grad = weight_grad(left, rows_ref[...].reshape(4 * rows, rows_ref.shape[2]))
-        project_ref[tile] = grad.astype(B16)
+    @pl.loop(0, 8)
+    def _(tile):
         share = jnp.sum(
-            grad * weight_ref[tile_columns(tile), :].astype(F32), axis=1, keepdims=True
+            project_ref[tile].astype(F32) * weight_ref[tile_columns(tile), :].astype(F32),
+            axis=1,
+            keepdims=True,
         )
         sums_ref[tile, 0:1, :] = lie(share[:128])
         sums_ref[tile, 1:2, :] = lie(share[128:])
 
-    side, across, core = neighbours()
-    near, far = planes()
-    hops = [
-        lambda hop=hop, device=device: wires.copy(
-            base + 2 * FOLD_KINDS, hop, sums_ref, sums_recv.at[hop], device
-        )
-        for hop, device in enumerate((core, across, near, far))
-    ]
-
-    def add(hop):
-        hops[hop]().wait()
-        sums_ref[...] = sums_ref[...] + sums_recv[hop]
+    side_device, across, core = neighbours()
+    near, mirror = planes()
+
+    def hop(index):
+        slot, device = ((0, core), (1, across), (2, near), (3, mirror), (2, near))[index]
+        kind, chunk = divmod(index, 4)
+        return wires.copy(
+            base + 2 * FOLD_KINDS + kind, chunk, sums_ref, sums_recv.at[slot], device
+        )
+
+    def add(slot):
+        sums_ref[...] = sums_ref[...] + sums_recv[slot]
 
     reduce = Reduce(wires, rows_ref, weight_ref, True, bufs)
-    reduce.start((lambda: stats.step(0), lambda: stats.step(1)))
     loads.wait(2, 3)
-    make_tiles(project, make, 0, 8)
-    hops[0]().start()
+    hop(0).start()
+    reduce.give(0)
+    hop(0).wait()
+    add(0)
+    hop(1).start()
+    stats.step(0)
+
+    def after_two():
+        hop(1).wait()
+        add(1)
+
+        @pl.when(jnp.logical_not(inner()))
+        def _():
+            hop(2).start()
+
+        project.start()
+        stats.step(1)
+
+    reduce.rest((after_two, lambda: None))
     loads.wait(3, 6)
     out.step()
-    add(0)
-    hops[1]().start()
+    ends_line = jnp.logical_not(inner())
+
+    @pl.when(inner())
+    def _():
+        hop(2).wait_recv()
+        add(2)
+        hop(3).start()
+
+    out.middle()
     reduce.middle()
-    out.middle()
-    project.step()
     stats.finish(2)
     pull_columns(stats_ref, scale_ref, column_ref, width)
-    add(1)
-    hops[2]().start()
+
+    @pl.when(inner())
+    def _():
+        hop(3).wait()
+        add(3)
+        hop(4).start()
+
+    project.step()
     project.middle()
-    add(2)
-    hops[3]().start()
 
     @pl.loop(0, width // CHUNK)
     def _(chunk):
@@ -1929,11 +1978,20 @@
         )
         result_ref[:, at] = result.astype(B16)
 
+    @pl.when(inner())
+    def _():
+        hop(4).wait_send()
+
+    @pl.when(ends_line)
+    def _():
+        hop(2).wait_send()
+        hop(4).wait_recv()
+        sums_ref[...] = sums_recv[2]
+
+    move = wires.copy(base + 2 * FOLD_KINDS + 1, 1, sums_ref, sums_recv.at[4], side_device)
+    move.start()
     out.late()
     project.late()
-    add(3)
-    move = wires.copy(base + 2 * FOLD_KINDS + 1, 0, sums_ref, sums_recv.at[4], side)
-    move.start()
     move.wait()
     totals_ref[0:4] = sums_ref[0:4] + sums_recv[4, 4:8]
     totals_ref[4:8] = sums_ref[4:8] + sums_recv[4, 0:4]
@@ -1945,7 +2003,7 @@
     reduce.close()
 
 
-def last_call(rows, weight, stats, scale, value, gain, base, extra, out, first, number):
+def last_call(rows, weight, stats, scale, value, gain, base, extra, out, project, number):
     height, width = value.shape
     count = width // CHUNK
     quarter, branch = out.shape[1:]
@@ -1972,7 +2030,6 @@
         + [
             pltpu.VMEM((8, quarter, branch), B16),
             pltpu.VMEM((8, quarter, columns), B16),
-            pltpu.VMEM((4, height, 2 * width), B16),
             pltpu.VMEM((10, 8, 128), F32),
             pltpu.VMEM((5, 10, 8, 128), F32),
             pltpu.SemaphoreType.DMA((6,)),
@@ -1982,7 +2039,7 @@
         + load_scratch((rows, weight, value, base))[:4],
         compiler_params=remote_params(number),
         cost_estimate=cost(32 * height * columns * width, 64 * height * width),
-    )(rows, weight, value, base, stats, scale, gain, extra, out, first)
+    )(rows, weight, value, base, stats, scale, gain, extra, out, project)
 
 
 def back_kernel(
@@ -1991,19 +2048,60 @@
     key_gain_ref,
     *refs,
 ):
-    operands, refs = refs[:12], refs[12:]
-    rest_ref, refs = refs[0], refs[1:]
-    output_ref, result_ref, stats_ref, gains_ref = refs[:4]
-    ends, scratch = refs[4:6], refs[6:]
+    operands, refs = refs[:13], refs[13:]
+    rest_ref, whole_ref, first_ref = refs[:3]
+    output_ref, result_ref, stats_ref, gains_ref, out_ref, project_ref = refs[3:9]
+    ends, scratch = refs[9:11], refs[11:]
     bufs = scratch[:7]
-    query_acc, key_acc, value_acc, send_sems, recv_sems, rest_sem = scratch[7:13]
-    tiles, fold_recv = scratch[13:15]
-    held, load_sem = scratch[15:27], scratch[27]
-    hidden_ref, down_ref, upstream, starts_ref, cosine_ref, sine_ref = held[:6]
-    projected_ref, query_ref, key_ref, value_ref, log_ref, residual_ref = held[6:]
+    key_acc, value_acc, send_sems, recv_sems, rest_sem = scratch[7:12]
+    tiles, fold_recv = scratch[12:14]
+    held, load_sem = scratch[14:27], scratch[27]
+    upstream, acc, stream, stream_sem, stage, stage_sem = scratch[28:]
+    hidden_ref, down_ref, branch_ref, mixed_ref, starts_ref, cosine_ref, sine_ref = held[:7]
+    projected_ref, query_ref, key_ref, value_ref, log_ref, residual_ref = held[7:]
     attend_loads = Loads(operands, held, load_sem)
     attend_loads.start()
     width = residual_ref.shape[1]
+    rows = residual_ref.shape[0]
+
+    def fetch(ref, tile):
+        slot = lax.rem(tile, 2)
+        return pltpu.make_async_copy(
+            ref.at[:, :, tile_columns(tile)], stream.at[slot], stream_sem.at[slot]
+        )
+
+    def each_tile(ref, target, right, work):
+        columns = target.shape[2]
+
+        def store(tile):
+            slot = lax.rem(tile, 2)
+            return pltpu.make_async_copy(
+                stage.at[slot, :, :columns], target.at[tile], stage_sem.at[slot]
+            )
+
+        @pl.loop(0, 8)
+        def _(tile):
+            @pl.when(tile < 7)
+            def _():
+                fetch(ref, tile + 1).start()
+
+            fetch(ref, tile).wait()
+
+            @pl.when(tile >= 2)
+            def _():
+                store(tile - 2).wait()
+
+            left = stream[lax.rem(tile, 2)].reshape(4 * rows, BLOCK)
+            work(tile, left)
+            stage[lax.rem(tile, 2), :, :columns] = weight_grad(
+                left, right[...].reshape(4 * rows, columns)
+            ).astype(B16)
+            store(tile).start()
+
+        for tile in (6, 7):
+            store(tile).wait()
+
+    fetch(whole_ref, 0).start()
     core = lax.rem(lax.axis_index("tx"), 2)
     load = pltpu.make_async_copy(rest_ref, tiles, rest_sem)
     load.start()
@@ -2014,8 +2112,17 @@
     reduce = Reduce(wires, hidden_ref, down_ref, False, bufs)
     attend_loads.wait(0, 2)
     reduce.start()
-    attend_loads.wait(2, 12)
+    attend_loads.wait(2, 13)
     load.wait()
+    acc[...] = jnp.zeros_like(acc)
+
+    def branch_work(tile, left):
+        acc[...] += rows_dot(left, branch_ref[:, tile_columns(tile)])
+
+    each_tile(whole_ref, out_ref, mixed_ref, branch_work)
+    fetch(first_ref, 0).start()
+    upstream[...] = acc[...].astype(B16).reshape(upstream.shape)
+    fold.step()
     stats_ref[...] = jnp.zeros_like(stats_ref)
     fixed_refs = (starts_ref, cosine_ref, sine_ref, query_gain_ref, key_gain_ref)
     saved_refs = (query_ref, key_ref, value_ref, log_ref)
@@ -2033,15 +2140,16 @@
             result_ref,
             stats_ref,
             gains_ref,
-            (query_acc, key_acc, value_acc),
+            (acc, key_acc, value_acc),
         )
 
         @pl.when(seq == 0)
         def _():
             reduce.middle()
-            fold.step()
 
     fold.middle()
+
+    each_tile(first_ref, project_ref, result_ref, lambda tile, left: None)
 
 
     @pl.loop(0, width // CHUNK)
@@ -2054,7 +2162,9 @@
     reduce.close()
 
 
-def back_call(upstream, hidden, w_back, residual, fixed_args, projected, saved, rest, most, number):
+def back_call(
+    whole, first, w_branch, mixed, hidden, w_back, residual, fixed_args, projected, saved, rest, most, number
+):
     height, width = residual.shape
     _, cosine, _, query_gain, _ = fixed_args
     depth = query_gain.shape[1]
@@ -2062,7 +2172,7 @@
     columns = projected.shape[2]
     heads = columns // depth - 2
     quarter, columns_left = rest.shape[1:]
-    loaded = (hidden, w_back, upstream) + fixed_args[:3] + (projected,) + saved + (residual,)
+    loaded = (hidden, w_back, w_branch, mixed) + fixed_args[:3] + (projected,) + saved + (residual,)
     return pl.pallas_call(
         lambda *refs: back_kernel(most, *refs),
         out_shape=(
@@ -2070,23 +2180,32 @@
             shape((4, height, columns)),
             shape((8, 8, 128), F32),
             shape((2, 8, depth), F32),
+            shape((8, quarter, heads * depth)),
+            shape((8, quarter, columns)),
         )
         + (shape((quarter, columns_left), F32), shape((quarter, columns_left))),
-        in_specs=[IN_VMEM] * 2 + [IN_ANY] * 13,
-        out_specs=[IN_VMEM] * 5 + [IN_ANY],
+        in_specs=[IN_VMEM] * 2 + [IN_ANY] * 16,
+        out_specs=[IN_VMEM] * 4 + [IN_ANY] * 2 + [IN_VMEM, IN_ANY],
         scratch_shapes=reduce_scratch(height, width)
         + [
-            pltpu.VMEM((length, heads * depth), F32),
             pltpu.VMEM((length, depth), F32),
             pltpu.VMEM((length, depth), F32),
         ]
         + wire_scratch(REDUCE_KINDS + FOLD_KINDS, width // CHUNK)
         + [pltpu.SemaphoreType.DMA, pltpu.VMEM(rest.shape, B16)]
         + fold_scratch(quarter, columns_left)
-        + load_scratch(loaded),
+        + load_scratch(loaded)
+        + [
+            pltpu.VMEM((4, height, heads * depth), B16),
+            pltpu.VMEM((4 * height, heads * depth), F32),
+            pltpu.VMEM((2, 4, height, BLOCK), B16),
+            pltpu.SemaphoreType.DMA((2,)),
+            pltpu.VMEM((2, quarter, columns), B16),
+            pltpu.SemaphoreType.DMA((2,)),
+        ],
         compiler_params=remote_params(number),
         cost_estimate=cost(16 * height * hidden.shape[2] * width, 64 * height * width),
-    )(*fixed_args[3:], *loaded, rest)
+    )(*fixed_args[3:], *loaded, rest, whole, first)
 
 
 def finish_kernel(place_ref, *refs):
@@ -2164,10 +2283,6 @@
     )(place, *parts, totals, gain)
 
 
-def product_grad(left, right):
-    return weight_grad(left, right).astype(B16)
-
-
 def plane_device(
     tokens,
     seg_ids,
@@ -2194,8 +2309,8 @@
     half = jnp.arange(depth // 2, dtype=F32)
     rate = THETA ** (-half * 2.0 / depth)
     rate = jnp.concatenate([rate, rate])[None]
-    gains, starts, cosine, sine, token_whole, w_project, w_branch = open_call(
-        tokens, w_query, w_key, w_value, w_out, jnp.stack([attn_gain, mlp_gain]), seg_ids, rate, 0
+    attn_row, mlp_row, starts, cosine, sine, token_whole, w_project, w_branch = open_call(
+        tokens, w_query, w_key, w_value, w_out, attn_gain[None], mlp_gain[None], seg_ids, rate, 0
     )
     fixed_args = (starts, cosine, sine, query_gain[None], key_gain[None])
     (
@@ -2211,7 +2326,7 @@
         w_back,
         gate_quarter,
     ) = front_call(
-        token_whole, w_project, gains[0:1], fixed_args, most, cotangent, w_down, w_gate, 1
+        token_whole, w_project, attn_row, fixed_args, most, cotangent, w_down, w_gate, 1
     )
     residual, residual_whole, w_uppers, w_gates = branch_call(
         mixed, w_branch, tokens, w_up, w_gate, gate_quarter, 2
@@ -2219,15 +2334,12 @@
     flat = (4 * rows, 2 * width)
     grad_flat = grad_whole.reshape(flat)
     second, hidden, unit_grads, second_scale, unit_stats = units_call(
-        residual_whole.reshape(flat), grad_flat, w_gates, w_uppers, w_back, gains[1:2]
-    )
-    tiles = lambda grad: grad.reshape(8, -1, grad.shape[1])
+        residual_whole.reshape(flat), grad_flat, w_gates, w_uppers, w_back, mlp_row
+    )
     (
         residual_grad,
         mlp_gain_part,
-        upstream,
-        out_tiles,
-        _,
+        branch_whole,
         rest_tiles,
         *ends,
     ) = middle_call(
@@ -2235,18 +2347,20 @@
         w_gates,
         w_uppers,
         unit_stats,
-        second_scale[:rows],
+        second_scale,
         residual,
         mlp_gain[None],
         cotangent,
-        tiles(product_grad(grad_flat, hidden)),
+        hidden.reshape(4, rows, units),
+        grad_whole,
         second.reshape(4, rows, 2 * width),
+        3,
+    )
+    output, proj_grads, proj_stats, gain_parts, out_tiles, project_tiles, *rest_ends = back_call(
+        branch_whole,
+        first,
         w_branch,
         mixed,
-        3,
-    )
-    output, proj_grads, proj_stats, gain_parts, *rest_ends = back_call(
-        upstream,
         hidden.reshape(4, rows, units),
         w_back,
         residual,
@@ -2273,7 +2387,7 @@
         residual_grad,
         extra,
         out_tiles,
-        first,
+        project_tiles,
         5,
     )
     place = lax.axis_index("ty").reshape(1).astype(jnp.int32)
@@ -2291,7 +2405,7 @@
         place,
         (*ends, *rest_ends, out_mine, out_theirs, project_mine, project_theirs),
         totals,
-        gains[0].reshape(16, 128),
+        attn_row.reshape(16, 128),
         (2 * head_width, 2 * kv_width, 2 * head_width, 2 * units),
     )
     attn_total, mlp_total = attn_total.reshape(-1), mlp_total.reshape(-1)

time: 538 us -> 515 us (0.957)
  the two profiles are of different devices: /device:TPU:10 before, /device:TPU:0 now
where the time goes in v5:
time: 515 us; the launch traced here: 506 us
  Pallas kernels  500 us (97%)
    pallas_call x1, Pallas kernels, middle_call(): pl.pallas_call(middle_kernel, out_shape=[shape((height, width), F32), sha...  114 us
    pallas_call x1, Pallas kernels, branch_call(): pl.pallas_call(branch_kernel, out_shape=(shape((height, width), F32), sha...  92.8 us
    pallas_call x1, Pallas kernels, back_call(): pl.pallas_call(lambda *refs: back_kernel(most, *refs), out_shape=(shape((...  80.2 us
    pallas_call x1, Pallas kernels, last_call(): pl.pallas_call(last_kernel, out_shape=(shape((height, width)), shape((11,...  62.2 us
    pallas_call x1, Pallas kernels, front_call(): pl.pallas_call(lambda *refs: front_kernel(most, *refs), out_shape=outs, i...  60.1 us
    pallas_call x1, Pallas kernels, open_call(): pl.pallas_call(open_kernel, out_shape=(shape((1, 2 * width), F32), shape(...  53 us
    pallas_call x1, Pallas kernels, units_call(): pl.pallas_call(units_kernel, out_shape=(shape((tokens, width)), shape((to...  31.5 us

profile of v5, /device:TPU:0, one launch (start us, length us, event | category | flops | bytes accessed | tf_op | source)
XLA Modules:
  0.0 506.0 jit_solution(138809121867401268)
XLA Ops:
  0.7 0.6 maximum_bitcast_fusion.rate_ref
  1.2 53.0 %shard_map.237 = (f32[1,2048]{1,0:T(1,128)}, f32[1,2048]{1,0:T(1,128)}, s32[2,1024,1]{2,1,0:T(8,128)}, f32[2,1024,128]{2,1,0:T(8,128)}, f32[2,1024,128]{2,1,0:T(...) custom-call(bf16[512,1024]{1,0:T(8,128)(2,1)} %value_in_ref.1, ...), custom_call_target="tpu_custom_call" | custom-call | bytes 16777216 | tf_op jit(solution)/shard_map/pallas_call | solution.py:1218
  54.3 60.1 %shard_map.238 = (bf16[4,512,2048]{2,1,0:T(8,128)(2,1)}, f32[512,128]{1,0:T(8,128)}, f32[4,512,512]{2,1,0:T(8,128)}, bf16[4,512,256]{2,1,0:T(8,128)(2,1)}, bf16[...) custom-call(bf16[4,512,2048]{2,1,0:T(8,128)(2,1)} %get-tuple-element, ...), custom_call_target="tpu_custom_call" | custom-call | flops 4294967296 | bytes 33554432 | tf_op jit(solution)/shard_map/pallas_call | solution.py:1401
  114.4 92.8 %shard_map.239 = (f32[512,1024]{1,0:T(8,128)}, bf16[4,512,2048]{2,1,0:T(8,128)(2,1)}, bf16[2048,768]{1,0:T(8,128)(2,1)}, bf16[2048,768]{1,0:T(8,128)(2,1)}) custom-call(bf16[4,512,256]{2,1,0:T(8,128)(2,1)} %get-tuple-element.78.rows_in_ref.refs_5_, bf16[256,2048]{1,0:T(8,128)(2,1)} %get-tuple-element.79.weight_in_ref.refs_4_, ...), custom_call_target="tpu_custom_call" | custom-call | flops 2147483648 | bytes 33554432 | tf_op jit(solution)/shard_map/pallas_call | solution.py:1490
  207.2 31.5 %shard_map.240 = (bf16[2048,2048]{1,0:T(8,128)(2,1)}, bf16[2048,768]{1,0:T(8,128)(2,1)}, bf16[2048,1536]{1,0:T(8,128)(2,1)}, f32[2048,128]{1,0:T(8,128)}, f32[8,8,128]{2,1,0:T(8,128)}) custom-call(bf16[2048,2048]{1,0:T(8,128)(2,1)} %bitcast.35, bf16[2048,2048]{1,0:T(8,128)(2,1)} %bitcast.34, bf16[2048,768]{1,0:T(8,128)(2,1)} %get-tuple-element.83.gates_ref.gates_in_ref, ...), custom_call_target="tpu_custom_call" | custom-call | flops 19327352832 | bytes 41943040 | tf_op jit(solution)/shard_map/pallas_call | solution.py:1554
  238.7 114.1 %shard_map.241 = (f32[512,1024]{1,0:T(8,128)}, f32[1,1024]{1,0:T(1,128)}, bf16[4,512,2048]{2,1,0:T(8,128)(2,1)}, bf16[8,256,1024]{2,1,0:T(8,128)(2,1)}, f32[256,...) custom-call(bf16[4,512,1536]{2,1,0:T(8,128)(2,1)} %bitcast.39, ...), custom_call_target="tpu_custom_call" | custom-call | flops 19327352832 | bytes 33554432 | tf_op jit(solution)/shard_map/pallas_call | solution.py:1818
  352.8 0.0 copy-start.2
  352.8 80.2 %shard_map.242 = (bf16[512,1024]{1,0:T(8,128)(2,1)}, bf16[4,512,512]{2,1,0:T(8,128)(2,1)}, f32[8,8,128]{2,1,0:T(8,128)}, f32[2,8,128]{2,1,0:T(8,128)}, bf16[8,25...) custom-call(f32[1,128]{1,0:T(1,128)} %bitcast.31, ...), custom_call_target="tpu_custom_call" | custom-call | flops 6442450944 | bytes 33554432 | tf_op jit(solution)/shard_map/pallas_call | solution.py:2176
  433.0 0.7 slice_reduce_fusion
  433.7 0.0 copy-done.2
  433.7 0.6 pad_maximum_fusion.extra_ref
  434.3 62.2 %shard_map.243 = (bf16[512,1024]{1,0:T(8,128)(2,1)}, f32[11,8,128]{2,1,0:T(8,128)}, f32[256,256]{1,0:T(8,128)}, bf16[256,256]{1,0:T(8,128)(2,1)}, f32[256,512]{1,0:T(8,128)}, /*index=5*/bf16[256,512]{1,0:T(8,128)(2,1)}) custom-call(bf16[4,512,512]{2,1,0:T(8,128)(2,1)} %get-tuple-element.102.rows_in_ref, ...), custom_call_target="tpu_custom_call" | custom-call | flops 8589934592 | bytes 33554432 | tf_op jit(solution)/shard_map/pallas_call | solution.py:2011
  496.6 0.0 copy-start
  496.6 0.0 copy-start.1
  496.6 5.7 %shard_map.244 = (f32[256,512]{1,0:T(8,128)}, f32[256,256]{1,0:T(8,128)}, f32[256,256]{1,0:T(8,128)}, f32[512,256]{1,0:T(8,128)}, f32[256,1536]{1,0:T(8,128)}, /...) custom-call(s32[1]{0:T(128)} %bitcast.12.place_ref, ...), custom_call_target="tpu_custom_call" | custom-call | bytes 16777216 | tf_op jit(solution)/shard_map/pallas_call | solution.py:2266
  502.3 1.3 slice_bitcast_fusion
  503.6 0.0 copy-done
  503.6 1.0 copy.29
  504.6 0.0 copy-done.1
  504.6 1.0 copy.30
  (2 shorter events, 0.0 us)
Async XLA Ops:
  352.8 80.9 %copy-start.2 = (f32[1,1024]{1,0:T(1,128)S(1)}, f32[1,1024]{1,0:T(1,128)}, u32[]{:S(2)}) copy-start(f32[1,1024]{1,0:T(1,128)} %get-tuple-element.106) | copy-start | bytes 12292
  496.6 7.0 %copy-start = (bf16[512,1024]{1,0:T(8,128)(2,1)S(1)}, bf16[512,1024]{1,0:T(8,128)(2,1)}, u32[]{:S(2)}) copy-start(bf16[512,1024]{1,0:T(8,128)(2,1)} %get-tuple-element.146) | copy-start | bytes 3145732
  496.6 8.0 %copy-start.1 = (bf16[512,1024]{1,0:T(8,128)(2,1)S(1)}, bf16[512,1024]{1,0:T(8,128)(2,1)}, u32[]{:S(2)}) copy-start(bf16[512,1024]{1,0:T(8,128)(2,1)} %get-tuple-element.147) | copy-start | bytes 3145732

commit v6 on v5

--- a/solution.py
+++ b/solution.py
@@ -1032,11 +1032,12 @@
                 self.sibling(chunk - 2, half).wait_send()
             self.give(chunk)
             self.take(chunk)
+            self.middle(chunk - 2, chunk - 1)
 
         between[1]()
 
-    def middle(self):
-        @pl.loop(0, self.count)
+    def middle(self, low=None, high=None):
+        @pl.loop(self.count - 2 if low is None else low, self.count if high is None else high)
         def _(chunk):
             even = lax.rem(chunk, 2) == 0
             self.corner(chunk, neighbours()[0]).wait_recv()
@@ -1180,9 +1181,31 @@
     shares[0].middle()
     shares[1].middle()
 
+    def between(seq, piece):
+        @pl.when(seq == 0)
+        def _():
+            if piece == 4:
+                gather.relay(0, 1)
+            elif piece == 6:
+                shares[0].late()
+                shares[1].late()
+
+        @pl.when(seq == 1)
+        def _():
+            if piece == 0:
+                gather.relay(1, 2)
+            elif piece == 2:
+                shares[0].later()
+                shares[1].later()
+            elif piece == 3:
+                gather.relay(2, 3)
+            elif piece == 6:
+                gather.relay(3, 4)
+
     @pl.loop(0, 2)
     def _(seq):
         for low in range(0, length, 128):
+            between(seq, low // 128)
             here = stand(seg_all[seq, :, low : low + 128])
             before = jnp.zeros((128, 128), F32)
             for other in range(0, length, 128):
@@ -1197,15 +1220,6 @@
             sine = jnp.sin(angle)
             sine_ref[seq, at, :] = jnp.where(lane < 64, -sine, sine)
 
-        @pl.when(seq == 0)
-        def _():
-            shares[0].late()
-            shares[1].late()
-            gather.relay(0, 2)
-            shares[0].later()
-            shares[1].later()
-
-    gather.relay(2)
     gather.close()
     shares[0].close()
     shares[1].close()
@@ -1309,11 +1323,12 @@
         neighbours()[0],
     )
     back.cross(0).start()
-    gate.start()
 
     @pl.loop(0, gather.count)
     def _(chunk):
         gather.send(chunk)
+
+    gate.start()
 
     loads.wait(0, 1)
     back.local(0).start()
@@ -1362,10 +1377,18 @@
             @pl.when(seq == 0)
             def _():
                 if turn == 0:
+                    gather.relay(0, 1)
+                elif turn == 1:
                     back.late()
                 elif turn == 2:
+                    gather.relay(1, 2)
+                else:
                     back.later()
-                gather.relay(turn, turn + 1)
+
+            @pl.when(seq == 1)
+            def _():
+                if turn < 2:
+                    gather.relay(turn + 2, turn + 3)
 
         attend_sequence(
             core, seq, most, projected_ref, fixed_refs, mixed_ref, saved_refs, between
@@ -1442,7 +1465,7 @@
     greet(neighbours() + planes())
     wires = Wires(send_sems, recv_sems)
     reduce = Reduce(wires, rows_ref, weight_ref, False, bufs)
-    gather = Gather(wires, REDUCE_KINDS, whole_ref, own, gather_sem, 0)
+    gather = Gather(wires, REDUCE_KINDS, whole_ref, own, gather_sem, 2)
     up = Share(
         wires, REDUCE_KINDS + GATHER_KINDS, (up_in_ref,), up_ref, True, up_sem, (up_held,)
     )
@@ -1734,12 +1757,14 @@
         make_tiles(down, make_down, 2, 4)
 
     def second_part():
+        down.step()
         stats.step(1)
-        make_tiles(down, make_down, 4, 8)
+        make_tiles(down, make_down, 4, 6)
 
     reduce.start((first_part, second_part))
+    reduce.middle()
+    make_tiles(down, make_down, 6, 8)
     fetch(second_ref, 0, turn_tile(0)).start()
-    down.step()
 
     def store(step):
         slot = lax.rem(step, 2)
@@ -1770,13 +1795,10 @@
         store(step).start()
 
     make_tiles(made, make, 0, 4)
-    reduce.middle()
     loads.wait(4, 7)
     stats.finish(2)
     pull_columns(stats_ref, scale_ref, column_ref, width)
-    down.middle()
-    make_tiles(made, make, 4, 8)
-    gather = Gather(wires, REDUCE_KINDS + 1, whole_ref, own, gather_sem)
+    gather = Gather(wires, REDUCE_KINDS + 1, whole_ref, own, gather_sem, 2)
 
     @pl.loop(0, width // CHUNK)
     def _(chunk):
@@ -1788,12 +1810,14 @@
         gather.send(chunk)
         gain_grad_ref[:, at] = jnp.sum(share, axis=0, keepdims=True)
 
+    down.middle()
+    make_tiles(made, make, 4, 8)
     for step in (6, 7):
         store(step).wait()
+    gather.relay(0, 3)
     down.late()
-    gather.relay(0, 2)
     made.step()
-    gather.relay(2)
+    gather.relay(3)
     made.middle()
     gather.close()
     made.late()

time: 515 us -> 497 us (0.965)
  the two profiles are of different devices: /device:TPU:0 before, /device:TPU:10 now
where the time goes in v6:
time: 497 us; the launch traced here: 487 us
  Pallas kernels  481 us (97%)
    pallas_call x1, Pallas kernels, middle_call(): pl.pallas_call(middle_kernel, out_shape=[shape((height, width), F32), sha...  108 us
    pallas_call x1, Pallas kernels, branch_call(): pl.pallas_call(branch_kernel, out_shape=(shape((height, width), F32), sha...  87.4 us
    pallas_call x1, Pallas kernels, back_call(): pl.pallas_call(lambda *refs: back_kernel(most, *refs), out_shape=(shape((...  79.4 us
    pallas_call x1, Pallas kernels, last_call(): pl.pallas_call(last_kernel, out_shape=(shape((height, width)), shape((11,...  62.4 us
    pallas_call x1, Pallas kernels, front_call(): pl.pallas_call(lambda *refs: front_kernel(most, *refs), out_shape=outs, i...  57.1 us
    pallas_call x1, Pallas kernels, open_call(): pl.pallas_call(open_kernel, out_shape=(shape((1, 2 * width), F32), shape(...  49.5 us
    pallas_call x1, Pallas kernels, units_call(): pl.pallas_call(units_kernel, out_shape=(shape((tokens, width)), shape((to...  31 us

profile of v6, /device:TPU:10, one launch (start us, length us, event | category | flops | bytes accessed | tf_op | source)
XLA Modules:
  0.0 487.2 jit_solution(3157064702279088956)
XLA Ops:
  0.7 0.6 maximum_bitcast_fusion.rate_ref
  1.2 49.5 %shard_map.237 = (f32[1,2048]{1,0:T(1,128)}, f32[1,2048]{1,0:T(1,128)}, s32[2,1024,1]{2,1,0:T(8,128)}, f32[2,1024,128]{2,1,0:T(8,128)}, f32[2,1024,128]{2,1,0:T(...) custom-call(bf16[512,1024]{1,0:T(8,128)(2,1)} %value_in_ref.1, ...), custom_call_target="tpu_custom_call" | custom-call | bytes 16777216 | tf_op jit(solution)/shard_map/pallas_call | solution.py:1232
  50.8 57.1 %shard_map.238 = (bf16[4,512,2048]{2,1,0:T(8,128)(2,1)}, f32[512,128]{1,0:T(8,128)}, f32[4,512,512]{2,1,0:T(8,128)}, bf16[4,512,256]{2,1,0:T(8,128)(2,1)}, bf16[...) custom-call(bf16[4,512,2048]{2,1,0:T(8,128)(2,1)} %get-tuple-element, ...), custom_call_target="tpu_custom_call" | custom-call | flops 4294967296 | bytes 33554432 | tf_op jit(solution)/shard_map/pallas_call | solution.py:1424
  107.9 87.4 %shard_map.239 = (f32[512,1024]{1,0:T(8,128)}, bf16[4,512,2048]{2,1,0:T(8,128)(2,1)}, bf16[2048,768]{1,0:T(8,128)(2,1)}, bf16[2048,768]{1,0:T(8,128)(2,1)}) custom-call(bf16[4,512,256]{2,1,0:T(8,128)(2,1)} %get-tuple-element.78.rows_in_ref.refs_5_, bf16[256,2048]{1,0:T(8,128)(2,1)} %get-tuple-element.79.weight_in_ref.refs_4_, ...), custom_call_target="tpu_custom_call" | custom-call | flops 2147483648 | bytes 33554432 | tf_op jit(solution)/shard_map/pallas_call | solution.py:1513
  195.3 31.0 %shard_map.240 = (bf16[2048,2048]{1,0:T(8,128)(2,1)}, bf16[2048,768]{1,0:T(8,128)(2,1)}, bf16[2048,1536]{1,0:T(8,128)(2,1)}, f32[2048,128]{1,0:T(8,128)}, f32[8,8,128]{2,1,0:T(8,128)}) custom-call(bf16[2048,2048]{1,0:T(8,128)(2,1)} %bitcast.35, bf16[2048,2048]{1,0:T(8,128)(2,1)} %bitcast.34, bf16[2048,768]{1,0:T(8,128)(2,1)} %get-tuple-element.83.gates_ref.gates_in_ref, ...), custom_call_target="tpu_custom_call" | custom-call | flops 19327352832 | bytes 41943040 | tf_op jit(solution)/shard_map/pallas_call | solution.py:1577
  226.4 108.3 %shard_map.241 = (f32[512,1024]{1,0:T(8,128)}, f32[1,1024]{1,0:T(1,128)}, bf16[4,512,2048]{2,1,0:T(8,128)(2,1)}, bf16[8,256,1024]{2,1,0:T(8,128)(2,1)}, f32[256,...) custom-call(bf16[4,512,1536]{2,1,0:T(8,128)(2,1)} %bitcast.39, ...), custom_call_target="tpu_custom_call" | custom-call | flops 19327352832 | bytes 33554432 | tf_op jit(solution)/shard_map/pallas_call | solution.py:1842
  334.7 0.0 copy-start.2
  334.7 79.4 %shard_map.242 = (bf16[512,1024]{1,0:T(8,128)(2,1)}, bf16[4,512,512]{2,1,0:T(8,128)(2,1)}, f32[8,8,128]{2,1,0:T(8,128)}, f32[2,8,128]{2,1,0:T(8,128)}, bf16[8,25...) custom-call(f32[1,128]{1,0:T(1,128)} %bitcast.31, ...), custom_call_target="tpu_custom_call" | custom-call | flops 6442450944 | bytes 33554432 | tf_op jit(solution)/shard_map/pallas_call | solution.py:2200
  414.0 0.7 slice_reduce_fusion
  414.7 0.0 copy-done.2
  414.7 0.6 pad_maximum_fusion.extra_ref
  415.3 62.4 %shard_map.243 = (bf16[512,1024]{1,0:T(8,128)(2,1)}, f32[11,8,128]{2,1,0:T(8,128)}, f32[256,256]{1,0:T(8,128)}, bf16[256,256]{1,0:T(8,128)(2,1)}, f32[256,512]{1,0:T(8,128)}, /*index=5*/bf16[256,512]{1,0:T(8,128)(2,1)}) custom-call(bf16[4,512,512]{2,1,0:T(8,128)(2,1)} %get-tuple-element.102.rows_in_ref, ...), custom_call_target="tpu_custom_call" | custom-call | flops 8589934592 | bytes 33554432 | tf_op jit(solution)/shard_map/pallas_call | solution.py:2035
  477.8 0.0 copy-start
  477.8 0.0 copy-start.1
  477.8 5.7 %shard_map.244 = (f32[256,512]{1,0:T(8,128)}, f32[256,256]{1,0:T(8,128)}, f32[256,256]{1,0:T(8,128)}, f32[512,256]{1,0:T(8,128)}, f32[256,1536]{1,0:T(8,128)}, /...) custom-call(s32[1]{0:T(128)} %bitcast.12.place_ref, ...), custom_call_target="tpu_custom_call" | custom-call | bytes 16777216 | tf_op jit(solution)/shard_map/pallas_call | solution.py:2290
  483.5 1.3 slice_bitcast_fusion
  484.8 0.0 copy-done
  484.8 1.0 copy.29
  485.8 0.0 copy-done.1
  485.8 1.0 copy.30
  (2 shorter events, 0.0 us)
Async XLA Ops:
  334.7 80.1 %copy-start.2 = (f32[1,1024]{1,0:T(1,128)S(1)}, f32[1,1024]{1,0:T(1,128)}, u32[]{:S(2)}) copy-start(f32[1,1024]{1,0:T(1,128)} %get-tuple-element.106) | copy-start | bytes 12292
  477.8 7.0 %copy-start = (bf16[512,1024]{1,0:T(8,128)(2,1)S(1)}, bf16[512,1024]{1,0:T(8,128)(2,1)}, u32[]{:S(2)}) copy-start(bf16[512,1024]{1,0:T(8,128)(2,1)} %get-tuple-element.146) | copy-start | bytes 3145732
  477.8 8.0 %copy-start.1 = (bf16[512,1024]{1,0:T(8,128)(2,1)S(1)}, bf16[512,1024]{1,0:T(8,128)(2,1)}, u32[]{:S(2)}) copy-start(bf16[512,1024]{1,0:T(8,128)(2,1)} %get-tuple-element.147) | copy-start | bytes 3145732

commit v7 on v6

--- a/solution.py
+++ b/solution.py
@@ -1,5 +1,6 @@
 import jax
 import jax.numpy as jnp
+import numpy as np
 from jax import lax
 from jax.experimental import pallas as pl
 from jax.experimental.pallas import tpu as pltpu
@@ -1272,8 +1273,8 @@
     down_in_ref,
     gate_in_ref,
     first_ref,
+    projected_out_ref,
     scale_ref,
-    projected_ref,
     mixed_ref,
     query_ref,
     key_ref,
@@ -1289,6 +1290,8 @@
     loads = Loads(
         (down_in_ref, starts_in_ref, cosine_in_ref, sine_in_ref), scratch[8:12], scratch[12]
     )
+    projected_ref, projected_sem = scratch[13:]
+    keep = pltpu.make_async_copy(projected_ref, projected_out_ref, projected_sem)
     core = lax.rem(lax.axis_index("tx"), 2)
     cut(own, grad_ref)
     rows = whole_ref.shape[1]
@@ -1367,6 +1370,7 @@
         def _():
             back.middle()
 
+    keep.start()
     loads.wait(1, 4)
     fixed_refs = (starts_ref, cosine_ref, sine_ref, query_gain_ref, key_gain_ref)
     saved_refs = (query_ref, key_ref, value_ref, log_ref)
@@ -1399,6 +1403,7 @@
     gather.close()
     back.close()
     gate.wait()
+    keep.wait()
 
 
 def front_call(whole, w_project, gain, fixed_args, most, cotangent, w_down, w_gate, number):
@@ -1410,8 +1415,8 @@
     heads = columns // depth - 2
     outs = (
         shape((4, rows, 2 * width)),
+        shape((4, rows, columns), F32),
         shape((rows, 128), F32),
-        shape((4, rows, columns), F32),
         shape((4, rows, heads * depth)),
         shape((2, length, heads * depth)),
         shape((2, length, depth)),
@@ -1425,7 +1430,7 @@
         lambda *refs: front_kernel(most, *refs),
         out_shape=outs,
         in_specs=[IN_ANY] + [IN_VMEM] * 5 + [IN_ANY] * 5,
-        out_specs=[IN_ANY] + [IN_VMEM] * 7 + [IN_ANY] * 3,
+        out_specs=[IN_ANY] * 2 + [IN_VMEM] * 6 + [IN_ANY] * 3,
         scratch_shapes=gather_scratch(rows, width)
         + wire_scratch(GATHER_KINDS + SHARE_KINDS + 1, width // CHUNK)
         + [
@@ -1434,7 +1439,8 @@
             pltpu.VMEM((2, BLOCK, 2 * width), B16),
             pltpu.SemaphoreType.DMA((2, 2)),
         ]
-        + load_scratch((w_down, starts, cosine, sine)),
+        + load_scratch((w_down, starts, cosine, sine))
+        + [pltpu.VMEM((4, rows, columns), F32), pltpu.SemaphoreType.DMA],
         compiler_params=remote_params(number),
         cost_estimate=cost(16 * rows * width * columns, 64 * rows * width),
     )(whole, w_project, gain, query_gain, key_gain, cotangent, starts, cosine, sine, w_down, w_gate)
@@ -1763,8 +1769,6 @@
 
     reduce.start((first_part, second_part))
     reduce.middle()
-    make_tiles(down, make_down, 6, 8)
-    fetch(second_ref, 0, turn_tile(0)).start()
 
     def store(step):
         slot = lax.rem(step, 2)
@@ -1794,22 +1798,27 @@
             ).astype(B16)
         store(step).start()
 
-    make_tiles(made, make, 0, 4)
     loads.wait(4, 7)
     stats.finish(2)
     pull_columns(stats_ref, scale_ref, column_ref, width)
     gather = Gather(wires, REDUCE_KINDS + 1, whole_ref, own, gather_sem, 2)
 
-    @pl.loop(0, width // CHUNK)
-    def _(chunk):
-        at, result, share = pulled(
-            reduce, chunk, (scale_ref, value_ref, gain_ref, base_ref), column_ref
-        )
-        result_ref[:, at] = result
-        own[chunk] = result.astype(B16)
-        gather.send(chunk)
-        gain_grad_ref[:, at] = jnp.sum(share, axis=0, keepdims=True)
-
+    def finish_chunks(low, high):
+        @pl.loop(low, high)
+        def _(chunk):
+            at, result, share = pulled(
+                reduce, chunk, (scale_ref, value_ref, gain_ref, base_ref), column_ref
+            )
+            result_ref[:, at] = result
+            own[chunk] = result.astype(B16)
+            gather.send(chunk)
+            gain_grad_ref[:, at] = jnp.sum(share, axis=0, keepdims=True)
+
+    finish_chunks(0, 2)
+    make_tiles(down, make_down, 6, 8)
+    fetch(second_ref, 0, turn_tile(0)).start()
+    make_tiles(made, make, 0, 4)
+    finish_chunks(2, width // CHUNK)
     down.middle()
     make_tiles(made, make, 4, 8)
     for step in (6, 7):
@@ -2235,8 +2244,13 @@
 def finish_kernel(place_ref, *refs):
     downs, both, out, project = refs[0:2], refs[2:6], refs[6:8], refs[8:10]
     totals_ref, gain_ref = refs[10:12]
-    query_ref, key_ref, value_ref, out_ref, gate_ref, up_ref, down_ref = refs[12:19]
-    attn_ref, mlp_ref = refs[19:]
+    moved, refs = refs[12:14], refs[14:]
+    query_ref, key_ref, value_ref, out_ref, gate_ref, up_ref, down_ref = refs[:7]
+    attn_ref, mlp_ref, query_gain_ref, key_gain_ref = refs[7:11]
+    for source, target in zip(moved, refs[11:]):
+        target[...] = source[...]
+    query_gain_ref[...] = totals_ref[10, 0:1]
+    key_gain_ref[...] = totals_ref[10, 1:2]
     first = place_ref[0] == 0
 
     def ordered(mine, theirs):
@@ -2284,7 +2298,7 @@
     mlp_ref[0:8], mlp_ref[8:16] = low, high
 
 
-def finish_call(place, parts, totals, gain, sizes):
+def finish_call(place, parts, totals, gain, moved, sizes):
     quarter = parts[0].shape[0]
     queries, keys, branch, units = sizes
     return pl.pallas_call(
@@ -2299,12 +2313,15 @@
             shape((units, quarter), F32),
             shape((16, 128), F32),
             shape((16, 128), F32),
-        ),
-        in_specs=[pl.BlockSpec(memory_space=pltpu.SMEM)] + [IN_VMEM] * (len(parts) + 2),
-        out_specs=[IN_VMEM] * 9,
+            shape((1, 128), F32),
+            shape((1, 128), F32),
+        )
+        + tuple(shape(item.shape, item.dtype) for item in moved),
+        in_specs=[pl.BlockSpec(memory_space=pltpu.SMEM)] + [IN_VMEM] * (len(parts) + 4),
+        out_specs=[IN_VMEM] * 13,
         compiler_params=pltpu.CompilerParams(vmem_limit_bytes=VMEM_MOST),
         cost_estimate=cost(0, 16 * 1024 * 1024),
-    )(place, *parts, totals, gain)
+    )(place, *parts, totals, gain, *moved)
 
 
 def plane_device(
@@ -2330,17 +2347,16 @@
     kv_width = w_key.shape[1] // 2
     units = w_gate.shape[1] // 2
 
-    half = jnp.arange(depth // 2, dtype=F32)
-    rate = THETA ** (-half * 2.0 / depth)
-    rate = jnp.concatenate([rate, rate])[None]
+    rate = np.float64(THETA) ** (-np.arange(depth // 2) * 2.0 / depth)
+    rate = jnp.asarray(np.concatenate([rate, rate])[None].astype(np.float32))
     attn_row, mlp_row, starts, cosine, sine, token_whole, w_project, w_branch = open_call(
         tokens, w_query, w_key, w_value, w_out, attn_gain[None], mlp_gain[None], seg_ids, rate, 0
     )
     fixed_args = (starts, cosine, sine, query_gain[None], key_gain[None])
     (
         first,
+        projected,
         first_scale,
-        projected,
         mixed,
         query,
         keys,
@@ -2425,15 +2441,20 @@
         down_share,
         attn_total,
         mlp_total,
+        query_total,
+        key_total,
+        output,
+        input_grad,
     ) = finish_call(
         place,
         (*ends, *rest_ends, out_mine, out_theirs, project_mine, project_theirs),
         totals,
         attn_row.reshape(16, 128),
+        (output, input_grad),
         (2 * head_width, 2 * kv_width, 2 * head_width, 2 * units),
     )
     attn_total, mlp_total = attn_total.reshape(-1), mlp_total.reshape(-1)
-    query_total, key_total = totals[10, 0], totals[10, 1]
+    query_total, key_total = query_total.reshape(-1), key_total.reshape(-1)
     return (
         output,
         input_grad,

time: 497 us -> 492 us (0.990)
  no operation moved by 1% of the time
where the time goes in v7:
time: 492 us; the launch traced here: 483 us
  Pallas kernels  480 us (98%)
    pallas_call x1, Pallas kernels, middle_call(): pl.pallas_call(middle_kernel, out_shape=[shape((height, width), F32), sha...  106 us
    pallas_call x1, Pallas kernels, branch_call(): pl.pallas_call(branch_kernel, out_shape=(shape((height, width), F32), sha...  87.3 us
    pallas_call x1, Pallas kernels, back_call(): pl.pallas_call(lambda *refs: back_kernel(most, *refs), out_shape=(shape((...  79 us
    pallas_call x1, Pallas kernels, last_call(): pl.pallas_call(last_kernel, out_shape=(shape((height, width)), shape((11,...  64.3 us
    pallas_call x1, Pallas kernels, front_call(): pl.pallas_call(lambda *refs: front_kernel(most, *refs), out_shape=outs, i...  55.8 us
    pallas_call x1, Pallas kernels, open_call(): pl.pallas_call(open_kernel, out_shape=(shape((1, 2 * width), F32), shape(...  49.6 us
    pallas_call x1, Pallas kernels, units_call(): pl.pallas_call(units_kernel, out_shape=(shape((tokens, width)), shape((to...  31 us

profile of v7, /device:TPU:10, one launch (start us, length us, event | category | flops | bytes accessed | tf_op | source)
XLA Modules:
  0.0 482.5 jit_solution(346789439286545996)
XLA Ops:
  0.6 49.6 %shard_map.246 = (f32[1,2048]{1,0:T(1,128)}, f32[1,2048]{1,0:T(1,128)}, s32[2,1024,1]{2,1,0:T(8,128)}, f32[2,1024,128]{2,1,0:T(8,128)}, f32[2,1024,128]{2,1,0:T(...) custom-call(bf16[512,1024]{1,0:T(8,128)(2,1)} %value_in_ref.1, ...), custom_call_target="tpu_custom_call" | custom-call | bytes 16777216 | tf_op jit(solution)/shard_map/pallas_call | solution.py:1233
  50.2 55.8 %shard_map.247 = (bf16[4,512,2048]{2,1,0:T(8,128)(2,1)}, f32[4,512,512]{2,1,0:T(8,128)}, f32[512,128]{1,0:T(8,128)}, bf16[4,512,256]{2,1,0:T(8,128)(2,1)}, bf16[...) custom-call(bf16[4,512,2048]{2,1,0:T(8,128)(2,1)} %get-tuple-element, ...), custom_call_target="tpu_custom_call" | custom-call | flops 4294967296 | bytes 33554432 | tf_op jit(solution)/shard_map/pallas_call | solution.py:1429
  106.1 87.3 %shard_map.248 = (f32[512,1024]{1,0:T(8,128)}, bf16[4,512,2048]{2,1,0:T(8,128)(2,1)}, bf16[2048,768]{1,0:T(8,128)(2,1)}, bf16[2048,768]{1,0:T(8,128)(2,1)}) custom-call(bf16[4,512,256]{2,1,0:T(8,128)(2,1)} %get-tuple-element.82.rows_in_ref.refs_5_, bf16[256,2048]{1,0:T(8,128)(2,1)} %get-tuple-element.83.weight_in_ref.refs_4_, ...), custom_call_target="tpu_custom_call" | custom-call | flops 2147483648 | bytes 33554432 | tf_op jit(solution)/shard_map/pallas_call | solution.py:1519
  193.4 31.0 %shard_map.249 = (bf16[2048,2048]{1,0:T(8,128)(2,1)}, bf16[2048,768]{1,0:T(8,128)(2,1)}, bf16[2048,1536]{1,0:T(8,128)(2,1)}, f32[2048,128]{1,0:T(8,128)}, f32[8,8,128]{2,1,0:T(8,128)}) custom-call(bf16[2048,2048]{1,0:T(8,128)(2,1)} %bitcast.31, bf16[2048,2048]{1,0:T(8,128)(2,1)} %bitcast.30, bf16[2048,768]{1,0:T(8,128)(2,1)} %get-tuple-element.87.gates_ref.gates_in_ref, ...), custom_call_target="tpu_custom_call" | custom-call | flops 19327352832 | bytes 41943040 | tf_op jit(solution)/shard_map/pallas_call | solution.py:1583
  224.4 106.0 %shard_map.250 = (f32[512,1024]{1,0:T(8,128)}, f32[1,1024]{1,0:T(1,128)}, bf16[4,512,2048]{2,1,0:T(8,128)(2,1)}, bf16[8,256,1024]{2,1,0:T(8,128)(2,1)}, f32[256,...) custom-call(bf16[4,512,1536]{2,1,0:T(8,128)(2,1)} %bitcast.37, ...), custom_call_target="tpu_custom_call" | custom-call | flops 19327352832 | bytes 33554432 | tf_op jit(solution)/shard_map/pallas_call | solution.py:1851
  330.5 0.0 copy-start
  330.5 79.0 %shard_map.251 = (bf16[512,1024]{1,0:T(8,128)(2,1)}, bf16[4,512,512]{2,1,0:T(8,128)(2,1)}, f32[8,8,128]{2,1,0:T(8,128)}, f32[2,8,128]{2,1,0:T(8,128)}, bf16[8,25...) custom-call(f32[1,128]{1,0:T(1,128)} %bitcast.27, ...), custom_call_target="tpu_custom_call" | custom-call | flops 6442450944 | bytes 33554432 | tf_op jit(solution)/shard_map/pallas_call | solution.py:2209
  409.5 0.7 slice_reduce_fusion
  410.2 0.0 copy-done
  410.2 0.6 pad_maximum_fusion.extra_ref
  410.8 64.3 %shard_map.252 = (bf16[512,1024]{1,0:T(8,128)(2,1)}, f32[11,8,128]{2,1,0:T(8,128)}, f32[256,256]{1,0:T(8,128)}, bf16[256,256]{1,0:T(8,128)(2,1)}, f32[256,512]{1,0:T(8,128)}, /*index=5*/bf16[256,512]{1,0:T(8,128)(2,1)}) custom-call(bf16[4,512,512]{2,1,0:T(8,128)(2,1)} %get-tuple-element.111.rows_in_ref, ...), custom_call_target="tpu_custom_call" | custom-call | flops 8589934592 | bytes 33554432 | tf_op jit(solution)/shard_map/pallas_call | solution.py:2044
  475.1 6.9 %shard_map.253 = (f32[256,512]{1,0:T(8,128)}, f32[256,256]{1,0:T(8,128)}, f32[256,256]{1,0:T(8,128)}, f32[512,256]{1,0:T(8,128)}, f32[256,1536]{1,0:T(8,128)}, /...) custom-call(s32[1]{0:T(128)} %bitcast.place_ref, ...), custom_call_target="tpu_custom_call" | custom-call | bytes 16777216 | tf_op jit(solution)/shard_map/pallas_call | solution.py:2304
  (1 shorter events, 0.0 us)
Async XLA Ops:
  330.5 79.7 %copy-start = (f32[1,1024]{1,0:T(1,128)S(1)}, f32[1,1024]{1,0:T(1,128)}, u32[]{:S(2)}) copy-start(f32[1,1024]{1,0:T(1,128)} %get-tuple-element.115) | copy-start | bytes 12292

commit v8 on v7

--- a/solution.py
+++ b/solution.py
@@ -1792,10 +1792,7 @@
         left = stream[slot].reshape(4 * rows, BLOCK)
         flat = rows_ref[...].reshape(4 * rows, columns)
         made.tiles[turn_tile(step)] = weight_grad(left, flat[:, :SPLIT]).astype(B16)
-        for low in range(SPLIT, columns, SPLIT):
-            stage[slot, :, low - SPLIT : low] = weight_grad(
-                left, flat[:, low : low + SPLIT]
-            ).astype(B16)
+        stage[slot] = weight_grad(left, flat[:, SPLIT:]).astype(B16)
         store(step).start()
 
     loads.wait(4, 7)
@@ -1891,7 +1888,8 @@
     stats_in_ref,
     scale_ref,
     gain_ref,
-    extra_ref,
+    mlp_ref,
+    heads_ref,
     out_in_ref,
     project_in_ref,
     result_ref,
@@ -1916,8 +1914,9 @@
     loads.start()
     stats_ref[...] = stats_in_ref[...]
     sums_ref[...] = jnp.zeros_like(sums_ref)
-    sums_ref[8] = extra_ref[0]
-    sums_ref[9] = extra_ref[1]
+    for row in range(8):
+        sums_ref[8, row : row + 1, :] = mlp_ref[:, row * 128 : (row + 1) * 128]
+    sums_ref[9, 0:2, :] = heads_ref[0, 0:2, :] + heads_ref[1, 0:2, :]
     greet(neighbours() + planes())
     wires = Wires(send_sems, recv_sems)
     base = REDUCE_KINDS + 1
@@ -2036,7 +2035,9 @@
     reduce.close()
 
 
-def last_call(rows, weight, stats, scale, value, gain, base, extra, out, project, number):
+def last_call(
+    rows, weight, stats, scale, value, gain, base, mlp_part, head_parts, out, project, number
+):
     height, width = value.shape
     count = width // CHUNK
     quarter, branch = out.shape[1:]
@@ -2051,7 +2052,7 @@
             shape((quarter, columns), F32),
             shape((quarter, columns)),
         ),
-        in_specs=[IN_ANY] * 4 + [IN_VMEM] * 4 + [IN_ANY] * 2,
+        in_specs=[IN_ANY] * 4 + [IN_VMEM] * 5 + [IN_ANY] * 2,
         out_specs=(IN_VMEM, IN_VMEM) + (IN_VMEM, IN_ANY) * 2,
         scratch_shapes=reduce_scratch(height, width)
         + [
@@ -2072,7 +2073,7 @@
         + load_scratch((rows, weight, value, base))[:4],
         compiler_params=remote_params(number),
         cost_estimate=cost(32 * height * columns * width, 64 * height * width),
-    )(rows, weight, value, base, stats, scale, gain, extra, out, project)
+    )(rows, weight, value, base, stats, scale, gain, mlp_part, head_parts, out, project)
 
 
 def back_kernel(
@@ -2411,12 +2412,6 @@
         most,
         4,
     )
-    extra = jnp.stack(
-        [
-            mlp_gain_part.reshape(8, 128),
-            jnp.pad(jnp.sum(gain_parts[:, :2], axis=0), ((0, 6), (0, 0))),
-        ]
-    )
     input_grad, totals, out_mine, out_theirs, project_mine, project_theirs = last_call(
         proj_grads,
         w_project,
@@ -2425,7 +2420,8 @@
         tokens,
         attn_gain[None],
         residual_grad,
-        extra,
+        mlp_gain_part,
+        gain_parts,
         out_tiles,
         project_tiles,
         5,

time: 492 us -> 491 us (level)
  no operation moved by 1% of the time
where the time goes in v8:
time: 491 us; the launch traced here: 481 us
  Pallas kernels  480 us (98%)
    pallas_call x1, Pallas kernels, middle_call(): pl.pallas_call(middle_kernel, out_shape=[shape((height, width), F32), sha...  106 us
    pallas_call x1, Pallas kernels, branch_call(): pl.pallas_call(branch_kernel, out_shape=(shape((height, width), F32), sha...  87.4 us
    pallas_call x1, Pallas kernels, back_call(): pl.pallas_call(lambda *refs: back_kernel(most, *refs), out_shape=(shape((...  79.1 us
    pallas_call x1, Pallas kernels, last_call(): pl.pallas_call(last_kernel, out_shape=(shape((height, width)), shape((11,...  64.3 us
    pallas_call x1, Pallas kernels, front_call(): pl.pallas_call(lambda *refs: front_kernel(most, *refs), out_shape=outs, i...  55.8 us
    pallas_call x1, Pallas kernels, open_call(): pl.pallas_call(open_kernel, out_shape=(shape((1, 2 * width), F32), shape(...  49.6 us
    pallas_call x1, Pallas kernels, units_call(): pl.pallas_call(units_kernel, out_shape=(shape((tokens, width)), shape((to...  31 us

profile of v8, /device:TPU:10, one launch (start us, length us, event | category | flops | bytes accessed | tf_op | source)
XLA Modules:
  0.0 481.3 jit_solution(8794826549036463218)
XLA Ops:
  0.6 49.6 %shard_map.246 = (f32[1,2048]{1,0:T(1,128)}, f32[1,2048]{1,0:T(1,128)}, s32[2,1024,1]{2,1,0:T(8,128)}, f32[2,1024,128]{2,1,0:T(8,128)}, f32[2,1024,128]{2,1,0:T(...) custom-call(bf16[512,1024]{1,0:T(8,128)(2,1)} %value_in_ref.1, ...), custom_call_target="tpu_custom_call" | custom-call | bytes 16777216 | tf_op jit(solution)/shard_map/pallas_call | solution.py:1233
  50.2 55.8 %shard_map.247 = (bf16[4,512,2048]{2,1,0:T(8,128)(2,1)}, f32[4,512,512]{2,1,0:T(8,128)}, f32[512,128]{1,0:T(8,128)}, bf16[4,512,256]{2,1,0:T(8,128)(2,1)}, bf16[...) custom-call(bf16[4,512,2048]{2,1,0:T(8,128)(2,1)} %get-tuple-element, ...), custom_call_target="tpu_custom_call" | custom-call | flops 4294967296 | bytes 33554432 | tf_op jit(solution)/shard_map/pallas_call | solution.py:1429
  106.1 87.4 %shard_map.248 = (f32[512,1024]{1,0:T(8,128)}, bf16[4,512,2048]{2,1,0:T(8,128)(2,1)}, bf16[2048,768]{1,0:T(8,128)(2,1)}, bf16[2048,768]{1,0:T(8,128)(2,1)}) custom-call(bf16[4,512,256]{2,1,0:T(8,128)(2,1)} %get-tuple-element.82.rows_in_ref.refs_5_, bf16[256,2048]{1,0:T(8,128)(2,1)} %get-tuple-element.83.weight_in_ref.refs_4_, ...), custom_call_target="tpu_custom_call" | custom-call | flops 2147483648 | bytes 33554432 | tf_op jit(solution)/shard_map/pallas_call | solution.py:1519
  193.4 31.0 %shard_map.249 = (bf16[2048,2048]{1,0:T(8,128)(2,1)}, bf16[2048,768]{1,0:T(8,128)(2,1)}, bf16[2048,1536]{1,0:T(8,128)(2,1)}, f32[2048,128]{1,0:T(8,128)}, f32[8,8,128]{2,1,0:T(8,128)}) custom-call(bf16[2048,2048]{1,0:T(8,128)(2,1)} %bitcast.27, bf16[2048,2048]{1,0:T(8,128)(2,1)} %bitcast.26, bf16[2048,768]{1,0:T(8,128)(2,1)} %get-tuple-element.87.gates_ref.gates_in_ref, ...), custom_call_target="tpu_custom_call" | custom-call | flops 19327352832 | bytes 41943040 | tf_op jit(solution)/shard_map/pallas_call | solution.py:1583
  224.5 106.0 %shard_map.250 = (f32[512,1024]{1,0:T(8,128)}, f32[1,1024]{1,0:T(1,128)}, bf16[4,512,2048]{2,1,0:T(8,128)(2,1)}, bf16[8,256,1024]{2,1,0:T(8,128)(2,1)}, f32[256,...) custom-call(bf16[4,512,1536]{2,1,0:T(8,128)(2,1)} %bitcast.33, ...), custom_call_target="tpu_custom_call" | custom-call | flops 19327352832 | bytes 33554432 | tf_op jit(solution)/shard_map/pallas_call | solution.py:1848
  330.5 79.1 %shard_map.251 = (bf16[512,1024]{1,0:T(8,128)(2,1)}, bf16[4,512,512]{2,1,0:T(8,128)(2,1)}, f32[8,8,128]{2,1,0:T(8,128)}, f32[2,8,128]{2,1,0:T(8,128)}, bf16[8,25...) custom-call(f32[1,128]{1,0:T(1,128)} %bitcast.23, ...), custom_call_target="tpu_custom_call" | custom-call | flops 6442450944 | bytes 33554432 | tf_op jit(solution)/shard_map/pallas_call | solution.py:2210
  409.6 64.3 %shard_map.252 = (bf16[512,1024]{1,0:T(8,128)(2,1)}, f32[11,8,128]{2,1,0:T(8,128)}, f32[256,256]{1,0:T(8,128)}, bf16[256,256]{1,0:T(8,128)(2,1)}, f32[256,512]{1,0:T(8,128)}, /*index=5*/bf16[256,512]{1,0:T(8,128)(2,1)}) custom-call(bf16[4,512,512]{2,1,0:T(8,128)(2,1)} %get-tuple-element.111.rows_in_ref, ...), custom_call_target="tpu_custom_call" | custom-call | flops 8589934592 | bytes 33554432 | tf_op jit(solution)/shard_map/pallas_call | solution.py:2045
  473.9 6.9 %shard_map.253 = (f32[256,512]{1,0:T(8,128)}, f32[256,256]{1,0:T(8,128)}, f32[256,256]{1,0:T(8,128)}, f32[512,256]{1,0:T(8,128)}, f32[256,1536]{1,0:T(8,128)}, /...) custom-call(s32[1]{0:T(128)} %bitcast.place_ref, ...), custom_call_target="tpu_custom_call" | custom-call | bytes 16777216 | tf_op jit(solution)/shard_map/pallas_call | solution.py:2305

commit v9 on v8

--- a/solution.py
+++ b/solution.py
@@ -1994,13 +1994,14 @@
     stats.finish(2)
     pull_columns(stats_ref, scale_ref, column_ref, width)
 
+    project.step()
+
     @pl.when(inner())
     def _():
         hop(3).wait()
         add(3)
         hop(4).start()
 
-    project.step()
     project.middle()
 
     @pl.loop(0, width // CHUNK)

time: 491 us -> 491 us (level)
  no operation moved by 1% of the time
where the time goes in v9:
time: 491 us; the launch traced here: 481 us
  Pallas kernels  480 us (98%)
    pallas_call x1, Pallas kernels, middle_call(): pl.pallas_call(middle_kernel, out_shape=[shape((height, width), F32), sha...  106 us
    pallas_call x1, Pallas kernels, branch_call(): pl.pallas_call(branch_kernel, out_shape=(shape((height, width), F32), sha...  87.4 us
    pallas_call x1, Pallas kernels, back_call(): pl.pallas_call(lambda *refs: back_kernel(most, *refs), out_shape=(shape((...  79.1 us
    pallas_call x1, Pallas kernels, last_call(): pl.pallas_call(last_kernel, out_shape=(shape((height, width)), shape((11,...  64.3 us
    pallas_call x1, Pallas kernels, front_call(): pl.pallas_call(lambda *refs: front_kernel(most, *refs), out_shape=outs, i...  55.8 us
    pallas_call x1, Pallas kernels, open_call(): pl.pallas_call(open_kernel, out_shape=(shape((1, 2 * width), F32), shape(...  49.6 us
    pallas_call x1, Pallas kernels, units_call(): pl.pallas_call(units_kernel, out_shape=(shape((tokens, width)), shape((to...  31 us

profile of v9, /device:TPU:10, one launch (start us, length us, event | category | flops | bytes accessed | tf_op | source)
XLA Modules:
  0.0 481.3 jit_solution(13606372920864008318)
XLA Ops:
  0.6 49.6 %shard_map.246 = (f32[1,2048]{1,0:T(1,128)}, f32[1,2048]{1,0:T(1,128)}, s32[2,1024,1]{2,1,0:T(8,128)}, f32[2,1024,128]{2,1,0:T(8,128)}, f32[2,1024,128]{2,1,0:T(...) custom-call(bf16[512,1024]{1,0:T(8,128)(2,1)} %value_in_ref.1, ...), custom_call_target="tpu_custom_call" | custom-call | bytes 16777216 | tf_op jit(solution)/shard_map/pallas_call | solution.py:1233
  50.2 55.8 %shard_map.247 = (bf16[4,512,2048]{2,1,0:T(8,128)(2,1)}, f32[4,512,512]{2,1,0:T(8,128)}, f32[512,128]{1,0:T(8,128)}, bf16[4,512,256]{2,1,0:T(8,128)(2,1)}, bf16[...) custom-call(bf16[4,512,2048]{2,1,0:T(8,128)(2,1)} %get-tuple-element, ...), custom_call_target="tpu_custom_call" | custom-call | flops 4294967296 | bytes 33554432 | tf_op jit(solution)/shard_map/pallas_call | solution.py:1429
  106.1 87.4 %shard_map.248 = (f32[512,1024]{1,0:T(8,128)}, bf16[4,512,2048]{2,1,0:T(8,128)(2,1)}, bf16[2048,768]{1,0:T(8,128)(2,1)}, bf16[2048,768]{1,0:T(8,128)(2,1)}) custom-call(bf16[4,512,256]{2,1,0:T(8,128)(2,1)} %get-tuple-element.82.rows_in_ref.refs_5_, bf16[256,2048]{1,0:T(8,128)(2,1)} %get-tuple-element.83.weight_in_ref.refs_4_, ...), custom_call_target="tpu_custom_call" | custom-call | flops 2147483648 | bytes 33554432 | tf_op jit(solution)/shard_map/pallas_call | solution.py:1519
  193.4 31.0 %shard_map.249 = (bf16[2048,2048]{1,0:T(8,128)(2,1)}, bf16[2048,768]{1,0:T(8,128)(2,1)}, bf16[2048,1536]{1,0:T(8,128)(2,1)}, f32[2048,128]{1,0:T(8,128)}, f32[8,8,128]{2,1,0:T(8,128)}) custom-call(bf16[2048,2048]{1,0:T(8,128)(2,1)} %bitcast.27, bf16[2048,2048]{1,0:T(8,128)(2,1)} %bitcast.26, bf16[2048,768]{1,0:T(8,128)(2,1)} %get-tuple-element.87.gates_ref.gates_in_ref, ...), custom_call_target="tpu_custom_call" | custom-call | flops 19327352832 | bytes 41943040 | tf_op jit(solution)/shard_map/pallas_call | solution.py:1583
  224.5 106.0 %shard_map.250 = (f32[512,1024]{1,0:T(8,128)}, f32[1,1024]{1,0:T(1,128)}, bf16[4,512,2048]{2,1,0:T(8,128)(2,1)}, bf16[8,256,1024]{2,1,0:T(8,128)(2,1)}, f32[256,...) custom-call(bf16[4,512,1536]{2,1,0:T(8,128)(2,1)} %bitcast.33, ...), custom_call_target="tpu_custom_call" | custom-call | flops 19327352832 | bytes 33554432 | tf_op jit(solution)/shard_map/pallas_call | solution.py:1848
  330.5 79.1 %shard_map.251 = (bf16[512,1024]{1,0:T(8,128)(2,1)}, bf16[4,512,512]{2,1,0:T(8,128)(2,1)}, f32[8,8,128]{2,1,0:T(8,128)}, f32[2,8,128]{2,1,0:T(8,128)}, bf16[8,25...) custom-call(f32[1,128]{1,0:T(1,128)} %bitcast.23, ...), custom_call_target="tpu_custom_call" | custom-call | flops 6442450944 | bytes 33554432 | tf_op jit(solution)/shard_map/pallas_call | solution.py:2211
  409.6 64.3 %shard_map.252 = (bf16[512,1024]{1,0:T(8,128)(2,1)}, f32[11,8,128]{2,1,0:T(8,128)}, f32[256,256]{1,0:T(8,128)}, bf16[256,256]{1,0:T(8,128)(2,1)}, f32[256,512]{1,0:T(8,128)}, /*index=5*/bf16[256,512]{1,0:T(8,128)(2,1)}) custom-call(bf16[4,512,512]{2,1,0:T(8,128)(2,1)} %get-tuple-element.111.rows_in_ref, ...), custom_call_target="tpu_custom_call" | custom-call | flops 8589934592 | bytes 33554432 | tf_op jit(solution)/shard_map/pallas_call | solution.py:2046
  473.9 6.9 %shard_map.253 = (f32[256,512]{1,0:T(8,128)}, f32[256,256]{1,0:T(8,128)}, f32[256,256]{1,0:T(8,128)}, f32[512,256]{1,0:T(8,128)}, f32[256,1536]{1,0:T(8,128)}, /...) custom-call(s32[1]{0:T(128)} %bitcast.place_ref, ...), custom_call_target="tpu_custom_call" | custom-call | bytes 16777216 | tf_op jit(solution)/shard_map/pallas_call | solution.py:2306
